TPU v7x, 32 devices: a whole 2x2x4 slice. The times are simulated.
32 devices in a mesh: dp: 4 (over y, x), row: 2 (over core), col: 4 (over z).
Axes of the slice: x: 2, y: 2, z: 4, core: 2. Of those that a mesh axis runs over, the one named last changes fastest.
Arguments:
- inputs: bfloat16 [6144, 6144], P('dp', 'row'), may hold values from -6 to 6
- pre_act: bfloat16 [6144, 12288], P(('dp', 'row'), 'col'), may hold values from -8 to 8
- out_grad: bfloat16 [6144, 12288], P(('dp', 'row'), 'col'), may hold values from -6 to 6
- weight: bfloat16 [6144, 12288], P('row', 'col'), may hold values from -6 to 6
- swag_mean: float32 [4, 1536, 12288], P('dp', 'row', 'col'), may hold values from -6 to 6
- swag_square: float32 [4, 1536, 12288], P('dp', 'row', 'col'), may hold values from 0.5 to 3
- snapshots: int32 [1], replicated, may hold values from 1 to 32
- update_flag: int32 [4, 1536], P('dp', 'row'), may hold values 0 or 1
Outputs:
- input_grad: bfloat16 [6144, 6144], P(('dp', 'col'), 'row')
- new_weight: float32 [4, 1536, 12288], P('dp', 'row', 'col')
- mean_out: float32 [4, 1536, 12288], P('dp', 'row', 'col')
- square_out: float32 [4, 1536, 12288], P('dp', 'row', 'col')
All inputs are finite; a program needn't handle non-finite values. No bound on the sum of `update_flag` on one device may be relied on, other than what follows from the above.
Results may differ from a plain program's by a relative error of at most 0.013.
Values may be sent and summed in bfloat16 or wider, within the bound.
No kernel may reach another device: no remote copies, remote signals or barrier semaphores. Data moves between devices by JAX's collectives and lax.ppermute only.
A program may use at most 192 MiB of HBM per device.

v0:
```python
import jax
import jax.numpy as jnp
from jax import lax
from jax.sharding import PartitionSpec as P

D = 6144


learning_rate = 0.5


def gelu_slope(values):
    normal_cdf = 0.5 * (1.0 + lax.erf(values * 0.7071067811865476))
    density = jnp.exp(-0.5 * values * values) * 0.3989422804014327
    return normal_cdf + values * density


def body(inputs, pre_act, out_grad, weight, swag_mean, swag_square, snapshots, update_flag):
    replica_tokens = inputs.shape[0]
    row_width = weight.shape[0]
    groups = lax.axis_size("dp")
    share_rows = row_width // groups
    multiplier = 1.0 / D**0.5
    local_grad = (out_grad.astype(jnp.float32) * gelu_slope(pre_act.astype(jnp.float32))).astype(
        jnp.bfloat16
    )
    portion = lax.all_gather(local_grad, "row", axis=0, tiled=True)
    grad_acc = lax.dot_general(
        inputs, portion, (((0,), (0,)), ((), ())), preferred_element_type=jnp.float32
    )
    term_rows = (
        lax.dot_general(
            portion, weight, (((1,), (1,)), ((), ())), preferred_element_type=jnp.float32
        )
        * multiplier
    )
    input_grad = lax.psum_scatter(
        term_rows.astype(jnp.bfloat16), "col", scatter_dimension=0, tiled=True
    )
    replica_index = lax.axis_index("dp")
    share = lax.psum_scatter(
        grad_acc.astype(jnp.bfloat16), "dp", scatter_dimension=0, tiled=True
    ).astype(jnp.float32)
    own_rows = lax.dynamic_slice_in_dim(weight, replica_index * share_rows, share_rows, 0).astype(
        jnp.float32
    )
    total_tokens = replica_tokens * groups
    stepped = own_rows - learning_rate * (share / total_tokens**0.5)
    blend = update_flag[0].astype(jnp.float32)[:, None] / (snapshots[0].astype(jnp.float32) + 1.0)
    mean_old = swag_mean[0]
    square_old = swag_square[0]
    mean_new = mean_old + blend * (stepped - mean_old)
    square_new = square_old + blend * (stepped * stepped - square_old)
    return (input_grad, stepped[None], mean_new[None], square_new[None])


def solution(mesh):
    in_specs = (
        P("dp", "row"),
        P(("dp", "row"), "col"),
        P(("dp", "row"), "col"),
        P("row", "col"),
        P("dp", "row", "col"),
        P("dp", "row", "col"),
        P(),
        P("dp", "row"),
    )
    out_specs = (
        P(("dp", "col"), "row"),
        P("dp", "row", "col"),
        P("dp", "row", "col"),
        P("dp", "row", "col"),
    )
    return jax.shard_map(body, mesh=mesh, in_specs=in_specs, out_specs=out_specs, check_vma=False)
```

profile of v0, /device:TPU:0, one launch (start us, length us, event | category | flops | bytes accessed | tf_op | source)
XLA Modules:
  0.0 420.0 jit_solution(9647816436397516292)
XLA Ops:
  7.2 0.0 all-gather.2.cloned.1.call-start
  7.2 8.2 %fusion.11 = bf16[768,3072]{1,0:T(8,128)(2,1)} fusion(bf16[768,3072]{1,0:T(8,128)(2,1)} %param.9, bf16[768,3072]{1,0:T(8,128)(2,1)} %param.10), kind=kLoop, calls=%fused_computation.22 | loop fusion | flops 28311552 | bytes 14155776 | tf_op jit(solution)/shard_map/convert_element_type | solution.py:24
  15.4 0.0 all-gather.2.cloned.1.call-update
  15.5 0.0 reduce-scatter.5.cloned.1.call-start
  15.5 24.7 %all-gather.2.cloned.1.call-done = bf16[1536,3072]{1,0:T(8,128)(2,1)} async-done(((bf16[768,3072]{1,0:T(8,128)(2,1)}), bf16[1536,3072]{1,0:T(8,128)(2,1)}) %all-gather.2.cloned.1.call-update) | async-done | bytes 9437200 | tf_op jit(solution)/shard_map/all_gather | solution.py:27
  40.2 36.8 %convert_bitcast_fusion = bf16[3072,3072]{0,1:T(8,128)(2,1)} fusion(bf16[1536,3072]{1,0:T(8,128)(2,1)} %all-gather.2.cloned.1.call-done, bf16[1536,3072]{1,0:T(8,128)(2,1)} %param.8), kind=kOutput, calls=%fused_computation | convolution fusion | flops 29000466432 | bytes 37748736 | tf_op jit(solution)/shard_map/dot_general | solution.py:28
  76.9 0.0 reduce-scatter.5.cloned.1.call-update
  77.0 0.2 reduce-scatter.3.cloned.1.call-start
  77.2 37.3 %multiply_convert_fusion = bf16[1536,3072]{1,0:T(8,128)(2,1)} fusion(bf16[1536,3072]{1,0:T(8,128)(2,1)} %all-gather.2.cloned.1.call-done, bf16[3072,3072]{1,0:T(8,128)(2,1)} %param.11), kind=kOutput, calls=%fused_computation.1 | convolution fusion | flops 29000466432 | bytes 37748736 | tf_op jit(solution)/shard_map/dot_general | solution.py:32
  114.5 0.0 reduce-scatter.3.cloned.1.call-update
  115.2 5.1 %constant_dynamic-slice_fusion = bf16[768,3072]{1,0:T(8,128)(2,1)} fusion(bf16[3072,3072]{1,0:T(8,128)(2,1)} %param.11, s32[]{:T(128)S(6)} %select_n.3), kind=kLoop, calls=%fused_computation.25 | loop fusion | bytes 9437188 | tf_op jit(solution)/shard_map/dynamic_slice | solution.py:44
  120.2 6.7 %copy.18 = bf16[768,3072]{0,1:T(8,128)(2,1)} copy(bf16[768,3072]{1,0:T(8,128)(2,1)} %constant_dynamic-slice_fusion) | data formatting | bytes 9437184
  126.9 9.8 %copy.13 = f32[1,768,3072]{1,2,0:T(8,128)} copy(f32[1,768,3072]{2,1,0:T(8,128)} %param.12) | data formatting | bytes 18874368 | tf_op args[4]
  136.6 0.0 copy-start
  136.6 9.7 %copy.14 = f32[1,768,3072]{1,2,0:T(8,128)} copy(f32[1,768,3072]{2,1,0:T(8,128)} %param.13) | data formatting | bytes 18874368 | tf_op args[5]
  146.4 0.0 copy-done
  146.4 102.7 %reduce-scatter.5.cloned.1.call-done = bf16[768,3072]{0,1:T(8,128)(2,1)} async-done(((bf16[3072,3072]{0,1:T(8,128)(2,1)}), bf16[768,3072]{0,1:T(8,128)(2,1)}) %reduce-scatter.5.cloned.1.call-update) | async-done | bytes 4718608 | tf_op jit(solution)/shard_map/reduce_scatter | solution.py:41
  249.1 20.9 %fusion.8 = (f32[1,768,3072]{1,2,0:T(8,128)}, f32[1,768,3072]{1,2,0:T(8,128)}, f32[1,768,3072]{1,2,0:T(8,128)}) fusion(f32[1,768,3072]{1,2,0:T(8,128)} %copy.14, bf16[768,3072]{0,1:T(8,128)(2,1)} %reduce-scatter.5.cloned.1.call-done, bf16[768,3072]{0,1:T(8,128)(2,1)} %copy.18, f32[768]{0:T(1024)S(1)} %divide_reduce_fusion, f32[1,768,3072]{1,2,0:T(8,128)} %copy.13), kind=kLoop, calls=%fused_computation.16 | loop fusion | flops 25952256 | bytes 56626176 | tf_op jit(solution)/shard_map/broadcast_in_dim | solution.py:54
  270.0 9.6 %copy.17 = f32[1,768,3072]{2,1,0:T(8,128)} copy(f32[1,768,3072]{1,2,0:T(8,128)} %get-tuple-element.8) | data formatting | bytes 18874368
  279.6 9.6 %copy.16 = f32[1,768,3072]{2,1,0:T(8,128)} copy(f32[1,768,3072]{1,2,0:T(8,128)} %get-tuple-element.9) | data formatting | bytes 18874368
  289.2 9.6 %copy.15 = f32[1,768,3072]{2,1,0:T(8,128)} copy(f32[1,768,3072]{1,2,0:T(8,128)} %get-tuple-element.10) | data formatting | bytes 18874368
  298.8 114.7 %reduce-scatter.3.cloned.1.call-done = bf16[384,3072]{1,0:T(8,128)(2,1)} async-done(((bf16[1536,3072]{1,0:T(8,128)(2,1)}), bf16[384,3072]{1,0:T(8,128)(2,1)}) %reduce-scatter.3.cloned.1.call-update) | async-done | bytes 2359312 | tf_op jit(solution)/shard_map/reduce_scatter | solution.py:37
  (1 shorter events, 0.0 us)
Async XLA Ops:
  7.2 33.0 %all-gather.2.cloned.1.call-start = ((), (), s32[]{:S(2)}) async-start(), calls=%async_computation.2 | async-start | bytes 14155776 | tf_op jit(solution)/shard_map/all_gather | solution.py:27
  15.5 233.7 %reduce-scatter.5.cloned.1.call-start = ((), (), s32[]{:S(2)}) async-start(), calls=%async_computation.4 | async-start | bytes 23592960 | tf_op jit(solution)/shard_map/reduce_scatter | solution.py:41
  77.0 336.5 %reduce-scatter.3.cloned.1.call-start = ((), (), s32[]{:S(2)}) async-start(), calls=%async_computation.3 | async-start | bytes 11796480 | tf_op jit(solution)/shard_map/reduce_scatter | solution.py:37
  136.6 9.7 %copy-start = (s32[1,768]{1,0:T(1,128)S(1)}, s32[1,768]{1,0:T(1,128)}, u32[]{:S(2)}) copy-start(s32[1,768]{1,0:T(1,128)} %param.15) | copy-start | bytes 9220
Sparse Core Ops, SparseCore 0:
  15.6 24.5 all-gather.1
  77.1 171.9 reduce-scatter.4
  252.2 161.2 reduce-scatter.2
where the time goes:
time: 421 us; the launch traced here: 420 us
  waiting for transfers between devices  242 us (57%)
  matrix products  74.1 us (18%)
  local copies, waits for them, and re-layouts  60 us (14%)
  other arithmetic  29.1 us (7%)
  between operations  14.4 us (3%)
    reduce_scatter x1, waiting for transfers between devices, body(): lax.psum_scatter(term_rows.astype(jnp.bfloat16), 'col', scatter_dimension...  115 us
    reduce_scatter x1, waiting for transfers between devices, body(): lax.psum_scatter(grad_acc.astype(jnp.bfloat16), 'dp', scatter_dimension=0...  103 us
    unnamed x8, local copies, waits for them, and re-layouts  55 us
    dot_general x1, matrix products, body(): lax.dot_general(portion, weight, (((1,), (1,)), ((), ())), preferred_elem...  37.3 us
    dot_general x1, matrix products, body(): lax.dot_general(inputs, portion, (((0,), (0,)), ((), ())), preferred_elem...  36.8 us
    all_gather x1, waiting for transfers between devices, body(): portion = lax.all_gather(local_grad, 'row', axis=0, tiled=True)  24.7 us
    broadcast_in_dim x1, other arithmetic, body(): return (input_grad, stepped[None], mean_new[None], square_new[None])  20.9 us
  transfers between devices with their start and end apart: 3, of which 3 were waited for; matrix products, arithmetic and copies ran while one was open for 28% of the time, Pallas kernels for 0%

commit v1 on v0

v1 whole, which is shorter than its diff:
```python
import jax
import jax.numpy as jnp
from jax import lax
from jax.experimental import pallas as pl
from jax.experimental.pallas import tpu as pltpu
from jax.sharding import PartitionSpec as P

D = 6144


learning_rate = 0.5
VMEM_LIMIT = 56 * 1024 * 1024
LANES = 128
TOKEN = (8, LANES)


def gelu_slope(values):
    normal_cdf = 0.5 * (1.0 + lax.erf(values * 0.7071067811865476))
    density = jnp.exp(-0.5 * values * values) * 0.3989422804014327
    return normal_cdf + values * density


def times_slope(out_grad, pre_act):
    return (out_grad.astype(jnp.float32) * gelu_slope(pre_act.astype(jnp.float32))).astype(jnp.bfloat16)


def dot(a, b, dims):
    return lax.dot_general(a, b, (dims, ((), ())), preferred_element_type=jnp.float32)


def params():
    return pltpu.CompilerParams(dimension_semantics=("arbitrary",), vmem_limit_bytes=VMEM_LIMIT)


def anywhere(arrays):
    return [pl.BlockSpec(memory_space=pl.ANY)] * len(arrays)


def block_width(width, most):
    return max(b for b in range(LANES, min(width, most) + 1, LANES) if width % b == 0)


def weight_product(inputs, local, remote, ids, share, start, width, deps=(), add=None):
    half = local.shape[0]
    bn = block_width(width, 512)
    first = start // bn

    def kernel(ids_ref, a0, a1, g0, g1, *rest):
        more, (out, token, t0, t1) = rest[: -4], rest[-4:]

        @pl.when(pl.program_id(0) == 0)
        def _():
            t0[...] = a0[...].T
            t1[...] = a1[...].T
            token[...] = jnp.zeros_like(token)

        acc = dot(t0[...], g0[...], ((1,), (0,))) + dot(t1[...], g1[...], ((1,), (0,)))
        if add is not None:
            acc = acc + more[0][...].astype(jnp.float32)
        out[...] = acc.astype(out.dtype)

    extra = [] if add is None else [add]
    return pl.pallas_call(
        kernel,
        grid_spec=pltpu.PrefetchScalarGridSpec(
            num_scalar_prefetch=1,
            grid=(width // bn,),
            in_specs=[
                pl.BlockSpec((half, share), lambda j, ids: (ids[1], ids[0])),
                pl.BlockSpec((half, share), lambda j, ids: (ids[2], ids[0])),
                pl.BlockSpec((half, bn), lambda j, ids: (0, first + j)),
                pl.BlockSpec((half, bn), lambda j, ids: (0, first + j)),
            ]
            + [pl.BlockSpec((share, bn), lambda j, ids: (0, j))] * len(extra)
            + anywhere(deps),
            out_specs=[
                pl.BlockSpec((share, bn), lambda j, ids: (0, j)),
                pl.BlockSpec(TOKEN, lambda j, ids: (0, 0)),
            ],
            scratch_shapes=[pltpu.VMEM((share, half), jnp.bfloat16)] * 2,
        ),
        out_shape=[jax.ShapeDtypeStruct((share, width), jnp.bfloat16), jax.ShapeDtypeStruct(TOKEN, jnp.float32)],
        compiler_params=params(),
        cost_estimate=pl.CostEstimate(
            flops=4 * half * share * width,
            bytes_accessed=2 * (2 * half * (share + width) + share * width * (1 + len(extra))),
            transcendentals=0,
        ),
        name="weight_product",
    )(ids, inputs, inputs, local, remote, *extra, *deps)


def input_product(weight, locals_, remotes, ids, rows, multiplier, deps=()):
    width, hidden = weight.shape
    bn = block_width(width, 512)
    count = len(locals_)

    def kernel(ids_ref, w, *rest):
        mine, others = rest[:count], rest[count : 2 * count]
        out, token, lhs = rest[-3:]

        @pl.when(pl.program_id(0) == 0)
        def _():
            token[...] = jnp.zeros_like(token)

        for chosen, refs in ((1, mine), (0, others)):

            @pl.when((pl.program_id(0) == 0) & (ids_ref[1] == chosen))
            def _():
                at = 0
                for ref in refs:
                    lhs[:, at : at + ref.shape[1]] = ref[...]
                    at += ref.shape[1]

        out[...] = (dot(lhs[...], w[...], ((1,), (1,))) * multiplier).astype(out.dtype)

    return pl.pallas_call(
        kernel,
        grid_spec=pltpu.PrefetchScalarGridSpec(
            num_scalar_prefetch=1,
            grid=(width // bn,),
            in_specs=[pl.BlockSpec((bn, hidden), lambda j, ids: (j, 0))]
            + [pl.BlockSpec((rows, a.shape[1]), lambda j, ids: (ids[0], 0)) for a in (*locals_, *remotes)]
            + anywhere(deps),
            out_specs=[
                pl.BlockSpec((rows, bn), lambda j, ids: (0, j)),
                pl.BlockSpec(TOKEN, lambda j, ids: (0, 0)),
            ],
            scratch_shapes=[pltpu.VMEM((rows, hidden), jnp.bfloat16)],
        ),
        out_shape=[jax.ShapeDtypeStruct((rows, width), jnp.bfloat16), jax.ShapeDtypeStruct(TOKEN, jnp.float32)],
        compiler_params=params(),
        cost_estimate=pl.CostEstimate(
            flops=2 * rows * width * hidden,
            bytes_accessed=2 * (width * hidden + 2 * rows * hidden + rows * width),
            transcendentals=0,
        ),
        name="input_product",
    )(ids, weight, *locals_, *remotes, *deps)


def update(inputs, local, remote, ids, received, weight, mean, square, blend, start, offset, width, scale, before):
    half = local.shape[0]
    share = mean.shape[1]
    bn = block_width(width, 256)
    first, place = start // bn, (offset + start) // bn
    terms = len(received)
    shape = jax.ShapeDtypeStruct(mean.shape, jnp.float32)

    def kernel(ids_ref, a0, a1, g0, g1, w, m, s, b, *rest):
        others = rest[:terms]
        new_w, new_m, new_s, t0, t1 = rest[-5:]

        @pl.when(pl.program_id(0) == 0)
        def _():
            t0[...] = a0[...].T
            t1[...] = a1[...].T

        total = dot(t0[...], g0[...], ((1,), (0,))) + dot(t1[...], g1[...], ((1,), (0,)))
        for other in others:
            total = total + other[...].astype(jnp.float32)
        stepped = w[...].astype(jnp.float32) - scale * total
        new_w[0] = stepped
        new_m[0] = m[0] + b[...] * (stepped - m[0])
        new_s[0] = s[0] + b[...] * (stepped * stepped - s[0])

    moment = pl.BlockSpec((1, share, bn), lambda j, ids: (0, 0, place + j))
    n_in = 9 + terms
    return pl.pallas_call(
        kernel,
        grid_spec=pltpu.PrefetchScalarGridSpec(
            num_scalar_prefetch=1,
            grid=(width // bn,),
            in_specs=[
                pl.BlockSpec((half, share), lambda j, ids: (ids[1], ids[0])),
                pl.BlockSpec((half, share), lambda j, ids: (ids[2], ids[0])),
                pl.BlockSpec((half, bn), lambda j, ids: (0, first + j)),
                pl.BlockSpec((half, bn), lambda j, ids: (0, first + j)),
                pl.BlockSpec((share, bn), lambda j, ids: (ids[0], place + j)),
                moment,
                moment,
                pl.BlockSpec((share, 1), lambda j, ids: (0, 0)),
            ]
            + [pl.BlockSpec((share, bn), lambda j, ids: (0, j))] * terms
            + anywhere(before),
            out_specs=[moment] * 3,
            scratch_shapes=[pltpu.VMEM((share, half), jnp.bfloat16)] * 2,
        ),
        out_shape=[shape] * 3,
        input_output_aliases={n_in + k: k for k in range(len(before))},
        compiler_params=params(),
        cost_estimate=pl.CostEstimate(
            flops=4 * half * share * width,
            bytes_accessed=2 * 2 * half * (share + width) + share * width * (2 + 8 + 12 + 2 * terms),
            transcendentals=0,
        ),
        name="update",
    )(ids, inputs, inputs, local, remote, weight, mean, square, blend, *received, *before)


def plain_body(inputs, pre_act, out_grad, weight, swag_mean, swag_square, snapshots, update_flag):
    row_width = weight.shape[0]
    groups = lax.axis_size("dp")
    share_rows = row_width // groups
    multiplier = 1.0 / D**0.5
    local_grad = times_slope(out_grad, pre_act)
    portion = lax.all_gather(local_grad, "row", axis=0, tiled=True)
    grad_acc = dot(inputs, portion, ((0,), (0,)))
    term_rows = dot(portion, weight, ((1,), (1,))) * multiplier
    input_grad = lax.psum_scatter(term_rows.astype(jnp.bfloat16), "col", scatter_dimension=0, tiled=True)
    share = lax.psum_scatter(grad_acc.astype(jnp.bfloat16), "dp", scatter_dimension=0, tiled=True).astype(jnp.float32)
    own_rows = lax.dynamic_slice_in_dim(weight, lax.axis_index("dp") * share_rows, share_rows, 0).astype(jnp.float32)
    total_tokens = inputs.shape[0] * groups
    stepped = own_rows - learning_rate * (share / total_tokens**0.5)
    blend = update_flag[0].astype(jnp.float32)[:, None] / (snapshots[0].astype(jnp.float32) + 1.0)
    mean_new = swag_mean[0] + blend * (stepped - swag_mean[0])
    square_new = swag_square[0] + blend * (stepped * stepped - swag_square[0])
    return (input_grad, stepped[None], mean_new[None], square_new[None])


def body(inputs, pre_act, out_grad, weight, swag_mean, swag_square, snapshots, update_flag):
    tokens = inputs.shape[0]
    half = pre_act.shape[0]
    width, hidden = weight.shape
    groups, cols = lax.axis_size("dp"), lax.axis_size("col")
    share = width // groups
    rows = tokens // cols
    multiplier = 1.0 / D**0.5
    scale = learning_rate / (tokens * groups) ** 0.5
    me, core, place = lax.axis_index("dp"), lax.axis_index("row"), lax.axis_index("col")

    def swap(value, axis, bit):
        return lax.ppermute(value, axis, [(i, i ^ bit) for i in range(lax.axis_size(axis))])

    piece = hidden // 2
    starts = (0, piece)
    mine = [times_slope(out_grad[:, s : s + piece], pre_act[:, s : s + piece]) for s in starts]
    theirs = [swap(value, "row", 1) for value in mine]
    blend = update_flag[0].astype(jnp.float32)[:, None] / (snapshots[0].astype(jnp.float32) + 1.0)

    def product(index, k, deps, add=None):
        ids = jnp.stack([index, core, 1 - core]).astype(jnp.int32)
        out, token = weight_product(inputs, mine[k], theirs[k], ids, share, 0, piece, deps, add)
        return out, [token]

    turns = []
    for i in range(cols):
        if 2 * i < cols:
            order = [c for c in range(cols - 1, i, -1)] + [c for c in range(i)] + [i]
        else:
            order = [c for c in range(i)] + [c for c in range(cols - 1, i, -1)] + [i]
        turns.append(order)
    turns = jnp.array(turns, jnp.int32)
    per_half = half // rows

    def chunk(turn, deps):
        index = turns[place, turn]
        ids = jnp.stack([index % per_half, (index // per_half == core).astype(jnp.int32)]).astype(jnp.int32)
        out, token = input_product(weight, mine, theirs, ids, rows, multiplier, deps)
        return out, [token]

    near = (1, 2)
    far = (2, 1)
    outer = ((0, 1), (cols - 1, cols - 2))
    middle = ((1, 2), (2, 1))
    inner = ((1, 0), (cols - 2, cols - 1))

    def along(value, pairs):
        return lax.ppermute(value, "col", pairs)

    def plus(*values):
        return sum(v.astype(jnp.float32) for v in values).astype(jnp.bfloat16)

    pass_a, order = product(me ^ 3, 0, [])
    got_pass_a = swap(pass_a, "dp", near[0])
    pass_b, order = product(me ^ 3, 1, order)
    got_pass_b = swap(pass_b, "dp", near[1])
    c0, order = chunk(0, order)
    got_o0 = along(c0, outer)
    keep_a, order = product(me ^ near[0], 0, order)
    got_keep_a = swap(keep_a, "dp", near[0])
    keep_b, order = product(me ^ near[1], 1, order)
    got_keep_b = swap(keep_b, "dp", near[1])
    c1, order = chunk(1, order)
    got_o1 = along(c1, outer)
    c2, order = chunk(2, order)
    got_o2 = along(c2, outer)
    c3, order = chunk(3, order)
    got_m1 = along(plus(c0, got_o0), middle)
    last_a, order = product(me ^ far[0], 0, order, got_pass_a)
    got_last_a = swap(last_a, "dp", far[0])
    last_b, order = product(me ^ far[1], 1, order, got_pass_b)
    got_last_b = swap(last_b, "dp", far[1])
    got_m2 = along(plus(c1, got_o1), middle)
    got_i = along(plus(c2, got_m1), inner)

    ids = jnp.stack([me, core, 1 - core]).astype(jnp.int32)
    outs = ()
    for k, got in ((0, (got_keep_a, got_last_a)), (1, (got_keep_b, got_last_b))):
        outs = update(
            inputs, mine[k], theirs[k], ids, got, weight, swag_mean, swag_square, blend, 0, starts[k], piece, scale, outs
        )
    input_grad = plus(c3, got_o2, got_m2, got_i)
    return (input_grad, *outs)


def solution(mesh):
    in_specs = (
        P("dp", "row"),
        P(("dp", "row"), "col"),
        P(("dp", "row"), "col"),
        P("row", "col"),
        P("dp", "row", "col"),
        P("dp", "row", "col"),
        P(),
        P("dp", "row"),
    )
    out_specs = (
        P(("dp", "col"), "row"),
        P("dp", "row", "col"),
        P("dp", "row", "col"),
        P("dp", "row", "col"),
    )
    scheduled = dict(mesh.shape) == {"dp": 4, "row": 2, "col": 4}
    return jax.shard_map(
        body if scheduled else plain_body, mesh=mesh, in_specs=in_specs, out_specs=out_specs, check_vma=False
    )
```

time: 421 us -> 280 us (0.67)
  waiting for transfers between devices: 242 us -> 56.9 us
  Pallas kernels: 0 us -> 150 us
  matrix products: 74.1 us -> 0 us
  local copies, waits for them, and re-layouts: 60 us -> 3.21 us
  starting transfers between devices: 0.3 us -> 25.4 us
    reduce_scatter x2 -> x0, waiting for transfers between devices: 217 us -> none  [the longest x1 115 us: body(): lax.psum_scatter(term_rows.astype(jnp.bfloat16), 'col', scatter_dimension...]
    pallas_call x0 -> x12, Pallas kernels: none -> 150 us  [the longest x4 59.9 us: input_product(): pl.pallas_call(kernel, grid_spec=pltpu.PrefetchScalarGridSpec(num_scalar_...]
    dot_general x2 -> x0, matrix products: 74.1 us -> none  [the longest x1 37.3 us: body(): lax.dot_general(portion, weight, (((1,), (1,)), ((), ())), preferred_elem...]
    ppermute x0 -> x14, waiting for transfers between devices: none -> 56.9 us  [the longest x8 56.8 us: swap(): lax.ppermute(value, axis, [(i, i ^ bit) for i in range(lax.axis_size(axis...]
    unnamed x8 -> x18, local copies, waits for them, and re-layouts: 55 us -> 1.44 us
    ppermute x0 -> x14, starting transfers between devices: none -> 25.4 us  [the longest x6 17.3 us: along(): return lax.ppermute(value, 'col', pairs)]
    all_gather x1 -> x0, waiting for transfers between devices: 24.7 us -> none  [body(): portion = lax.all_gather(local_grad, 'row', axis=0, tiled=True)]
    broadcast_in_dim x1 -> x0, other arithmetic: 20.9 us -> none  [body(): return (input_grad, stepped[None], mean_new[None], square_new[None])]
  transfers between devices with their start and end apart: 3 -> 14, of which waited for: 3 -> 3; matrix products, arithmetic and copies ran while one was open for 28% -> 7% of each run, Pallas kernels for 0% -> 45%
where the time goes in v1:
time: 280 us; the launch traced here: 279 us
  Pallas kernels  150 us (54%)
  waiting for transfers between devices  56.9 us (20%)
  other arithmetic  32 us (11%)
  starting transfers between devices  25.4 us (9%)
  between operations  11.8 us (4%)
  local copies, waits for them, and re-layouts  3.21 us (1%)
    pallas_call x4, Pallas kernels, input_product(): pl.pallas_call(kernel, grid_spec=pltpu.PrefetchScalarGridSpec(num_scalar_...  59.9 us
    ppermute x8, waiting for transfers between devices, swap(): lax.ppermute(value, axis, [(i, i ^ bit) for i in range(lax.axis_size(axis...  56.8 us
    pallas_call x6, Pallas kernels, weight_product(): pl.pallas_call(kernel, grid_spec=pltpu.PrefetchScalarGridSpec(num_scalar_...  54.6 us
    pallas_call x2, Pallas kernels, update(): pl.pallas_call(kernel, grid_spec=pltpu.PrefetchScalarGridSpec(num_scalar_...  35.2 us
    convert_element_type x4, other arithmetic, plus(): return sum((v.astype(jnp.float32) for v in values)).astype(jnp.bfloat16)  18.9 us
    ppermute x6, starting transfers between devices, along(): return lax.ppermute(value, 'col', pairs)  17.3 us
    convert_element_type x1, other arithmetic, times_slope(): (out_grad.astype(jnp.float32) * gelu_slope(pre_act.astype(jnp.float32)))....  8.31 us
    ppermute x8, starting transfers between devices, swap(): lax.ppermute(value, axis, [(i, i ^ bit) for i in range(lax.axis_size(axis...  8.08 us
  transfers between devices with their start and end apart: 14, of which 3 were waited for; matrix products, arithmetic and copies ran while one was open for 7% of the time, Pallas kernels for 45%

profile of v1, /device:TPU:0, one launch (start us, length us, event | category | flops | bytes accessed | tf_op | source)
XLA Modules:
  0.0 278.9 jit_solution(3005598939296423828)
XLA Ops:
  0.6 8.3 %fusion.14 = (bf16[768,1536]{1,0:T(8,128)(2,1)}, bf16[768,1536]{1,0:T(8,128)(2,1)S(1)}) fusion(bf16[768,3072]{1,0:T(8,128)(2,1)} %param.10, bf16[768,3072]{1,0:T(8,128)(2,1)} %param.11), kind=kLoop, calls=%fused_computation.26 | loop fusion | flops 28311552 | bytes 14155776 | tf_op jit(solution)/shard_map/convert_element_type | solution.py:24
  23.1 8.8 %weight_product.6 = (bf16[768,1536]{1,0:T(8,128)(2,1)}, f32[8,128]{1,0:T(8,128)}) custom-call(s32[3]{0:T(128)} %add_add_fusion.2.ids_ref, bf16[1536,3072]{1,0:T(8,128)(2,1)} %a1.15, bf16[1536,3072]{1,0:T(8,128)(2,1)} %a1.15, bf16[768,1536]{1,0:T(8,128)(2,1)} %copy-done, bf16[768,1536]{1,0:T(8,128)(2,1)} %collective-permute-done.g1.rest_2_), custom_call_target="tpu_custom_call" | custom-call | flops 3623878656 | bytes 9437184 | tf_op jit(solution)/shard_map/weight_product/pallas_call | solution.py:63
  31.9 8.8 %weight_product.7 = (bf16[768,1536]{1,0:T(8,128)(2,1)}, f32[8,128]{1,0:T(8,128)}) custom-call(s32[3]{0:T(128)} %add_add_fusion.2.ids_ref, bf16[1536,3072]{1,0:T(8,128)(2,1)} %a1.15, bf16[1536,3072]{1,0:T(8,128)(2,1)} %a1.15, bf16[768,1536]{1,0:T(8,128)(2,1)} %get-tuple-element.54.g0.rest_1_, bf16[768,1536]{1,0:T(8,128)(2,1)} %collective-permute-done.1.g1.rest_3_, ...), custom_call_target="tpu_custom_call" | custom-call | flops 3623878656 | bytes 9437184 | tf_op jit(solution)/shard_map/weight_product/pallas_call | solution.py:63
  40.7 14.9 %input_product.4 = (bf16[384,3072]{1,0:T(8,128)(2,1)}, f32[8,128]{1,0:T(8,128)}) custom-call(s32[2]{0:T(128)} %pad_add_fusion.3.ids_ref, bf16[3072,3072]{1,0:T(8,128)(2,1)} %w.11, bf16[768,1536]{1,0:T(8,128)(2,1)} %copy-done, bf16[768,1536]{1,0:T(8,128)(2,1)} %get-tuple-element.54.g0.rest_1_, bf16[768,1536]{1,0:T(8,128)(2,1)} %collective-permute-done.g1.rest_2_, ...), custom_call_target="tpu_custom_call" | custom-call | flops 7247757312 | bytes 25952256 | tf_op jit(solution)/shard_map/input_product/pallas_call | solution.py:117
  55.6 6.4 %collective-permute-start.5 = (bf16[384,3072]{1,0:T(8,128)(2,1)}, bf16[384,3072]{1,0:T(8,128)(2,1)}, u32[]{:S(2)}, u32[]{:S(2)}) collective-permute-start(bf16[384,3072]{1,0:T(8,128)(2,1)} %get-tuple-element.39), channel_id=1, source_target_pairs={{0,1},{3,2},{4,5},{7,6},{8,9},{11,10},{12,13},{15,14},{16,17},{19,... | collective-permute-start | bytes 7077896 | tf_op jit(solution)/shard_map/ppermute | solution.py:269
  63.8 1.5 collective-permute-start.10
  65.3 8.9 %weight_product.8 = (bf16[768,1536]{1,0:T(8,128)(2,1)}, f32[8,128]{1,0:T(8,128)}) custom-call(s32[3]{0:T(128)} %add_add_fusion.1.ids_ref, bf16[1536,3072]{1,0:T(8,128)(2,1)} %a1.15, bf16[1536,3072]{1,0:T(8,128)(2,1)} %a1.15, bf16[768,1536]{1,0:T(8,128)(2,1)} %copy-done, bf16[768,1536]{1,0:T(8,128)(2,1)} %collective-permute-done.g1.rest_2_, ...), custom_call_target="tpu_custom_call" | custom-call | flops 3623878656 | bytes 9437184 | tf_op jit(solution)/shard_map/weight_product/pallas_call | solution.py:63
  74.1 8.9 %weight_product.9 = (bf16[768,1536]{1,0:T(8,128)(2,1)}, f32[8,128]{1,0:T(8,128)}) custom-call(s32[3]{0:T(128)} %add_add_fusion.ids_ref, bf16[1536,3072]{1,0:T(8,128)(2,1)} %a1.15, bf16[1536,3072]{1,0:T(8,128)(2,1)} %a1.15, bf16[768,1536]{1,0:T(8,128)(2,1)} %get-tuple-element.54.g0.rest_1_, bf16[768,1536]{1,0:T(8,128)(2,1)} %collective-permute-done.1.g1.rest_3_, ...), custom_call_target="tpu_custom_call" | custom-call | flops 3623878656 | bytes 9437184 | tf_op jit(solution)/shard_map/weight_product/pallas_call | solution.py:63
  83.0 15.0 %input_product.5 = (bf16[384,3072]{1,0:T(8,128)(2,1)}, f32[8,128]{1,0:T(8,128)}) custom-call(s32[2]{0:T(128)} %pad_add_fusion.2.ids_ref, bf16[3072,3072]{1,0:T(8,128)(2,1)} %w.11, bf16[768,1536]{1,0:T(8,128)(2,1)} %copy-done, bf16[768,1536]{1,0:T(8,128)(2,1)} %get-tuple-element.54.g0.rest_1_, bf16[768,1536]{1,0:T(8,128)(2,1)} %collective-permute-done.g1.rest_2_, ...), custom_call_target="tpu_custom_call" | custom-call | flops 7247757312 | bytes 25952256 | tf_op jit(solution)/shard_map/input_product/pallas_call | solution.py:117
  98.0 2.7 collective-permute-start.3
  101.3 1.5 collective-permute-start.9
  102.8 15.0 %input_product.6 = (bf16[384,3072]{1,0:T(8,128)(2,1)}, f32[8,128]{1,0:T(8,128)}) custom-call(s32[2]{0:T(128)} %pad_add_fusion.1.ids_ref, bf16[3072,3072]{1,0:T(8,128)(2,1)} %w.11, bf16[768,1536]{1,0:T(8,128)(2,1)} %copy-done, bf16[768,1536]{1,0:T(8,128)(2,1)} %get-tuple-element.54.g0.rest_1_, bf16[768,1536]{1,0:T(8,128)(2,1)} %collective-permute-done.g1.rest_2_, ...), custom_call_target="tpu_custom_call" | custom-call | flops 7247757312 | bytes 25952256 | tf_op jit(solution)/shard_map/input_product/pallas_call | solution.py:117
  117.8 4.7 %add_convert_fusion.2 = bf16[384,3072]{1,0:T(8,128)(2,1)} fusion(bf16[384,3072]{1,0:T(8,128)(2,1)} %collective-permute-done.5, bf16[384,3072]{1,0:T(8,128)(2,1)} %get-tuple-element.39), kind=kLoop, calls=%fused_computation.24 | loop fusion | flops 4718592 | bytes 7077888 | tf_op jit(solution)/shard_map/convert_element_type | solution.py:272
  122.4 2.0 collective-permute-start.6
  124.5 15.0 %input_product.7 = (bf16[384,3072]{1,0:T(8,128)(2,1)}, f32[8,128]{1,0:T(8,128)}) custom-call(s32[2]{0:T(128)} %pad_add_fusion.ids_ref, bf16[3072,3072]{1,0:T(8,128)(2,1)} %w.11, bf16[768,1536]{1,0:T(8,128)(2,1)} %copy-done, bf16[768,1536]{1,0:T(8,128)(2,1)} %get-tuple-element.54.g0.rest_1_, bf16[768,1536]{1,0:T(8,128)(2,1)} %collective-permute-done.g1.rest_2_, ...), custom_call_target="tpu_custom_call" | custom-call | flops 7247757312 | bytes 25952256 | tf_op jit(solution)/shard_map/input_product/pallas_call | solution.py:117
  139.5 1.4 copy-done.2
  140.9 9.6 %weight_product.10 = (bf16[768,1536]{1,0:T(8,128)(2,1)}, f32[8,128]{1,0:T(8,128)}) custom-call(s32[3]{0:T(128)} %add_add_fusion.ids_ref, bf16[1536,3072]{1,0:T(8,128)(2,1)} %a1.15, bf16[1536,3072]{1,0:T(8,128)(2,1)} %a1.15, bf16[768,1536]{1,0:T(8,128)(2,1)} %copy-done, bf16[768,1536]{1,0:T(8,128)(2,1)} %collective-permute-done.g1.rest_2_, ...), custom_call_target="tpu_custom_call" | custom-call | flops 3623878656 | bytes 11796480 | tf_op jit(solution)/shard_map/weight_product/pallas_call | solution.py:63
  151.0 4.3 %collective-permute-done.9.rest_0_ = bf16[768,1536]{1,0:T(8,128)(2,1)S(1)} collective-permute-done((bf16[768,1536]{1,0:T(8,128)(2,1)}, bf16[768,1536]{1,0:T(8,128)(2,1)S(1)}, u32[]{:S(2)}, u32[]{:S(2)}) %collective-permute-start.9) | collective-permute-done | bytes 2359328 | tf_op jit(solution)/shard_map/ppermute | solution.py:233
  155.2 2.7 collective-permute-start.2
  157.9 9.7 %weight_product.11 = (bf16[768,1536]{1,0:T(8,128)(2,1)}, f32[8,128]{1,0:T(8,128)}) custom-call(s32[3]{0:T(128)} %add_add_fusion.1.ids_ref, bf16[1536,3072]{1,0:T(8,128)(2,1)} %a1.15, bf16[1536,3072]{1,0:T(8,128)(2,1)} %a1.15, bf16[768,1536]{1,0:T(8,128)(2,1)} %get-tuple-element.54.g0.rest_1_, bf16[768,1536]{1,0:T(8,128)(2,1)} %collective-permute-done.1.g1.rest_3_, ...), custom_call_target="tpu_custom_call" | custom-call | flops 3623878656 | bytes 11796480 | tf_op jit(solution)/shard_map/weight_product/pallas_call | solution.py:63
  167.7 2.0 collective-permute-start.8
  169.7 4.0 %add_convert_fusion.3 = bf16[384,3072]{1,0:T(8,128)(2,1)} fusion(bf16[384,3072]{1,0:T(8,128)(2,1)} %collective-permute-done.3, bf16[384,3072]{1,0:T(8,128)(2,1)S(1)} %copy-done.5), kind=kLoop, calls=%fused_computation.25 | loop fusion | flops 4718592 | bytes 7077888 | tf_op jit(solution)/shard_map/convert_element_type | solution.py:272
  173.6 1.5 collective-permute-start.11
  175.1 4.0 %add_convert_fusion.1 = bf16[384,3072]{1,0:T(8,128)(2,1)} fusion(bf16[384,3072]{1,0:T(8,128)(2,1)} %collective-permute-done.6, bf16[384,3072]{1,0:T(8,128)(2,1)S(1)} %copy-done.4), kind=kLoop, calls=%fused_computation.23 | loop fusion | flops 4718592 | bytes 7077888 | tf_op jit(solution)/shard_map/convert_element_type | solution.py:272
  179.1 2.1 collective-permute-start.4
  181.3 24.6 %collective-permute-done.13.rest_1_ = bf16[768,1536]{1,0:T(8,128)(2,1)} collective-permute-done((bf16[768,1536]{1,0:T(8,128)(2,1)}, bf16[768,1536]{1,0:T(8,128)(2,1)}, u32[]{:S(2)}, u32[]{:S(2)}) %collective-permute-start.13) | collective-permute-done | bytes 2359328 | tf_op jit(solution)/shard_map/ppermute | solution.py:233
  205.9 1.3 collective-permute-start.7
  207.9 1.0 copy.17.b
  209.4 17.5 %update.2 = (f32[1,768,3072]{2,1,0:T(8,128)}, f32[1,768,3072]{2,1,0:T(8,128)}, f32[1,768,3072]{2,1,0:T(8,128)}) custom-call(s32[3]{0:T(128)} %add_add_fusion.3.ids_ref, bf16[1536,3072]{1,0:T(8,128)(2,1)} %a1.15, bf16[1536,3072]{1,0:T(8,128)(2,1)} %a1.15, bf16[768,1536]{1,0:T(8,128)(2,1)} %copy-done, bf16[768,1536]{1,0:T(8,128)(2,1)} %collective-permute-done.g1.rest_2_, ...), custom_call_target="tpu_custom_call" | custom-call | flops 3623878656 | bytes 37748736 | tf_op jit(solution)/shard_map/update/pallas_call | solution.py:169
  226.9 28.0 %collective-permute-done.8.rest_0_ = bf16[768,1536]{1,0:T(8,128)(2,1)} collective-permute-done((bf16[768,1536]{1,0:T(8,128)(2,1)}, bf16[768,1536]{1,0:T(8,128)(2,1)}, u32[]{:S(2)}, u32[]{:S(2)}) %collective-permute-start.8) | collective-permute-done | bytes 2359328 | tf_op jit(solution)/shard_map/ppermute | solution.py:233
  254.9 17.7 %update.3 = (f32[1,768,3072]{2,1,0:T(8,128)}, f32[1,768,3072]{2,1,0:T(8,128)}, f32[1,768,3072]{2,1,0:T(8,128)}) custom-call(s32[3]{0:T(128)} %add_add_fusion.3.ids_ref, bf16[1536,3072]{1,0:T(8,128)(2,1)} %a1.15, bf16[1536,3072]{1,0:T(8,128)(2,1)} %a1.15, ...), custom_call_target="tpu_custom_call", output_to_operand_aliasing={{0}: (11, {}), {1}: (12, {}), {2}: (13, {})} | custom-call | flops 3623878656 | bytes 37748736 | tf_op jit(solution)/shard_map/update/pallas_call | solution.py:169
  272.7 6.3 %add_convert_fusion = bf16[384,3072]{1,0:T(8,128)(2,1)} fusion(bf16[384,3072]{1,0:T(8,128)(2,1)} %collective-permute-done.7, bf16[384,3072]{1,0:T(8,128)(2,1)} %collective-permute-done.4, bf16[384,3072]{1,0:T(8,128)(2,1)} %collective-permute-done.2, bf16[384,3072]{1,0:T(8,128)(2,1)S(1)} %copy-done.6), kind=kLoop, calls=%fused_computation.22 | loop fusion | flops 9437184 | bytes 11796480 | tf_op jit(solution)/shard_map/convert_element_type | solution.py:272
  (42 shorter events, 7.2 us)
Async XLA Ops:
  0.6 8.9 %copy-start.8 = (s32[4,4]{1,0:T(4,128)S(1)}, s32[4,4]{1,0:T(4,128)}, u32[]{:S(2)}) copy-start(s32[4,4]{1,0:T(4,128)} %constant.90.clone) | copy-start | bytes 196
  9.0 14.1 %copy-start = (bf16[768,1536]{1,0:T(8,128)(2,1)}, bf16[768,1536]{1,0:T(8,128)(2,1)S(1)}, u32[]{:S(2)}) copy-start(bf16[768,1536]{1,0:T(8,128)(2,1)S(1)} %get-tuple-element.55.g0.rest_0_) | copy-start | bytes 7077892
  9.0 14.1 %collective-permute-start = (bf16[768,1536]{1,0:T(8,128)(2,1)S(1)}, bf16[768,1536]{1,0:T(8,128)(2,1)}, u32[]{:S(2)}, u32[]{:S(2)}) collective-permute-start(bf16[768,1536]{1,0:T(8,128)(2,1)S(1)} %get-tuple-element.55.g0.rest_0_), channel_id=1, source_target_pairs={{0,4},{4,0},{1,5},{5,1},{2,6},{6,2},{3,7},{7,3},{8,12},{12,8},{9,1... | collective-permute-start | bytes 7077896 | tf_op jit(solution)/shard_map/ppermute | solution.py:233
  9.4 22.5 %collective-permute-start.1 = (bf16[768,1536]{1,0:T(8,128)(2,1)}, bf16[768,1536]{1,0:T(8,128)(2,1)}, u32[]{:S(2)}, u32[]{:S(2)}) collective-permute-start(bf16[768,1536]{1,0:T(8,128)(2,1)} %get-tuple-element.54.g0.rest_1_), channel_id=1, source_target_pairs={{0,4},{4,0},{1,5},{5,1},{2,6},{6,2},{3,7},{7,3},{8,12},{12,8},{9,1... | collective-permute-start | bytes 7077896 | tf_op jit(solution)/shard_map/ppermute | solution.py:233
  55.6 62.2 %collective-permute-start.5 = (bf16[384,3072]{1,0:T(8,128)(2,1)}, bf16[384,3072]{1,0:T(8,128)(2,1)}, u32[]{:S(2)}, u32[]{:S(2)}) collective-permute-start(bf16[384,3072]{1,0:T(8,128)(2,1)} %get-tuple-element.39), channel_id=1, source_target_pairs={{0,1},{3,2},{4,5},{7,6},{8,9},{11,10},{12,13},{15,14},{16,17},{19,... | collective-permute-start | bytes 7077896 | tf_op jit(solution)/shard_map/ppermute | solution.py:269
  63.8 75.7 %collective-permute-start.10 = (bf16[768,1536]{1,0:T(8,128)(2,1)}, bf16[768,1536]{1,0:T(8,128)(2,1)S(1)}, u32[]{:S(2)}, u32[]{:S(2)}) collective-permute-start(bf16[768,1536]{1,0:T(8,128)(2,1)} %get-tuple-element.42), channel_id=1, source_target_pairs={{0,8},{8,0},{16,24},{24,16},{1,9},{9,1},{17,25},{25,17},{2,10},{10... | collective-permute-start | bytes 7077896 | tf_op jit(solution)/shard_map/ppermute | solution.py:233
  98.0 69.7 %collective-permute-start.3 = (bf16[384,3072]{1,0:T(8,128)(2,1)}, bf16[384,3072]{1,0:T(8,128)(2,1)}, u32[]{:S(2)}, u32[]{:S(2)}) collective-permute-start(bf16[384,3072]{1,0:T(8,128)(2,1)} %get-tuple-element.38), channel_id=1, source_target_pairs={{0,1},{3,2},{4,5},{7,6},{8,9},{11,10},{12,13},{15,14},{16,17},{19,... | collective-permute-start | bytes 7077896 | tf_op jit(solution)/shard_map/ppermute | solution.py:269
  100.7 78.4 %collective-permute-start.12 = (bf16[768,1536]{1,0:T(8,128)(2,1)}, bf16[768,1536]{1,0:T(8,128)(2,1)S(1)}, u32[]{:S(2)}, u32[]{:S(2)}) collective-permute-start(bf16[768,1536]{1,0:T(8,128)(2,1)} %get-tuple-element.46), channel_id=1, source_target_pairs={{0,8},{8,0},{16,24},{24,16},{1,9},{9,1},{17,25},{25,17},{2,10},{10... | collective-permute-start | bytes 7077896 | tf_op jit(solution)/shard_map/ppermute | solution.py:233
  101.3 54.0 %collective-permute-start.9 = (bf16[768,1536]{1,0:T(8,128)(2,1)}, bf16[768,1536]{1,0:T(8,128)(2,1)S(1)}, u32[]{:S(2)}, u32[]{:S(2)}) collective-permute-start(bf16[768,1536]{1,0:T(8,128)(2,1)} %get-tuple-element.41), channel_id=1, source_target_pairs={{0,16},{8,24},{16,0},{24,8},{1,17},{9,25},{17,1},{25,9},{2,18},{10... | collective-permute-start | bytes 7077896 | tf_op jit(solution)/shard_map/ppermute | solution.py:233
  122.4 51.2 %collective-permute-start.6 = (bf16[384,3072]{1,0:T(8,128)(2,1)}, bf16[384,3072]{1,0:T(8,128)(2,1)}, u32[]{:S(2)}, u32[]{:S(2)}) collective-permute-start(bf16[384,3072]{1,0:T(8,128)(2,1)} %add_convert_fusion.2), channel_id=1, source_target_pairs={{1,2},{2,1},{5,6},{6,5},{9,10},{10,9},{13,14},{14,13},{17,18},{18,... | collective-permute-start | bytes 7077896 | tf_op jit(solution)/shard_map/ppermute | solution.py:269
  139.5 1.4 copy-start.2
  150.5 55.4 %collective-permute-start.13 = (bf16[768,1536]{1,0:T(8,128)(2,1)}, bf16[768,1536]{1,0:T(8,128)(2,1)}, u32[]{:S(2)}, u32[]{:S(2)}) collective-permute-start(bf16[768,1536]{1,0:T(8,128)(2,1)} %get-tuple-element.47), channel_id=1, source_target_pairs={{0,16},{8,24},{16,0},{24,8},{1,17},{9,25},{17,1},{25,9},{2,18},{10... | collective-permute-start | bytes 7077896 | tf_op jit(solution)/shard_map/ppermute | solution.py:233
  155.2 2.7 copy-start.3
  155.2 117.4 %collective-permute-start.2 = (bf16[384,3072]{1,0:T(8,128)(2,1)}, bf16[384,3072]{1,0:T(8,128)(2,1)}, u32[]{:S(2)}, u32[]{:S(2)}) collective-permute-start(bf16[384,3072]{1,0:T(8,128)(2,1)} %get-tuple-element.37), channel_id=1, source_target_pairs={{0,1},{3,2},{4,5},{7,6},{8,9},{11,10},{12,13},{15,14},{16,17},{19,... | collective-permute-start | bytes 7077896 | tf_op jit(solution)/shard_map/ppermute | solution.py:269
  157.9 11.7 %copy-start.5 = (bf16[384,3072]{1,0:T(8,128)(2,1)S(1)}, bf16[384,3072]{1,0:T(8,128)(2,1)}, u32[]{:S(2)}) copy-start(bf16[384,3072]{1,0:T(8,128)(2,1)} %get-tuple-element.38) | copy-start | bytes 7077892
  167.6 7.5 %copy-start.4 = (bf16[384,3072]{1,0:T(8,128)(2,1)S(1)}, bf16[384,3072]{1,0:T(8,128)(2,1)}, u32[]{:S(2)}) copy-start(bf16[384,3072]{1,0:T(8,128)(2,1)} %get-tuple-element.37) | copy-start | bytes 7077892
  167.7 87.2 %collective-permute-start.8 = (bf16[768,1536]{1,0:T(8,128)(2,1)}, bf16[768,1536]{1,0:T(8,128)(2,1)}, u32[]{:S(2)}, u32[]{:S(2)}) collective-permute-start(bf16[768,1536]{1,0:T(8,128)(2,1)} %get-tuple-element.40), channel_id=1, source_target_pairs={{0,16},{8,24},{16,0},{24,8},{1,17},{9,25},{17,1},{25,9},{2,18},{10... | collective-permute-start | bytes 7077896 | tf_op jit(solution)/shard_map/ppermute | solution.py:233
  173.6 34.2 %copy-start.7 = (s32[1,768]{1,0:T(1,128)S(1)}, s32[1,768]{1,0:T(1,128)}, u32[]{:S(2)}) copy-start(s32[1,768]{1,0:T(1,128)} %param.16) | copy-start | bytes 9220
  173.6 81.2 %collective-permute-start.11 = (bf16[768,1536]{1,0:T(8,128)(2,1)}, bf16[768,1536]{1,0:T(8,128)(2,1)}, u32[]{:S(2)}, u32[]{:S(2)}) collective-permute-start(bf16[768,1536]{1,0:T(8,128)(2,1)} %get-tuple-element.45), channel_id=1, source_target_pairs={{0,8},{8,0},{16,24},{24,16},{1,9},{9,1},{17,25},{25,17},{2,10},{10... | collective-permute-start | bytes 7077896 | tf_op jit(solution)/shard_map/ppermute | solution.py:233
  179.1 30.3 %copy-start.1 = (bf16[768,1536]{1,0:T(8,128)(2,1)}, bf16[768,1536]{1,0:T(8,128)(2,1)S(1)}, u32[]{:S(2)}) copy-start(bf16[768,1536]{1,0:T(8,128)(2,1)S(1)} %collective-permute-done.12.rest_0_) | copy-start | bytes 7077892
  179.1 93.5 %collective-permute-start.4 = (bf16[384,3072]{1,0:T(8,128)(2,1)}, bf16[384,3072]{1,0:T(8,128)(2,1)}, u32[]{:S(2)}, u32[]{:S(2)}) collective-permute-start(bf16[384,3072]{1,0:T(8,128)(2,1)} %add_convert_fusion.3), channel_id=1, source_target_pairs={{1,2},{2,1},{5,6},{6,5},{9,10},{10,9},{13,14},{14,13},{17,18},{18,... | collective-permute-start | bytes 7077896 | tf_op jit(solution)/shard_map/ppermute | solution.py:269
  205.9 66.7 %collective-permute-start.7 = (bf16[384,3072]{1,0:T(8,128)(2,1)}, bf16[384,3072]{1,0:T(8,128)(2,1)}, u32[]{:S(2)}, u32[]{:S(2)}) collective-permute-start(bf16[384,3072]{1,0:T(8,128)(2,1)} %add_convert_fusion.1), channel_id=1, source_target_pairs={{1,0},{2,3},{5,4},{6,7},{9,8},{10,11},{13,12},{14,15},{17,16},{18,... | collective-permute-start | bytes 7077896 | tf_op jit(solution)/shard_map/ppermute | solution.py:269
  254.9 17.8 %copy-start.6 = (bf16[384,3072]{1,0:T(8,128)(2,1)S(1)}, bf16[384,3072]{1,0:T(8,128)(2,1)}, u32[]{:S(2)}) copy-start(bf16[384,3072]{1,0:T(8,128)(2,1)} %get-tuple-element.36) | copy-start | bytes 7077892

commit v2 on v0

v2 whole, which is shorter than its diff:
```python
import jax
import jax.numpy as jnp
from jax import lax
from jax.experimental import pallas as pl
from jax.experimental.pallas import tpu as pltpu
from jax.sharding import PartitionSpec as P

D = 6144


learning_rate = 0.5
VMEM_LIMIT = 24 * 1024 * 1024
LANES = 128
TOKEN = (8, LANES)
HINT = 20


def gelu_slope(values):
    normal_cdf = 0.5 * (1.0 + lax.erf(values * 0.7071067811865476))
    density = jnp.exp(-0.5 * values * values) * 0.3989422804014327
    return normal_cdf + values * density


def times_slope(out_grad, pre_act):
    return (out_grad.astype(jnp.float32) * gelu_slope(pre_act.astype(jnp.float32))).astype(jnp.bfloat16)


def dot(a, b, dims):
    return lax.dot_general(a, b, (dims, ((), ())), preferred_element_type=jnp.float32)


def params():
    return pltpu.CompilerParams(dimension_semantics=("arbitrary",), vmem_limit_bytes=VMEM_LIMIT)


def anywhere(arrays):
    return [pl.BlockSpec(memory_space=pl.ANY)] * len(arrays)


def block_width(width, most):
    return max(b for b in range(LANES, min(width, most) + 1, LANES) if width % b == 0)


def block_rows(rows, most):
    return max(b for b in range(16, min(rows, most) + 1, 16) if rows % b == 0)


def cost(flops, bytes_accessed):
    return pl.CostEstimate(flops=flops // HINT, bytes_accessed=bytes_accessed // HINT, transcendentals=0)


def held(array):
    return pltpu.with_memory_space_constraint(array, pltpu.HBM)


def clipped(first, count):
    return lambda j, ids: (0, jnp.clip(j - first, 0, count - 1))


def weight_product(inputs, mine, theirs, ids, share, bn, jobs, order, base=None):
    half = mine[0].shape[0]
    begins, steps = [], 0
    for job in jobs:
        begins.append(steps)
        steps += sum(job[4])
    kind = jnp.bfloat16 if base is None else jnp.float32

    def bits_at(j):
        bits = jobs[0][0]
        for begin, job in zip(begins[1:], jobs[1:]):
            bits = jnp.where(j >= begin, job[0], bits)
        return bits

    operands = [inputs, inputs]
    in_specs = [
        pl.BlockSpec((half, share), lambda j, ids: (ids[1], ids[0] ^ bits_at(j))),
        pl.BlockSpec((half, share), lambda j, ids: (1 - ids[1], ids[0] ^ bits_at(j))),
    ]
    out_specs, out_shape, plans = [], [], []
    for begin, (_, piece, first, received, outs) in zip(begins, jobs):
        count = sum(outs)

        def column(j, ids, begin=begin, first=first, count=count):
            return (0, first + jnp.clip(j - begin, 0, count - 1))

        grads = (len(operands), len(operands) + 1)
        operands += [mine[piece], theirs[piece]]
        in_specs += [pl.BlockSpec((half, bn), column)] * 2
        adds, at = [], begin
        for blocks, array in received:
            adds.append((at, at + blocks, len(operands)))
            operands.append(array)
            in_specs.append(pl.BlockSpec((share, bn), clipped(at, blocks)))
            at += blocks
        old = None
        if base is not None:
            old = len(operands)
            operands.append(held(base[0]))
            place = sum(m.shape[1] for m in mine[:piece]) // bn + first
            in_specs.append(
                pl.BlockSpec(
                    (share, bn),
                    lambda j, ids, begin=begin, place=place, count=count: (ids[0], place + jnp.clip(j - begin, 0, count - 1)),
                )
            )
        written, at = [], begin
        for blocks in outs:
            written.append((at, at + blocks, len(out_specs)))
            out_specs.append(pl.BlockSpec((share, bn), clipped(at, blocks)))
            out_shape.append(jax.ShapeDtypeStruct((share, blocks * bn), kind))
            at += blocks
        plans.append((begin, begin + count, grads, adds, old, written))

    def kernel(ids_ref, *refs):
        outs, token = refs[-1 - len(out_specs) : -1], refs[-1]
        step = pl.program_id(0)
        token[...] = jnp.zeros_like(token)
        for begin, end, grads, adds, old, written in plans:

            @pl.when((step >= begin) & (step < end))
            def _():
                result = sum(dot(refs[k][...], refs[g][...], ((0,), (0,))) for k, g in enumerate(grads))
                if adds:
                    more = refs[adds[0][2]][...]
                    for since, _, index in adds[1:]:
                        more = jnp.where(step >= since, refs[index][...], more)
                    result = result + more.astype(jnp.float32)
                if old is not None:
                    result = refs[old][...].astype(jnp.float32) - base[1] * result
                for since, until, index in written:

                    @pl.when((step >= since) & (step < until))
                    def _():
                        outs[index][...] = result.astype(kind)

    *arrays, token = pl.pallas_call(
        kernel,
        grid_spec=pltpu.PrefetchScalarGridSpec(
            num_scalar_prefetch=1,
            grid=(steps,),
            in_specs=in_specs + anywhere(order),
            out_specs=out_specs + [pl.BlockSpec(TOKEN, lambda j, ids: (0, 0))],
        ),
        out_shape=out_shape + [jax.ShapeDtypeStruct(TOKEN, jnp.float32)],
        compiler_params=params(),
        cost_estimate=cost(4 * half * share * bn * steps, 2 * steps * bn * (2 * half + share)),
        name="weight_product",
    )(ids, *operands, *order)
    order[:] = [token]
    return arrays


def chunk_of(turn, place, places):
    above = jnp.where(turn < places - 1 - place, places - 1 - turn, turn - (places - 1 - place))
    below = jnp.where(turn < place, turn, places - 1 - (turn - place))
    return jnp.where(turn == places - 1, place, jnp.where(2 * place < places, above, below))


def input_product(weight, mine, theirs, ids, turns, places, first, wide, multiplier, order):
    hidden = weight.shape[1]
    per_half = places // 2
    rows = mine[0].shape[0] // per_half
    bn = block_width(wide, 512)
    steps = wide // bn
    count = len(mine)

    def kernel(ids_ref, w, *rest):
        own, other = rest[:count], rest[count : 2 * count]
        (token, lhs, sem), outs = rest[-3:], rest[-3 - len(turns) : -3]

        @pl.when(pl.program_id(0) == 0)
        def _():
            token[...] = jnp.zeros_like(token)
            copies = []
            for k, turn in enumerate(turns):
                chunk = chunk_of(turn, ids_ref[2], places)
                here = chunk // per_half == ids_ref[1]
                at = 0
                for g in range(count):
                    columns = own[g].shape[1]
                    rows_at = pl.ds(pl.multiple_of((chunk % per_half) * rows, rows), rows)
                    target = lhs.at[pl.ds(k * rows, rows), pl.ds(at, columns)]
                    near = pltpu.make_async_copy(own[g].at[rows_at, :], target, sem.at[k, g])
                    far = pltpu.make_async_copy(other[g].at[rows_at, :], target, sem.at[k, g])
                    pl.when(here)(near.start)
                    pl.when(jnp.logical_not(here))(far.start)
                    copies.append(near)
                    at += columns
            for copy in copies:
                copy.wait()

        result = (dot(lhs[...], w[...], ((1,), (1,))) * multiplier).astype(jnp.bfloat16)
        for k, out in enumerate(outs):
            out[...] = result[k * rows : (k + 1) * rows]

    *arrays, token = pl.pallas_call(
        kernel,
        grid_spec=pltpu.PrefetchScalarGridSpec(
            num_scalar_prefetch=1,
            grid=(steps,),
            in_specs=[pl.BlockSpec((bn, hidden), lambda j, ids: (first // bn + j, 0))]
            + anywhere(mine)
            + anywhere(theirs)
            + anywhere(order),
            out_specs=[pl.BlockSpec((rows, bn), lambda j, ids: (0, j))] * len(turns)
            + [pl.BlockSpec(TOKEN, lambda j, ids: (0, 0))],
            scratch_shapes=[
                pltpu.VMEM((len(turns) * rows, hidden), jnp.bfloat16),
                pltpu.SemaphoreType.DMA((len(turns), count)),
            ],
        ),
        out_shape=[jax.ShapeDtypeStruct((rows, wide), jnp.bfloat16)] * len(turns)
        + [jax.ShapeDtypeStruct(TOKEN, jnp.float32)],
        compiler_params=params(),
        cost_estimate=cost(
            2 * len(turns) * rows * wide * hidden, 2 * (wide * hidden + len(turns) * rows * (hidden + wide))
        ),
        name="input_product",
    )(ids, held(weight), *mine, *theirs, *order)
    order[:] = [token]
    return arrays


def update(base, last, mean, square, blend, column, bn, scale, before, order):
    share, width = base.shape
    rows = block_rows(share, 256)
    across, place = width // bn, column // bn

    def kernel(old, arrived, m, s, b, *rest):
        new_w, new_m, new_s, token = rest[-4:]
        token[...] = jnp.zeros_like(token)
        stepped = old[...] - scale * arrived[...].astype(jnp.float32)
        new_w[0] = stepped
        new_m[0] = m[0] + b[...] * (stepped - m[0])
        new_s[0] = s[0] + b[...] * (stepped * stepped - s[0])

    moment = pl.BlockSpec((1, rows, bn), lambda i: (0, i // across, place + i % across))
    block = pl.BlockSpec((rows, bn), lambda i: (i // across, i % across))
    *outs, token = pl.pallas_call(
        kernel,
        grid=(share // rows * across,),
        in_specs=[block, block, moment, moment, pl.BlockSpec((rows, 1), lambda i: (i // across, 0))]
        + anywhere(before)
        + anywhere(order),
        out_specs=[moment] * 3 + [pl.BlockSpec(TOKEN, lambda i: (0, 0))],
        out_shape=[jax.ShapeDtypeStruct(mean.shape, jnp.float32)] * 3 + [jax.ShapeDtypeStruct(TOKEN, jnp.float32)],
        input_output_aliases={5 + k: k for k in range(len(before))},
        compiler_params=params(),
        cost_estimate=cost(10 * share * width, share * width * 26),
        name="update",
    )(base, last, held(mean), held(square), blend, *before, *order)
    order[:] = [token]
    return outs


def plain_body(inputs, pre_act, out_grad, weight, swag_mean, swag_square, snapshots, update_flag):
    row_width = weight.shape[0]
    groups = lax.axis_size("dp")
    share_rows = row_width // groups
    multiplier = 1.0 / D**0.5
    local_grad = times_slope(out_grad, pre_act)
    portion = lax.all_gather(local_grad, "row", axis=0, tiled=True)
    grad_acc = dot(inputs, portion, ((0,), (0,)))
    term_rows = dot(portion, weight, ((1,), (1,))) * multiplier
    input_grad = lax.psum_scatter(term_rows.astype(jnp.bfloat16), "col", scatter_dimension=0, tiled=True)
    share = lax.psum_scatter(grad_acc.astype(jnp.bfloat16), "dp", scatter_dimension=0, tiled=True).astype(jnp.float32)
    own_rows = lax.dynamic_slice_in_dim(weight, lax.axis_index("dp") * share_rows, share_rows, 0).astype(jnp.float32)
    total_tokens = inputs.shape[0] * groups
    stepped = own_rows - learning_rate * (share / total_tokens**0.5)
    blend = update_flag[0].astype(jnp.float32)[:, None] / (snapshots[0].astype(jnp.float32) + 1.0)
    mean_new = swag_mean[0] + blend * (stepped - swag_mean[0])
    square_new = swag_square[0] + blend * (stepped * stepped - swag_square[0])
    return (input_grad, stepped[None], mean_new[None], square_new[None])


def plus(terms, order):
    rows, width = terms[0].shape
    some = block_rows(rows, 192)

    def kernel(*refs):
        out, token = refs[-2:]
        token[...] = jnp.zeros_like(token)
        out[...] = sum(ref[...].astype(jnp.float32) for ref in refs[: len(terms)]).astype(out.dtype)

    block = pl.BlockSpec((some, width), lambda i: (i, 0))
    out, token = pl.pallas_call(
        kernel,
        grid=(rows // some,),
        in_specs=[block] * len(terms) + anywhere(order),
        out_specs=[block, pl.BlockSpec(TOKEN, lambda i: (0, 0))],
        out_shape=[jax.ShapeDtypeStruct((rows, width), jnp.bfloat16), jax.ShapeDtypeStruct(TOKEN, jnp.float32)],
        compiler_params=params(),
        cost_estimate=cost(rows * width * len(terms), 2 * rows * width * (len(terms) + 1)),
        name="plus",
    )(*terms, *order)
    order[:] = [token]
    return out


def plus_side_by_side(groups, order):
    rows, width = groups[0][0].shape
    some = block_rows(rows, 96)
    sizes = [len(group) for group in groups]

    def kernel(*refs):
        out, at = refs[-1], 0
        for k, size in enumerate(sizes):
            total = sum(ref[...].astype(jnp.float32) for ref in refs[at : at + size])
            out[:, k * width : (k + 1) * width] = total.astype(out.dtype)
            at += size

    return pl.pallas_call(
        kernel,
        grid=(rows // some,),
        in_specs=[pl.BlockSpec((some, width), lambda i: (i, 0))] * sum(sizes) + anywhere(order),
        out_specs=pl.BlockSpec((some, width * len(groups)), lambda i: (i, 0)),
        out_shape=jax.ShapeDtypeStruct((rows, width * len(groups)), jnp.bfloat16),
        compiler_params=params(),
        cost_estimate=cost(rows * width * sum(sizes), 2 * rows * width * (sum(sizes) + len(groups))),
        name="plus_side_by_side",
    )(*(a for group in groups for a in group), *order)


def body(inputs, pre_act, out_grad, weight, swag_mean, swag_square, snapshots, update_flag):
    tokens = inputs.shape[0]
    half = pre_act.shape[0]
    width, hidden = weight.shape
    groups, cols = lax.axis_size("dp"), lax.axis_size("col")
    share = width // groups
    multiplier = 1.0 / D**0.5
    scale = learning_rate / (tokens * groups) ** 0.5
    ids = jnp.stack([lax.axis_index(axis) for axis in ("dp", "row", "col")]).astype(jnp.int32)

    def swap(value, axis, bit):
        return lax.ppermute(value, axis, [(i, i ^ bit) for i in range(lax.axis_size(axis))])

    piece = hidden // 2
    first = times_slope(out_grad[:, :piece], pre_act[:, :piece])
    rest = lax.optimization_barrier((out_grad, pre_act, first))
    second = times_slope(rest[0][:, piece:], rest[1][:, piece:])
    mine = [first, second]
    theirs = [swap(value, "row", 1) for value in mine]
    blend = update_flag[0].astype(jnp.float32)[:, None] / (snapshots[0].astype(jnp.float32) + 1.0)

    order = []
    bn = block_width(piece, 512)
    blocks = piece // bn
    small = max(1, blocks // 3)
    large = blocks - small

    def products(*jobs, base=None):
        return weight_product(inputs, mine, theirs, ids, share, bn, jobs, order, base)

    parts = 2
    part = width // parts

    def chunks(turns, k):
        return input_product(weight, mine, theirs, ids, turns, cols, k * part, part, multiplier, order)

    near, far = (1, 2), (2, 1)
    middle = ((1, 2), (2, 1))

    def outer(value):
        return swap(value, "col", 1)

    def across(value):
        return lax.ppermute(value, "col", middle)

    (pass_a0,) = products((3, 0, 0, [], [small]))
    got_pass_a0 = swap(pass_a0, "dp", near[0])
    (pass_b0,) = products((3, 1, 0, [], [small]))
    got_pass_b0 = swap(pass_b0, "dp", near[1])
    (c0_a,) = chunks([0], 0)
    got_0a = outer(c0_a)
    pass_a1, pass_b1 = products((3, 0, small, [], [large]), (3, 1, small, [], [large]))
    got_pass_a1, got_pass_b1 = swap(pass_a1, "dp", near[0]), swap(pass_b1, "dp", near[1])
    c0_b, c1_b = chunks([0, 1], 1)
    got_0b, got_1b = outer(c0_b), outer(c1_b)
    keep_a, keep_b = products((near[0], 0, 0, [], [blocks]), (near[1], 1, 0, [], [blocks]))
    got_keep_a, got_keep_b = swap(keep_a, "dp", near[0]), swap(keep_b, "dp", near[1])
    order += [got_pass_a0, got_pass_b0]
    got_m1a = across(plus([c0_a, got_0a], order))
    c1_a, c2_a, c3_a = chunks([1, 2, 3], 0)
    got_1a = outer(c1_a)
    order += [got_pass_a1, got_pass_b1]
    got_m1b = across(plus([c0_b, got_0b], order))
    c2_b, c3_b = chunks([2, 3], 1)
    last_b0, last_b1, last_a0, last_a1 = products(
        (far[1], 1, 0, [(small, got_pass_b0), (large, got_pass_b1)], [large, small]),
        (far[0], 0, 0, [(small, got_pass_a0), (large, got_pass_a1)], [large, small]),
    )
    got_last_b = [swap(v, "dp", far[1]) for v in (last_b0, last_b1)]
    got_last_a = [swap(v, "dp", far[0]) for v in (last_a0, last_a1)]
    got_2a = outer(plus([c2_a, got_m1a], order))
    got_m2b = across(plus([c1_b, got_1b], order))
    *base_b, base_a0, base_a1 = products(
        (0, 1, 0, [(blocks, got_keep_b)], [large, small]),
        (0, 0, 0, [(blocks, got_keep_a)], [large, small]),
        base=(weight, scale),
    )
    base_a = [base_a0, base_a1]
    got_2b = outer(plus([c2_b, got_m1b], order))
    got_m2a = across(plus([c1_a, got_1a], order))
    order += [got_2a, got_m2b]
    outs = ()
    for k in range(2):
        for start, base, last in ((piece, base_b, got_last_b), (0, base_a, got_last_a)):
            column = start + k * large * bn
            outs = update(base[k], last[k], swag_mean, swag_square, blend, column, bn, scale, outs, order)
    input_grad = plus_side_by_side([[c3_a, got_2a, got_m2a], [c3_b, got_2b, got_m2b]], order)
    return (input_grad, *outs)


def solution(mesh):
    in_specs = (
        P("dp", "row"),
        P(("dp", "row"), "col"),
        P(("dp", "row"), "col"),
        P("row", "col"),
        P("dp", "row", "col"),
        P("dp", "row", "col"),
        P(),
        P("dp", "row"),
    )
    out_specs = (
        P(("dp", "col"), "row"),
        P("dp", "row", "col"),
        P("dp", "row", "col"),
        P("dp", "row", "col"),
    )
    scheduled = dict(mesh.shape) == {"dp": 4, "row": 2, "col": 4}
    return jax.shard_map(
        body if scheduled else plain_body, mesh=mesh, in_specs=in_specs, out_specs=out_specs, check_vma=False
    )
```

time: 421 us -> 239 us (0.57)
  waiting for transfers between devices: 242 us -> 23.2 us
  Pallas kernels: 0 us -> 153 us
  matrix products: 74.1 us -> 0 us
  local copies, waits for them, and re-layouts: 60 us -> 17.4 us
  starting transfers between devices: 0.3 us -> 32.7 us
  other arithmetic: 29.1 us -> 9.48 us
  between operations: 14.4 us -> 1.73 us
    reduce_scatter x2 -> x0, waiting for transfers between devices: 217 us -> none  [the longest x1 115 us: body(): lax.psum_scatter(term_rows.astype(jnp.bfloat16), 'col', scatter_dimension...]
    pallas_call x0 -> x21, Pallas kernels: none -> 153 us  [the longest x6 58.1 us: weight_product(): pl.pallas_call(kernel, grid_spec=pltpu.PrefetchScalarGridSpec(num_scalar_...]
    dot_general x2 -> x0, matrix products: 74.1 us -> none  [the longest x1 37.3 us: body(): lax.dot_general(portion, weight, (((1,), (1,)), ((), ())), preferred_elem...]
    unnamed x8 -> x76, local copies, waits for them, and re-layouts: 55 us -> 17.2 us
    ppermute x0 -> x22, starting transfers between devices: none -> 32.7 us  [the longest x18 26.9 us: swap(): lax.ppermute(value, axis, [(i, i ^ bit) for i in range(lax.axis_size(axis...]
    all_gather x1 -> x0, waiting for transfers between devices: 24.7 us -> none  [body(): portion = lax.all_gather(local_grad, 'row', axis=0, tiled=True)]
    ppermute x0 -> x22, waiting for transfers between devices: none -> 23.2 us  [the longest x18 23.2 us: swap(): lax.ppermute(value, axis, [(i, i ^ bit) for i in range(lax.axis_size(axis...]
    broadcast_in_dim x1 -> x0, other arithmetic: 20.9 us -> none  [body(): return (input_grad, stepped[None], mean_new[None], square_new[None])]
  transfers between devices with their start and end apart: 3 -> 22, of which waited for: 3 -> 2; matrix products, arithmetic and copies ran while one was open for 28% -> 2% of each run, Pallas kernels for 0% -> 57%
where the time goes in v2:
time: 239 us; the launch traced here: 238 us
  Pallas kernels  153 us (64%)
  starting transfers between devices  32.7 us (14%)
  waiting for transfers between devices  23.2 us (10%)
  local copies, waits for them, and re-layouts  17.4 us (7%)
  other arithmetic  9.48 us (4%)
    pallas_call x6, Pallas kernels, weight_product(): pl.pallas_call(kernel, grid_spec=pltpu.PrefetchScalarGridSpec(num_scalar_...  58.1 us
    pallas_call x4, Pallas kernels, input_product(): pl.pallas_call(kernel, grid_spec=pltpu.PrefetchScalarGridSpec(num_scalar_...  54.2 us
    ppermute x18, starting transfers between devices, swap(): lax.ppermute(value, axis, [(i, i ^ bit) for i in range(lax.axis_size(axis...  26.9 us
    pallas_call x4, Pallas kernels, update(): pl.pallas_call(kernel, grid=(share // rows * across,), in_specs=[block, b...  26.7 us
    ppermute x18, waiting for transfers between devices, swap(): lax.ppermute(value, axis, [(i, i ^ bit) for i in range(lax.axis_size(axis...  23.2 us
    unnamed x76, local copies, waits for them, and re-layouts  17.2 us
    pallas_call x6, Pallas kernels, plus(): pl.pallas_call(kernel, grid=(rows // some,), in_specs=[block] * len(terms...  10.3 us
    convert_element_type x2, other arithmetic, times_slope(): (out_grad.astype(jnp.float32) * gelu_slope(pre_act.astype(jnp.float32)))....  9.4 us
  transfers between devices with their start and end apart: 22, of which 2 were waited for; matrix products, arithmetic and copies ran while one was open for 2% of the time, Pallas kernels for 57%

profile of v2, /device:TPU:0, one launch (start us, length us, event | category | flops | bytes accessed | tf_op | source)
XLA Modules:
  0.0 237.9 jit_solution(14006746406371858498)
XLA Ops:
  0.6 4.5 %fusion.15.refs_2_.rest_0_.refs_6_ = bf16[768,1536]{1,0:T(8,128)(2,1)S(1)} fusion(bf16[768,3072]{1,0:T(8,128)(2,1)} %param.9, bf16[768,3072]{1,0:T(8,128)(2,1)} %param.10), kind=kLoop, calls=%fused_computation.23 | loop fusion | flops 14155776 | bytes 7077888 | tf_op jit(solution)/shard_map/convert_element_type | solution.py:25
  5.7 4.9 %fusion.14.refs_2_.rest_1_.refs_4_ = bf16[768,1536]{1,0:T(8,128)(2,1)} fusion(bf16[768,3072]{1,0:T(8,128)(2,1)S(1)} %copy-done.33, bf16[768,3072]{1,0:T(8,128)(2,1)} %param.10), kind=kLoop, calls=%fused_computation.22 | loop fusion | flops 14155776 | bytes 7077888 | tf_op jit(solution)/shard_map/convert_element_type | solution.py:25
  10.7 3.7 %copy-done = bf16[1536,3072]{1,0:T(8,128)(2,1)S(1)} copy-done((bf16[1536,3072]{1,0:T(8,128)(2,1)S(1)}, bf16[1536,3072]{1,0:T(8,128)(2,1)}, u32[]{:S(2)}) %copy-start) | copy-done | bytes 9437208
  14.4 3.3 %weight_product.6 = (bf16[768,512]{1,0:T(8,128)(2,1)S(1)}, f32[8,128]{1,0:T(8,128)S(1)}) custom-call(s32[3]{0:T(128)S(1)} %pad_add_fusion.ids_ref, bf16[1536,3072]{1,0:T(8,128)(2,1)S(1)} %copy-done, bf16[1536,3072]{1,0:T(8,128)(2,1)S(1)} %copy-done, bf16[768,1536]{1,0:T(8,128)(2,1)S(1)} %fusion.15.refs_2_.rest_0_.refs_6_, ...), custom_call_target="tpu_custom_call" | custom-call | flops 60397976 | bytes 117964 | tf_op jit(solution)/shard_map/weight_product/pallas_call | solution.py:136
  17.7 3.4 %weight_product.7 = (bf16[768,512]{1,0:T(8,128)(2,1)S(1)}, f32[8,128]{1,0:T(8,128)S(1)}) custom-call(s32[3]{0:T(128)S(1)} %pad_add_fusion.ids_ref, bf16[1536,3072]{1,0:T(8,128)(2,1)S(1)} %copy-done, bf16[1536,3072]{1,0:T(8,128)(2,1)S(1)} %copy-done, bf16[768,1536]{1,0:T(8,128)(2,1)} %fusion.14.refs_2_.rest_1_.refs_4_, ...), custom_call_target="tpu_custom_call" | custom-call | flops 60397976 | bytes 117964 | tf_op jit(solution)/shard_map/weight_product/pallas_call | solution.py:136
  21.1 10.2 %input_product.4 = (bf16[384,1536]{1,0:T(8,128)(2,1)S(1)}, f32[8,128]{1,0:T(8,128)S(1)}) custom-call(s32[3]{0:T(128)S(1)} %pad_add_fusion.ids_ref, bf16[3072,3072]{1,0:T(8,128)(2,1)} %refs_9_.1, bf16[768,1536]{1,0:T(8,128)(2,1)S(1)} %fusion.15.refs_2_.rest_0_.refs_6_, bf16[768,1536]{1,0:T(8,128)(2,1)} %fusion.14.refs_2_.rest_1_.refs_4_, ...), custom_call_target="tpu_custom_call" | custom-call | flops 181193936 | bytes 648806 | tf_op jit(solution)/shard_map/input_product/pallas_call | solution.py:196
  31.3 3.1 %collective-permute-start.2 = (bf16[384,1536]{1,0:T(8,128)(2,1)S(1)}, bf16[384,1536]{1,0:T(8,128)(2,1)S(1)}, u32[]{:S(2)}, u32[]{:S(2)}) collective-permute-start(bf16[384,1536]{1,0:T(8,128)(2,1)S(1)} %get-tuple-element.70.refs_0_), channel_id=1, source_target_pairs={{0,1},{1,0},{2,3},{3,2},{4,5},{5,4},{6,7},{7,6},{8,9},{9,8},{10,11... | collective-permute-start | bytes 3538952 | tf_op jit(solution)/shard_map/ppermute | solution.py:335
  37.4 9.4 %weight_product.8 = (bf16[768,1024]{1,0:T(8,128)(2,1)}, bf16[768,1024]{1,0:T(8,128)(2,1)}, f32[8,128]{1,0:T(8,128)S(1)}) custom-call(s32[3]{0:T(128)S(1)} %pad_add_fusion.ids_ref, bf16[1536,3072]{1,0:T(8,128)(2,1)S(1)} %bitcast.7, bf16[1536,3072]{1,0:T(8,128)(2,1)S(1)} %bitcast.7, bf16[768,1536]{1,0:T(8,128)(2,1)S(1)} %fusion.15.refs_2_.rest_0_.refs_6_, ...), custom_call_target="tpu_custom_call" | custom-call | flops 241591904 | bytes 471859 | tf_op jit(solution)/shard_map/weight_product/pallas_call | solution.py:136
  47.2 13.9 %input_product.5 = (bf16[384,1536]{1,0:T(8,128)(2,1)S(1)}, bf16[384,1536]{1,0:T(8,128)(2,1)}, f32[8,128]{1,0:T(8,128)S(1)}) custom-call(s32[3]{0:T(128)S(1)} %pad_add_fusion.ids_ref, bf16[3072,3072]{1,0:T(8,128)(2,1)} %refs_9_.1, bf16[768,1536]{1,0:T(8,128)(2,1)S(1)} %fusion.15.refs_2_.rest_0_.refs_6_, bf16[768,1536]{1,0:T(8,128)(2,1)} %fusion.14.refs_2_.rest_1_.refs_4_, ...), custom_call_target="tpu_custom_call" | custom-call | flops 362387872 | bytes 825753 | tf_op jit(solution)/shard_map/input_product/pallas_call | solution.py:196
  61.8 13.0 %weight_product.9 = (bf16[768,1536]{1,0:T(8,128)(2,1)}, bf16[768,1536]{1,0:T(8,128)(2,1)}, f32[8,128]{1,0:T(8,128)S(1)}) custom-call(s32[3]{0:T(128)S(1)} %pad_add_fusion.ids_ref, bf16[1536,3072]{1,0:T(8,128)(2,1)S(1)} %bitcast.7, bf16[1536,3072]{1,0:T(8,128)(2,1)S(1)} %bitcast.7, bf16[768,1536]{1,0:T(8,128)(2,1)S(1)} %fusion.15.refs_2_.rest_0_.refs_6_, ...), custom_call_target="tpu_custom_call" | custom-call | flops 362387872 | bytes 707788 | tf_op jit(solution)/shard_map/weight_product/pallas_call | solution.py:136
  74.8 2.0 collective-permute-start.12
  78.3 8.8 %collective-permute-done.8.refs_1_ = bf16[384,1536]{1,0:T(8,128)(2,1)S(1)} collective-permute-done((bf16[384,1536]{1,0:T(8,128)(2,1)S(1)}, bf16[384,1536]{1,0:T(8,128)(2,1)S(1)}, u32[]{:S(2)}, u32[]{:S(2)}) %collective-permute-start.8) | collective-permute-done | bytes 1179680 | tf_op jit(solution)/shard_map/ppermute | solution.py:335
  88.9 1.7 collective-permute-start.5
  90.6 17.5 %input_product.6 = (bf16[384,1536]{1,0:T(8,128)(2,1)}, bf16[384,1536]{1,0:T(8,128)(2,1)S(1)}, bf16[384,1536]{1,0:T(8,128)(2,1)S(1)}, f32[8,128]{1,0:T(8,128)S(1)}) custom-call(s32[3]{0:T(128)S(1)} %pad_add_fusion.ids_ref, bf16[3072,3072]{1,0:T(8,128)(2,1)} %refs_9_.1, bf16[768,1536]{1,0:T(8,128)(2,1)S(1)} %fusion.15.refs_2_.rest_0_.refs_6_, ...), custom_call_target="tpu_custom_call" | custom-call | flops 543581824 | bytes 1002700 | tf_op jit(solution)/shard_map/input_product/pallas_call | solution.py:196
  109.6 1.7 collective-permute-start.11
  111.3 12.6 %input_product.7 = (bf16[384,1536]{1,0:T(8,128)(2,1)S(1)}, bf16[384,1536]{1,0:T(8,128)(2,1)S(1)}, f32[8,128]{1,0:T(8,128)S(1)}) custom-call(s32[3]{0:T(128)S(1)} %pad_add_fusion.ids_ref, bf16[3072,3072]{1,0:T(8,128)(2,1)} %refs_9_.1, bf16[768,1536]{1,0:T(8,128)(2,1)S(1)} %fusion.15.refs_2_.rest_0_.refs_6_, bf16[768,1536]{1,0:T(8,128)(2,1)} %fusion.14.refs_2_.rest_1_.refs_4_, ...), custom_call_target="tpu_custom_call" | custom-call | flops 362387872 | bytes 825753 | tf_op jit(solution)/shard_map/input_product/pallas_call | solution.py:196
  125.0 1.8 copy-done.4
  126.8 14.1 %weight_product.10 = (bf16[768,1024]{1,0:T(8,128)(2,1)}, bf16[768,512]{1,0:T(8,128)(2,1)}, bf16[768,1024]{1,0:T(8,128)(2,1)}, bf16[768,512]{1,0:T(8,128)(2,1)}, f32[8,128]{1,0:T(8,128)S(1)}) custom-call(s32[3]{0:T(128)S(1)} %pad_add_fusion.ids_ref, bf16[1536,3072]{1,0:T(8,128)(2,1)S(1)} %bitcast.7, bf16[1536,3072]{1,0:T(8,128)(2,1)S(1)} %bitcast.7, ...), custom_call_target="tpu_custom_call" | custom-call | flops 362387872 | bytes 707788 | tf_op jit(solution)/shard_map/weight_product/pallas_call | solution.py:136
  142.2 4.4 %collective-permute-start.10 = (bf16[384,1536]{1,0:T(8,128)(2,1)}, bf16[384,1536]{1,0:T(8,128)(2,1)S(1)}, u32[]{:S(2)}, u32[]{:S(2)}) collective-permute-start(bf16[384,1536]{1,0:T(8,128)(2,1)} %get-tuple-element.89.refs_0_), channel_id=1, source_target_pairs={{0,1},{1,0},{2,3},{3,2},{4,5},{5,4},{6,7},{7,6},{8,9},{9,8},{10,11... | collective-permute-start | bytes 3538952 | tf_op jit(solution)/shard_map/ppermute | solution.py:335
  148.0 1.8 plus.9
  150.5 3.5 %collective-permute-start.9 = (bf16[384,1536]{1,0:T(8,128)(2,1)S(1)}, bf16[384,1536]{1,0:T(8,128)(2,1)S(1)}, u32[]{:S(2)}, u32[]{:S(2)}) collective-permute-start(bf16[384,1536]{1,0:T(8,128)(2,1)S(1)} %get-tuple-element.88), channel_id=1, source_target_pairs={{0,1},{1,0},{2,3},{3,2},{4,5},{5,4},{6,7},{7,6},{8,9},{9,8},{10,11... | collective-permute-start | bytes 3538952 | tf_op jit(solution)/shard_map/ppermute | solution.py:335
  155.5 15.0 %weight_product.11 = (f32[768,1024]{1,0:T(8,128)S(1)}, f32[768,512]{1,0:T(8,128)S(1)}, f32[768,1024]{1,0:T(8,128)S(1)}, f32[768,512]{1,0:T(8,128)S(1)}, f32[8,128]{1,0:T(8,128)S(1)}) custom-call(s32[3]{0:T(128)S(1)} %pad_add_fusion.ids_ref, bf16[1536,3072]{1,0:T(8,128)(2,1)} %refs_1_.11, bf16[1536,3072]{1,0:T(8,128)(2,1)} %refs_1_.11, ...), custom_call_target="tpu_custom_call" | custom-call | flops 362387872 | bytes 707788 | tf_op jit(solution)/shard_map/weight_product/pallas_call | solution.py:136
  173.4 3.1 %plus.10 = (bf16[384,1536]{1,0:T(8,128)(2,1)}, f32[8,128]{1,0:T(8,128)S(1)}) custom-call(bf16[384,1536]{1,0:T(8,128)(2,1)S(1)} %copy-done.22, bf16[384,1536]{1,0:T(8,128)(2,1)} %collective-permute-done.11.refs_1_, f32[8,128]{1,0:T(8,128)S(1)} %get-tuple-element.97.refs_2_), custom_call_target="tpu_custom_call" | custom-call | flops 58982 | bytes 176947 | tf_op jit(solution)/shard_map/plus/pallas_call | solution.py:286
  176.5 2.2 plus.11
  178.8 1.7 collective-permute-start.15
  184.6 14.4 %collective-permute-done.9.rest_1_.refs_1_ = bf16[384,1536]{1,0:T(8,128)(2,1)S(1)} collective-permute-done((bf16[384,1536]{1,0:T(8,128)(2,1)S(1)}, bf16[384,1536]{1,0:T(8,128)(2,1)S(1)}, u32[]{:S(2)}, u32[]{:S(2)}) %collective-permute-start.9) | collective-permute-done | bytes 1179680 | tf_op jit(solution)/shard_map/ppermute | solution.py:335
  203.7 1.9 copy-done.8
  207.0 7.9 %update.4 = (f32[1,768,3072]{2,1,0:T(8,128)}, f32[1,768,3072]{2,1,0:T(8,128)}, f32[1,768,3072]{2,1,0:T(8,128)}, f32[8,128]{1,0:T(8,128)S(1)}) custom-call(f32[768,1024]{1,0:T(8,128)S(1)} %copy-done.8, bf16[768,1024]{1,0:T(8,128)(2,1)S(1)} %copy-done.18, f32[1,768,3072]{2,1,0:T(8,128)} %m.7, f32[1,768,3072]{2,1,0:T(8,128)} %s.7, f32[768,1]{1,0:T(8,128)S(1)} %copy.24.b, ...), custom_call_target="tpu_custom_call" | custom-call | flops 393216 | bytes 1022361 | tf_op jit(solution)/shard_map/update/pallas_call | solution.py:239
  214.9 8.5 %update.5 = (f32[1,768,3072]{2,1,0:T(8,128)}, f32[1,768,3072]{2,1,0:T(8,128)}, f32[1,768,3072]{2,1,0:T(8,128)}, f32[8,128]{1,0:T(8,128)S(1)}) custom-call(f32[768,1024]{1,0:T(8,128)S(1)} %copy-done.12, bf16[768,1024]{1,0:T(8,128)(2,1)} %collective-permute-done.20.arrived, ...), custom_call_target="tpu_custom_call", output_to_operand_aliasing={{0}: (5, {}), {1}: (6, {}), {2}: (7, {})} | custom-call | flops 393216 | bytes 1022361 | tf_op jit(solution)/shard_map/update/pallas_call | solution.py:239
  223.4 5.3 %update.6 = (f32[1,768,3072]{2,1,0:T(8,128)}, f32[1,768,3072]{2,1,0:T(8,128)}, f32[1,768,3072]{2,1,0:T(8,128)}, f32[8,128]{1,0:T(8,128)S(1)}) custom-call(f32[768,512]{1,0:T(8,128)S(1)} %copy-done.16, bf16[768,512]{1,0:T(8,128)(2,1)} %collective-permute-done.19.arrived, ...), custom_call_target="tpu_custom_call", output_to_operand_aliasing={{0}: (5, {}), {1}: (6, {}), {2}: (7, {})} | custom-call | flops 196608 | bytes 511180 | tf_op jit(solution)/shard_map/update/pallas_call | solution.py:239
  228.7 5.0 %update.7 = (f32[1,768,3072]{2,1,0:T(8,128)}, f32[1,768,3072]{2,1,0:T(8,128)}, f32[1,768,3072]{2,1,0:T(8,128)}, f32[8,128]{1,0:T(8,128)S(1)}) custom-call(f32[768,512]{1,0:T(8,128)S(1)} %copy-done.14, bf16[768,512]{1,0:T(8,128)(2,1)S(1)} %collective-permute-done.18.arrived, ...), custom_call_target="tpu_custom_call", output_to_operand_aliasing={{0}: (5, {}), {1}: (6, {}), {2}: (7, {})} | custom-call | flops 196608 | bytes 511180 | tf_op jit(solution)/shard_map/update/pallas_call | solution.py:239
  233.7 4.2 %plus_side_by_side.1 = bf16[384,3072]{1,0:T(8,128)(2,1)} custom-call(bf16[384,1536]{1,0:T(8,128)(2,1)S(1)} %copy-done.26, bf16[384,1536]{1,0:T(8,128)(2,1)S(1)} %copy-done.6, bf16[384,1536]{1,0:T(8,128)(2,1)} %collective-permute-done.15.refs_2_, bf16[384,1536]{1,0:T(8,128)(2,1)S(1)} %copy-done.28, bf16[384,1536]{1,0:T(8,128)(2,1)} %collective-permute-done.16.refs_4_, ...), custom_call_target="tpu_custom_call" | custom-call | flops 176947 | bytes 471859 | tf_op jit(solution)/shard_map/plus_side_by_side/pallas_call | solution.py:312
  (115 shorter events, 28.1 us)
Async XLA Ops:
  5.1 5.6 %collective-permute-start = (bf16[768,1536]{1,0:T(8,128)(2,1)S(1)}, bf16[768,1536]{1,0:T(8,128)(2,1)}, u32[]{:S(2)}, u32[]{:S(2)}) collective-permute-start(bf16[768,1536]{1,0:T(8,128)(2,1)S(1)} %fusion.15.refs_2_.rest_0_.refs_6_), channel_id=1, source_target_pairs={{0,4},{4,0},{1,5},{5,1},{2,6},{6,2},{3,7},{7,3},{8,12},{12,8},{9,1... | collective-permute-start | bytes 7077896 | tf_op jit(solution)/shard_map/ppermute | solution.py:335
  10.6 7.1 %collective-permute-start.1 = (bf16[768,1536]{1,0:T(8,128)(2,1)}, bf16[768,1536]{1,0:T(8,128)(2,1)}, u32[]{:S(2)}, u32[]{:S(2)}) collective-permute-start(bf16[768,1536]{1,0:T(8,128)(2,1)} %fusion.14.refs_2_.rest_1_.refs_4_), channel_id=1, source_target_pairs={{0,4},{4,0},{1,5},{5,1},{2,6},{6,2},{3,7},{7,3},{8,12},{12,8},{9,1... | collective-permute-start | bytes 7077896 | tf_op jit(solution)/shard_map/ppermute | solution.py:335
  31.3 45.5 %collective-permute-start.2 = (bf16[384,1536]{1,0:T(8,128)(2,1)S(1)}, bf16[384,1536]{1,0:T(8,128)(2,1)S(1)}, u32[]{:S(2)}, u32[]{:S(2)}) collective-permute-start(bf16[384,1536]{1,0:T(8,128)(2,1)S(1)} %get-tuple-element.70.refs_0_), channel_id=1, source_target_pairs={{0,1},{1,0},{2,3},{3,2},{4,5},{5,4},{6,7},{7,6},{8,9},{9,8},{10,11... | collective-permute-start | bytes 3538952 | tf_op jit(solution)/shard_map/ppermute | solution.py:335
  34.4 27.3 %collective-permute-start.4 = (bf16[768,512]{1,0:T(8,128)(2,1)S(1)}, bf16[768,512]{1,0:T(8,128)(2,1)S(1)}, u32[]{:S(2)}, u32[]{:S(2)}) collective-permute-start(bf16[768,512]{1,0:T(8,128)(2,1)S(1)} %get-tuple-element.76), channel_id=1, source_target_pairs={{0,16},{8,24},{16,0},{24,8},{1,17},{9,25},{17,1},{25,9},{2,18},{10... | collective-permute-start | bytes 2359304 | tf_op jit(solution)/shard_map/ppermute | solution.py:335
  35.9 38.9 %collective-permute-start.3 = (bf16[768,512]{1,0:T(8,128)(2,1)S(1)}, bf16[768,512]{1,0:T(8,128)(2,1)S(1)}, u32[]{:S(2)}, u32[]{:S(2)}) collective-permute-start(bf16[768,512]{1,0:T(8,128)(2,1)S(1)} %get-tuple-element.75), channel_id=1, source_target_pairs={{0,8},{8,0},{16,24},{24,16},{1,9},{9,1},{17,25},{25,17},{2,10},{10... | collective-permute-start | bytes 2359304 | tf_op jit(solution)/shard_map/ppermute | solution.py:335
  46.7 42.1 %collective-permute-start.6 = (bf16[768,1024]{1,0:T(8,128)(2,1)}, bf16[768,1024]{1,0:T(8,128)(2,1)S(1)}, u32[]{:S(2)}, u32[]{:S(2)}) collective-permute-start(bf16[768,1024]{1,0:T(8,128)(2,1)} %get-tuple-element.81), channel_id=1, source_target_pairs={{0,16},{8,24},{16,0},{24,8},{1,17},{9,25},{17,1},{25,9},{2,18},{10... | collective-permute-start | bytes 4718600 | tf_op jit(solution)/shard_map/ppermute | solution.py:335
  61.1 25.9 %collective-permute-start.8 = (bf16[384,1536]{1,0:T(8,128)(2,1)S(1)}, bf16[384,1536]{1,0:T(8,128)(2,1)S(1)}, u32[]{:S(2)}, u32[]{:S(2)}) collective-permute-start(bf16[384,1536]{1,0:T(8,128)(2,1)S(1)} %get-tuple-element.83.refs_0_), channel_id=1, source_target_pairs={{0,1},{1,0},{2,3},{3,2},{4,5},{5,4},{6,7},{7,6},{8,9},{9,8},{10,11... | collective-permute-start | bytes 3538952 | tf_op jit(solution)/shard_map/ppermute | solution.py:335
  61.6 46.5 %collective-permute-start.7 = (bf16[768,1024]{1,0:T(8,128)(2,1)}, bf16[768,1024]{1,0:T(8,128)(2,1)S(1)}, u32[]{:S(2)}, u32[]{:S(2)}) collective-permute-start(bf16[768,1024]{1,0:T(8,128)(2,1)} %get-tuple-element.82), channel_id=1, source_target_pairs={{0,8},{8,0},{16,24},{24,16},{1,9},{9,1},{17,25},{25,17},{2,10},{10... | collective-permute-start | bytes 4718600 | tf_op jit(solution)/shard_map/ppermute | solution.py:335
  61.8 26.8 %copy-start.20 = (bf16[384,1536]{1,0:T(8,128)(2,1)S(1)}, bf16[384,1536]{1,0:T(8,128)(2,1)}, u32[]{:S(2)}) copy-start(bf16[384,1536]{1,0:T(8,128)(2,1)} %copy-done.19) | copy-start | bytes 3538948
  74.8 33.2 %copy-start.9 = (bf16[768,512]{1,0:T(8,128)(2,1)}, bf16[768,512]{1,0:T(8,128)(2,1)S(1)}, u32[]{:S(2)}) copy-start(bf16[768,512]{1,0:T(8,128)(2,1)S(1)} %collective-permute-done.3.refs_3_.refs_8_) | copy-start | bytes 2359300
  74.8 75.0 %collective-permute-start.12 = (bf16[768,1536]{1,0:T(8,128)(2,1)}, bf16[768,1536]{1,0:T(8,128)(2,1)}, u32[]{:S(2)}, u32[]{:S(2)}) collective-permute-start(bf16[768,1536]{1,0:T(8,128)(2,1)} %get-tuple-element.92), channel_id=1, source_target_pairs={{0,16},{8,24},{16,0},{24,8},{1,17},{9,25},{17,1},{25,9},{2,18},{10... | collective-permute-start | bytes 7077896 | tf_op jit(solution)/shard_map/ppermute | solution.py:335
  76.8 73.8 %collective-permute-start.13 = (bf16[768,1536]{1,0:T(8,128)(2,1)}, bf16[768,1536]{1,0:T(8,128)(2,1)}, u32[]{:S(2)}, u32[]{:S(2)}) collective-permute-start(bf16[768,1536]{1,0:T(8,128)(2,1)} %get-tuple-element.93), channel_id=1, source_target_pairs={{0,8},{8,0},{16,24},{24,16},{1,9},{9,1},{17,25},{25,17},{2,10},{10... | collective-permute-start | bytes 7077896 | tf_op jit(solution)/shard_map/ppermute | solution.py:335
  88.1 52.8 %collective-permute-start.14 = (bf16[384,1536]{1,0:T(8,128)(2,1)}, bf16[384,1536]{1,0:T(8,128)(2,1)}, u32[]{:S(2)}, u32[]{:S(2)}) collective-permute-start(bf16[384,1536]{1,0:T(8,128)(2,1)} %get-tuple-element.94.refs_0_), channel_id=1, source_target_pairs={{0,1},{1,0},{2,3},{3,2},{4,5},{5,4},{6,7},{7,6},{8,9},{9,8},{10,11... | collective-permute-start | bytes 3538952 | tf_op jit(solution)/shard_map/ppermute | solution.py:335
  88.9 19.2 %copy-start.1 = (bf16[768,1024]{1,0:T(8,128)(2,1)}, bf16[768,1024]{1,0:T(8,128)(2,1)S(1)}, u32[]{:S(2)}) copy-start(bf16[768,1024]{1,0:T(8,128)(2,1)S(1)} %collective-permute-done.6.refs_4_.refs_5_) | copy-start | bytes 4718596
  88.9 53.4 %collective-permute-start.5 = (bf16[384,1536]{1,0:T(8,128)(2,1)S(1)}, bf16[384,1536]{1,0:T(8,128)(2,1)}, u32[]{:S(2)}, u32[]{:S(2)}) collective-permute-start(bf16[384,1536]{1,0:T(8,128)(2,1)S(1)} %get-tuple-element.80), channel_id=1, source_target_pairs={{1,2},{2,1},{5,6},{6,5},{9,10},{10,9},{13,14},{14,13},{17,18},{18,... | collective-permute-start | bytes 3538952 | tf_op jit(solution)/shard_map/ppermute | solution.py:367
  90.6 17.6 %copy-start.30 = (bf16[384,1536]{1,0:T(8,128)(2,1)S(1)}, bf16[384,1536]{1,0:T(8,128)(2,1)}, u32[]{:S(2)}) copy-start(bf16[384,1536]{1,0:T(8,128)(2,1)} %copy-done.29) | copy-start | bytes 3538948
  90.6 17.6 %copy-start.32 = (bf16[384,1536]{1,0:T(8,128)(2,1)S(1)}, bf16[384,1536]{1,0:T(8,128)(2,1)}, u32[]{:S(2)}) copy-start(bf16[384,1536]{1,0:T(8,128)(2,1)} %copy-done.31) | copy-start | bytes 3538948
  109.6 44.4 %collective-permute-start.11 = (bf16[384,1536]{1,0:T(8,128)(2,1)}, bf16[384,1536]{1,0:T(8,128)(2,1)}, u32[]{:S(2)}, u32[]{:S(2)}) collective-permute-start(bf16[384,1536]{1,0:T(8,128)(2,1)} %get-tuple-element.91), channel_id=1, source_target_pairs={{1,2},{2,1},{5,6},{6,5},{9,10},{10,9},{13,14},{14,13},{17,18},{18,... | collective-permute-start | bytes 3538952 | tf_op jit(solution)/shard_map/ppermute | solution.py:367
  126.8 19.8 %copy-start.24 = (bf16[384,1536]{1,0:T(8,128)(2,1)S(1)}, bf16[384,1536]{1,0:T(8,128)(2,1)}, u32[]{:S(2)}) copy-start(bf16[384,1536]{1,0:T(8,128)(2,1)} %copy-done.23) | copy-start | bytes 3538948
  140.9 39.5 %collective-permute-start.21 = (bf16[768,1024]{1,0:T(8,128)(2,1)}, bf16[768,1024]{1,0:T(8,128)(2,1)S(1)}, u32[]{:S(2)}, u32[]{:S(2)}) collective-permute-start(bf16[768,1024]{1,0:T(8,128)(2,1)} %get-tuple-element.110), channel_id=1, source_target_pairs={{0,8},{8,0},{16,24},{24,16},{1,9},{9,1},{17,25},{25,17},{2,10},{10... | collective-permute-start | bytes 4718600 | tf_op jit(solution)/shard_map/ppermute | solution.py:335
  142.2 34.3 %collective-permute-start.10 = (bf16[384,1536]{1,0:T(8,128)(2,1)}, bf16[384,1536]{1,0:T(8,128)(2,1)S(1)}, u32[]{:S(2)}, u32[]{:S(2)}) collective-permute-start(bf16[384,1536]{1,0:T(8,128)(2,1)} %get-tuple-element.89.refs_0_), channel_id=1, source_target_pairs={{0,1},{1,0},{2,3},{3,2},{4,5},{5,4},{6,7},{7,6},{8,9},{9,8},{10,11... | collective-permute-start | bytes 3538952 | tf_op jit(solution)/shard_map/ppermute | solution.py:335
  149.8 33.4 %collective-permute-start.17 = (bf16[384,1536]{1,0:T(8,128)(2,1)S(1)}, bf16[384,1536]{1,0:T(8,128)(2,1)S(1)}, u32[]{:S(2)}, u32[]{:S(2)}) collective-permute-start(bf16[384,1536]{1,0:T(8,128)(2,1)S(1)} %get-tuple-element.102), channel_id=1, source_target_pairs={{1,2},{2,1},{5,6},{6,5},{9,10},{10,9},{13,14},{14,13},{17,18},{18,... | collective-permute-start | bytes 3538952 | tf_op jit(solution)/shard_map/ppermute | solution.py:367
  150.5 48.4 %collective-permute-start.9 = (bf16[384,1536]{1,0:T(8,128)(2,1)S(1)}, bf16[384,1536]{1,0:T(8,128)(2,1)S(1)}, u32[]{:S(2)}, u32[]{:S(2)}) collective-permute-start(bf16[384,1536]{1,0:T(8,128)(2,1)S(1)} %get-tuple-element.88), channel_id=1, source_target_pairs={{0,1},{1,0},{2,3},{3,2},{4,5},{5,4},{6,7},{7,6},{8,9},{9,8},{10,11... | collective-permute-start | bytes 3538952 | tf_op jit(solution)/shard_map/ppermute | solution.py:335
  154.0 60.9 %collective-permute-start.20 = (bf16[768,1024]{1,0:T(8,128)(2,1)}, bf16[768,1024]{1,0:T(8,128)(2,1)}, u32[]{:S(2)}, u32[]{:S(2)}) collective-permute-start(bf16[768,1024]{1,0:T(8,128)(2,1)} %get-tuple-element.108), channel_id=1, source_target_pairs={{0,16},{8,24},{16,0},{24,8},{1,17},{9,25},{17,1},{25,9},{2,18},{10... | collective-permute-start | bytes 4718600 | tf_op jit(solution)/shard_map/ppermute | solution.py:335
  155.5 17.9 %copy-start.22 = (bf16[384,1536]{1,0:T(8,128)(2,1)S(1)}, bf16[384,1536]{1,0:T(8,128)(2,1)}, u32[]{:S(2)}) copy-start(bf16[384,1536]{1,0:T(8,128)(2,1)} %copy-done.21) | copy-start | bytes 3538948
  173.4 28.8 %copy-start.7 = (f32[768,1024]{1,0:T(8,128)}, f32[768,1024]{1,0:T(8,128)S(1)}, u32[]{:S(2)}) copy-start(f32[768,1024]{1,0:T(8,128)S(1)} %get-tuple-element.109.old) | copy-start | bytes 9437188
  173.4 28.8 %copy-start.13 = (f32[768,512]{1,0:T(8,128)}, f32[768,512]{1,0:T(8,128)S(1)}, u32[]{:S(2)}) copy-start(f32[768,512]{1,0:T(8,128)S(1)} %get-tuple-element.103.old) | copy-start | bytes 4718596
  173.4 28.8 %copy-start.34 = (s32[1,768]{1,0:T(1,128)S(1)}, s32[1,768]{1,0:T(1,128)}, u32[]{:S(2)}) copy-start(s32[1,768]{1,0:T(1,128)} %param.15) | copy-start | bytes 9220
  178.8 54.9 %collective-permute-start.15 = (bf16[384,1536]{1,0:T(8,128)(2,1)}, bf16[384,1536]{1,0:T(8,128)(2,1)}, u32[]{:S(2)}, u32[]{:S(2)}) collective-permute-start(bf16[384,1536]{1,0:T(8,128)(2,1)} %get-tuple-element.99), channel_id=1, source_target_pairs={{1,2},{2,1},{5,6},{6,5},{9,10},{10,9},{13,14},{14,13},{17,18},{18,... | collective-permute-start | bytes 3538952 | tf_op jit(solution)/shard_map/ppermute | solution.py:367
  181.6 52.1 %collective-permute-start.16 = (bf16[384,1536]{1,0:T(8,128)(2,1)}, bf16[384,1536]{1,0:T(8,128)(2,1)}, u32[]{:S(2)}, u32[]{:S(2)}) collective-permute-start(bf16[384,1536]{1,0:T(8,128)(2,1)} %get-tuple-element.101), channel_id=1, source_target_pairs={{0,1},{1,0},{2,3},{3,2},{4,5},{5,4},{6,7},{7,6},{8,9},{9,8},{10,11... | collective-permute-start | bytes 3538952 | tf_op jit(solution)/shard_map/ppermute | solution.py:335
  183.2 40.2 %collective-permute-start.19 = (bf16[768,512]{1,0:T(8,128)(2,1)}, bf16[768,512]{1,0:T(8,128)(2,1)}, u32[]{:S(2)}, u32[]{:S(2)}) collective-permute-start(bf16[768,512]{1,0:T(8,128)(2,1)} %get-tuple-element.106), channel_id=1, source_target_pairs={{0,8},{8,0},{16,24},{24,16},{1,9},{9,1},{17,25},{25,17},{2,10},{10... | collective-permute-start | bytes 2359304 | tf_op jit(solution)/shard_map/ppermute | solution.py:335
  200.0 28.7 %collective-permute-start.18 = (bf16[768,512]{1,0:T(8,128)(2,1)}, bf16[768,512]{1,0:T(8,128)(2,1)S(1)}, u32[]{:S(2)}, u32[]{:S(2)}) collective-permute-start(bf16[768,512]{1,0:T(8,128)(2,1)} %get-tuple-element.104), channel_id=1, source_target_pairs={{0,16},{8,24},{16,0},{24,8},{1,17},{9,25},{17,1},{25,9},{2,18},{10... | collective-permute-start | bytes 2359304 | tf_op jit(solution)/shard_map/ppermute | solution.py:335
  (28 other events, 197.7 us)

commit v3 on v2

--- a/solution.py
+++ b/solution.py
@@ -12,7 +12,6 @@
 VMEM_LIMIT = 24 * 1024 * 1024
 LANES = 128
 TOKEN = (8, LANES)
-HINT = 20
 
 
 def gelu_slope(values):
@@ -29,8 +28,8 @@
     return lax.dot_general(a, b, (dims, ((), ())), preferred_element_type=jnp.float32)
 
 
-def params():
-    return pltpu.CompilerParams(dimension_semantics=("arbitrary",), vmem_limit_bytes=VMEM_LIMIT)
+def params(limit=VMEM_LIMIT):
+    return pltpu.CompilerParams(dimension_semantics=("arbitrary",), vmem_limit_bytes=limit)
 
 
 def anywhere(arrays):
@@ -46,7 +45,7 @@
 
 
 def cost(flops, bytes_accessed):
-    return pl.CostEstimate(flops=flops // HINT, bytes_accessed=bytes_accessed // HINT, transcendentals=0)
+    return pl.CostEstimate(flops=flops, bytes_accessed=bytes_accessed, transcendentals=0)
 
 
 def held(array):
@@ -221,7 +220,41 @@
     return arrays
 
 
-def update(base, last, mean, square, blend, column, bn, scale, before, order):
+def staged(arrays, pieces, order):
+    share = arrays[0].shape[1]
+
+    def kernel(*refs):
+        sem = refs[-1]
+        outs, token = refs[-2 - len(arrays) * len(pieces) : -2], refs[-2]
+        token[...] = jnp.zeros_like(token)
+        copies = []
+        for k, (start, width) in enumerate(pieces):
+            for g in range(len(arrays)):
+                at = k * len(arrays) + g
+                source = refs[g].at[0, :, pl.ds(start, width)]
+                copies.append(pltpu.make_async_copy(source, outs[at], sem.at[at]))
+        for copy in copies:
+            copy.start()
+        for copy in copies:
+            copy.wait()
+
+    count = len(arrays) * len(pieces)
+    *outs, token = pl.pallas_call(
+        kernel,
+        in_specs=anywhere(arrays) + anywhere(order),
+        out_specs=anywhere(range(count)) + [pl.BlockSpec(memory_space=pltpu.VMEM)],
+        out_shape=[pltpu.VMEM((share, width), jnp.float32) for _, width in pieces for _ in arrays]
+        + [jax.ShapeDtypeStruct(TOKEN, jnp.float32)],
+        scratch_shapes=[pltpu.SemaphoreType.DMA((count,))],
+        compiler_params=pltpu.CompilerParams(vmem_limit_bytes=VMEM_LIMIT // 8),
+        cost_estimate=cost(0, sum(8 * share * width for _, width in pieces) * len(arrays)),
+        name="staged",
+    )(*(held(a) for a in arrays), *order)
+    order[:] = [token]
+    return [outs[k : k + len(arrays)] for k in range(0, count, len(arrays))]
+
+
+def update(base, last, mean, square, whole, blend, column, bn, scale, before, order):
     share, width = base.shape
     rows = block_rows(share, 256)
     across, place = width // bn, column // bn
@@ -231,24 +264,22 @@
         token[...] = jnp.zeros_like(token)
         stepped = old[...] - scale * arrived[...].astype(jnp.float32)
         new_w[0] = stepped
-        new_m[0] = m[0] + b[...] * (stepped - m[0])
-        new_s[0] = s[0] + b[...] * (stepped * stepped - s[0])
+        new_m[0] = m[...] + b[...] * (stepped - m[...])
+        new_s[0] = s[...] + b[...] * (stepped * stepped - s[...])
 
     moment = pl.BlockSpec((1, rows, bn), lambda i: (0, i // across, place + i % across))
     block = pl.BlockSpec((rows, bn), lambda i: (i // across, i % across))
     *outs, token = pl.pallas_call(
         kernel,
         grid=(share // rows * across,),
-        in_specs=[block, block, moment, moment, pl.BlockSpec((rows, 1), lambda i: (i // across, 0))]
-        + anywhere(before)
-        + anywhere(order),
+        in_specs=[block] * 4 + [pl.BlockSpec((rows, 1), lambda i: (i // across, 0))] + anywhere(before) + anywhere(order),
         out_specs=[moment] * 3 + [pl.BlockSpec(TOKEN, lambda i: (0, 0))],
-        out_shape=[jax.ShapeDtypeStruct(mean.shape, jnp.float32)] * 3 + [jax.ShapeDtypeStruct(TOKEN, jnp.float32)],
+        out_shape=[jax.ShapeDtypeStruct(whole, jnp.float32)] * 3 + [jax.ShapeDtypeStruct(TOKEN, jnp.float32)],
         input_output_aliases={5 + k: k for k in range(len(before))},
-        compiler_params=params(),
+        compiler_params=params(VMEM_LIMIT // 2),
         cost_estimate=cost(10 * share * width, share * width * 26),
         name="update",
-    )(base, last, held(mean), held(square), blend, *before, *order)
+    )(base, last, *(pltpu.with_memory_space_constraint(a, pltpu.VMEM) for a in (mean, square)), blend, *before, *order)
     order[:] = [token]
     return outs
 
@@ -273,52 +304,38 @@
     return (input_grad, stepped[None], mean_new[None], square_new[None])
 
 
-def plus(terms, order):
+def plus(terms, order, beside=()):
     rows, width = terms[0].shape
-    some = block_rows(rows, 192)
+    some = block_rows(rows, 96)
+    count = len(terms)
 
     def kernel(*refs):
         out, token = refs[-2:]
         token[...] = jnp.zeros_like(token)
-        out[...] = sum(ref[...].astype(jnp.float32) for ref in refs[: len(terms)]).astype(out.dtype)
-
-    block = pl.BlockSpec((some, width), lambda i: (i, 0))
+        if not beside:
+            out[...] = sum(ref[...].astype(jnp.float32) for ref in refs[:count]).astype(out.dtype)
+        at = 0
+        for ref in refs[count : count + len(beside)]:
+            columns = slice(at, at + ref.shape[1])
+            total = sum(term[:, columns].astype(jnp.float32) for term in refs[:count]) + ref[...].astype(jnp.float32)
+            out[:, columns] = total.astype(out.dtype)
+            at += ref.shape[1]
+
+    def block(array):
+        return pl.BlockSpec((some, array.shape[1]), lambda i: (i, 0))
+
     out, token = pl.pallas_call(
         kernel,
         grid=(rows // some,),
-        in_specs=[block] * len(terms) + anywhere(order),
-        out_specs=[block, pl.BlockSpec(TOKEN, lambda i: (0, 0))],
+        in_specs=[block(a) for a in (*terms, *beside)] + anywhere(order),
+        out_specs=[block(terms[0]), pl.BlockSpec(TOKEN, lambda i: (0, 0))],
         out_shape=[jax.ShapeDtypeStruct((rows, width), jnp.bfloat16), jax.ShapeDtypeStruct(TOKEN, jnp.float32)],
         compiler_params=params(),
-        cost_estimate=cost(rows * width * len(terms), 2 * rows * width * (len(terms) + 1)),
+        cost_estimate=cost(rows * width * (count + 1), 2 * rows * width * (count + 2)),
         name="plus",
-    )(*terms, *order)
+    )(*terms, *beside, *order)
     order[:] = [token]
     return out
-
-
-def plus_side_by_side(groups, order):
-    rows, width = groups[0][0].shape
-    some = block_rows(rows, 96)
-    sizes = [len(group) for group in groups]
-
-    def kernel(*refs):
-        out, at = refs[-1], 0
-        for k, size in enumerate(sizes):
-            total = sum(ref[...].astype(jnp.float32) for ref in refs[at : at + size])
-            out[:, k * width : (k + 1) * width] = total.astype(out.dtype)
-            at += size
-
-    return pl.pallas_call(
-        kernel,
-        grid=(rows // some,),
-        in_specs=[pl.BlockSpec((some, width), lambda i: (i, 0))] * sum(sizes) + anywhere(order),
-        out_specs=pl.BlockSpec((some, width * len(groups)), lambda i: (i, 0)),
-        out_shape=jax.ShapeDtypeStruct((rows, width * len(groups)), jnp.bfloat16),
-        compiler_params=params(),
-        cost_estimate=cost(rows * width * sum(sizes), 2 * rows * width * (sum(sizes) + len(groups))),
-        name="plus_side_by_side",
-    )(*(a for group in groups for a in group), *order)
 
 
 def body(inputs, pre_act, out_grad, weight, swag_mean, swag_square, snapshots, update_flag):
@@ -348,14 +365,13 @@
     small = max(1, blocks // 3)
     large = blocks - small
 
-    def products(*jobs, base=None):
-        return weight_product(inputs, mine, theirs, ids, share, bn, jobs, order, base)
-
-    parts = 2
-    part = width // parts
-
-    def chunks(turns, k):
-        return input_product(weight, mine, theirs, ids, turns, cols, k * part, part, multiplier, order)
+    def products(*jobs, base=None, streamed=False):
+        return weight_product(held(inputs) if streamed else inputs, mine, theirs, ids, share, bn, jobs, order, base)
+
+    part = width // 2
+
+    def chunks(turns, first=0, wide=width):
+        return input_product(weight, mine, theirs, ids, turns, cols, first, wide, multiplier, order)
 
     near, far = (1, 2), (2, 1)
     middle = ((1, 2), (2, 1))
@@ -366,48 +382,43 @@
     def across(value):
         return lax.ppermute(value, "col", middle)
 
-    (pass_a0,) = products((3, 0, 0, [], [small]))
+    (pass_a0,) = products((3, 0, 0, [], [small]), streamed=True)
     got_pass_a0 = swap(pass_a0, "dp", near[0])
-    (pass_b0,) = products((3, 1, 0, [], [small]))
+    (c0_a,) = chunks([0], 0, part)
+    got_0a = outer(c0_a)
+    (pass_b0,) = products((3, 1, 0, [], [small]), streamed=True)
     got_pass_b0 = swap(pass_b0, "dp", near[1])
-    (c0_a,) = chunks([0], 0)
-    got_0a = outer(c0_a)
     pass_a1, pass_b1 = products((3, 0, small, [], [large]), (3, 1, small, [], [large]))
     got_pass_a1, got_pass_b1 = swap(pass_a1, "dp", near[0]), swap(pass_b1, "dp", near[1])
-    c0_b, c1_b = chunks([0, 1], 1)
-    got_0b, got_1b = outer(c0_b), outer(c1_b)
+    order += [got_pass_a0]
+    (c0_b,) = chunks([0], part, part)
+    got_0b = outer(c0_b)
     keep_a, keep_b = products((near[0], 0, 0, [], [blocks]), (near[1], 1, 0, [], [blocks]))
     got_keep_a, got_keep_b = swap(keep_a, "dp", near[0]), swap(keep_b, "dp", near[1])
-    order += [got_pass_a0, got_pass_b0]
+    order += [got_pass_b0]
     got_m1a = across(plus([c0_a, got_0a], order))
-    c1_a, c2_a, c3_a = chunks([1, 2, 3], 0)
-    got_1a = outer(c1_a)
+    (c1,) = chunks([1])
+    got_1 = outer(c1)
     order += [got_pass_a1, got_pass_b1]
     got_m1b = across(plus([c0_b, got_0b], order))
-    c2_b, c3_b = chunks([2, 3], 1)
-    last_b0, last_b1, last_a0, last_a1 = products(
-        (far[1], 1, 0, [(small, got_pass_b0), (large, got_pass_b1)], [large, small]),
-        (far[0], 0, 0, [(small, got_pass_a0), (large, got_pass_a1)], [large, small]),
+    order += [got_m1a]
+    c2, c3 = chunks([2, 3])
+    last_b, last_a = products(
+        (far[1], 1, 0, [(small, got_pass_b0), (large, got_pass_b1)], [blocks]),
+        (far[0], 0, 0, [(small, got_pass_a0), (large, got_pass_a1)], [blocks]),
     )
-    got_last_b = [swap(v, "dp", far[1]) for v in (last_b0, last_b1)]
-    got_last_a = [swap(v, "dp", far[0]) for v in (last_a0, last_a1)]
-    got_2a = outer(plus([c2_a, got_m1a], order))
-    got_m2b = across(plus([c1_b, got_1b], order))
-    *base_b, base_a0, base_a1 = products(
-        (0, 1, 0, [(blocks, got_keep_b)], [large, small]),
-        (0, 0, 0, [(blocks, got_keep_a)], [large, small]),
-        base=(weight, scale),
+    got_last_b, got_last_a = swap(last_b, "dp", far[1]), swap(last_a, "dp", far[0])
+    got_2 = outer(plus([c2], order, beside=[got_m1a, got_m1b]))
+    order += [got_keep_a, got_keep_b]
+    got_m2 = across(plus([c1, got_1], order))
+    base_b, base_a = products(
+        (0, 1, 0, [(blocks, got_keep_b)], [blocks]), (0, 0, 0, [(blocks, got_keep_a)], [blocks]), base=(weight, scale)
     )
-    base_a = [base_a0, base_a1]
-    got_2b = outer(plus([c2_b, got_m1b], order))
-    got_m2a = across(plus([c1_a, got_1a], order))
-    order += [got_2a, got_m2b]
+    (mean_b, square_b), (mean_a, square_a) = staged((swag_mean, swag_square), ((piece, piece), (0, piece)), order)
     outs = ()
-    for k in range(2):
-        for start, base, last in ((piece, base_b, got_last_b), (0, base_a, got_last_a)):
-            column = start + k * large * bn
-            outs = update(base[k], last[k], swag_mean, swag_square, blend, column, bn, scale, outs, order)
-    input_grad = plus_side_by_side([[c3_a, got_2a, got_m2a], [c3_b, got_2b, got_m2b]], order)
+    outs = update(base_b, got_last_b, mean_b, square_b, swag_mean.shape, blend, piece, bn, scale, outs, order)
+    outs = update(base_a, got_last_a, mean_a, square_a, swag_mean.shape, blend, 0, bn, scale, outs, order)
+    input_grad = plus([c3, got_2, got_m2], order)
     return (input_grad, *outs)
 
 

time: 239 us -> 212 us (0.89)
  local copies, waits for them, and re-layouts: 17.4 us -> 7.62 us
  waiting for transfers between devices: 23.2 us -> 13.8 us
  starting transfers between devices: 32.7 us -> 25.7 us
    unnamed x76 -> x42, local copies, waits for them, and re-layouts: 17.2 us -> 7.44 us
    ppermute x18 -> x14, waiting for transfers between devices: 23.2 us -> 13.8 us  [swap(): lax.ppermute(value, axis, [(i, i ^ bit) for i in range(lax.axis_size(axis...]
    ppermute x18 -> x14, starting transfers between devices: 26.9 us -> 21 us  [swap(): lax.ppermute(value, axis, [(i, i ^ bit) for i in range(lax.axis_size(axis...]
    ppermute x4 -> x3, starting transfers between devices: 5.79 us -> 4.72 us  [across(): return lax.ppermute(value, 'col', middle)]
    pallas_call x11 -> x8, Pallas kernels: 41.1 us -> 40.3 us  [the longest x5 16.9 us: plus(): pl.pallas_call(kernel, grid=(rows // some,), in_specs=[block(a) for a in...]
  transfers between devices with their start and end apart: 22 -> 17, of which waited for: 2 -> 1; matrix products, arithmetic and copies ran while one was open for 2% -> 2% of each run, Pallas kernels for 57% -> 70%
where the time goes in v3:
time: 212 us; the launch traced here: 210 us
  Pallas kernels  152 us (72%)
  starting transfers between devices  25.7 us (12%)
  waiting for transfers between devices  13.8 us (7%)
  other arithmetic  9.48 us (4%)
  local copies, waits for them, and re-layouts  7.62 us (4%)
    pallas_call x6, Pallas kernels, weight_product(): pl.pallas_call(kernel, grid_spec=pltpu.PrefetchScalarGridSpec(num_scalar_...  58 us
    pallas_call x4, Pallas kernels, input_product(): pl.pallas_call(kernel, grid_spec=pltpu.PrefetchScalarGridSpec(num_scalar_...  54 us
    ppermute x14, starting transfers between devices, swap(): lax.ppermute(value, axis, [(i, i ^ bit) for i in range(lax.axis_size(axis...  21 us
    pallas_call x5, Pallas kernels, plus(): pl.pallas_call(kernel, grid=(rows // some,), in_specs=[block(a) for a in...  16.9 us
    pallas_call x2, Pallas kernels, update(): pl.pallas_call(kernel, grid=(share // rows * across,), in_specs=[block] *...  16.9 us
    ppermute x14, waiting for transfers between devices, swap(): lax.ppermute(value, axis, [(i, i ^ bit) for i in range(lax.axis_size(axis...  13.8 us
    convert_element_type x2, other arithmetic, times_slope(): (out_grad.astype(jnp.float32) * gelu_slope(pre_act.astype(jnp.float32)))....  9.4 us
    unnamed x42, local copies, waits for them, and re-layouts  7.44 us
  transfers between devices with their start and end apart: 17, of which 1 were waited for; matrix products, arithmetic and copies ran while one was open for 2% of the time, Pallas kernels for 70%

profile of v3, /device:TPU:0, one launch (start us, length us, event | category | flops | bytes accessed | tf_op | source)
XLA Modules:
  0.0 210.5 jit_solution(16724202245067766925)
XLA Ops:
  0.6 4.5 %fusion.15.refs_2_.rest_0_.refs_6_ = bf16[768,1536]{1,0:T(8,128)(2,1)S(1)} fusion(bf16[768,3072]{1,0:T(8,128)(2,1)} %param.9, bf16[768,3072]{1,0:T(8,128)(2,1)} %param.10), kind=kLoop, calls=%fused_computation.23 | loop fusion | flops 14155776 | bytes 7077888 | tf_op jit(solution)/shard_map/convert_element_type | solution.py:24
  5.7 4.9 %fusion.14.rest_1_.refs_2_.refs_4_ = bf16[768,1536]{1,0:T(8,128)(2,1)} fusion(bf16[768,3072]{1,0:T(8,128)(2,1)S(1)} %copy-done.16, bf16[768,3072]{1,0:T(8,128)(2,1)} %param.10), kind=kLoop, calls=%fused_computation.22 | loop fusion | flops 14155776 | bytes 7077888 | tf_op jit(solution)/shard_map/convert_element_type | solution.py:24
  10.7 3.8 %weight_product.6 = (bf16[768,512]{1,0:T(8,128)(2,1)S(1)}, f32[8,128]{1,0:T(8,128)S(1)}) custom-call(s32[3]{0:T(128)S(1)} %pad_add_fusion.ids_ref, bf16[1536,3072]{1,0:T(8,128)(2,1)} %refs_1_.12, bf16[1536,3072]{1,0:T(8,128)(2,1)} %refs_1_.12, bf16[768,1536]{1,0:T(8,128)(2,1)S(1)} %fusion.15.refs_2_.rest_0_.refs_6_, ...), custom_call_target="tpu_custom_call" | custom-call | flops 1207959552 | bytes 2359296 | tf_op jit(solution)/shard_map/weight_product/pallas_call | solution.py:135
  14.5 3.0 %collective-permute-start.2 = (bf16[768,512]{1,0:T(8,128)(2,1)S(1)}, bf16[768,512]{1,0:T(8,128)(2,1)S(1)}, u32[]{:S(2)}, u32[]{:S(2)}) collective-permute-start(bf16[768,512]{1,0:T(8,128)(2,1)S(1)} %get-tuple-element.59), channel_id=1, source_target_pairs={{0,8},{8,0},{16,24},{24,16},{1,9},{9,1},{17,25},{25,17},{2,10},{10... | collective-permute-start | bytes 2359304 | tf_op jit(solution)/shard_map/ppermute | solution.py:352
  17.5 9.1 %input_product.4 = (bf16[384,1536]{1,0:T(8,128)(2,1)S(1)}, f32[8,128]{1,0:T(8,128)S(1)}) custom-call(s32[3]{0:T(128)S(1)} %pad_add_fusion.ids_ref, bf16[3072,3072]{1,0:T(8,128)(2,1)} %refs_9_.1, bf16[768,1536]{1,0:T(8,128)(2,1)S(1)} %fusion.15.refs_2_.rest_0_.refs_6_, bf16[768,1536]{1,0:T(8,128)(2,1)} %fusion.14.rest_1_.refs_2_.refs_4_, ...), custom_call_target="tpu_custom_call" | custom-call | flops 3623878656 | bytes 12976128 | tf_op jit(solution)/shard_map/input_product/pallas_call | solution.py:195
  26.7 4.3 %weight_product.7 = (bf16[768,512]{1,0:T(8,128)(2,1)S(1)}, f32[8,128]{1,0:T(8,128)S(1)}) custom-call(s32[3]{0:T(128)S(1)} %pad_add_fusion.ids_ref, bf16[1536,3072]{1,0:T(8,128)(2,1)} %refs_1_.12, bf16[1536,3072]{1,0:T(8,128)(2,1)} %refs_1_.12, bf16[768,1536]{1,0:T(8,128)(2,1)} %fusion.14.rest_1_.refs_2_.refs_4_, ...), custom_call_target="tpu_custom_call" | custom-call | flops 1207959552 | bytes 2359296 | tf_op jit(solution)/shard_map/weight_product/pallas_call | solution.py:135
  31.0 1.6 collective-permute-start.5
  32.6 1.6 collective-permute-start.4
  34.2 9.4 %weight_product.8 = (bf16[768,1024]{1,0:T(8,128)(2,1)}, bf16[768,1024]{1,0:T(8,128)(2,1)}, f32[8,128]{1,0:T(8,128)S(1)}) custom-call(s32[3]{0:T(128)S(1)} %pad_add_fusion.ids_ref, bf16[1536,3072]{1,0:T(8,128)(2,1)S(1)} %bitcast.7, bf16[1536,3072]{1,0:T(8,128)(2,1)S(1)} %bitcast.7, bf16[768,1536]{1,0:T(8,128)(2,1)S(1)} %fusion.15.refs_2_.rest_0_.refs_6_, ...), custom_call_target="tpu_custom_call" | custom-call | flops 4831838208 | bytes 9437184 | tf_op jit(solution)/shard_map/weight_product/pallas_call | solution.py:135
  44.6 9.1 %input_product.5 = (bf16[384,1536]{1,0:T(8,128)(2,1)S(1)}, f32[8,128]{1,0:T(8,128)S(1)}) custom-call(s32[3]{0:T(128)S(1)} %pad_add_fusion.ids_ref, bf16[3072,3072]{1,0:T(8,128)(2,1)} %refs_9_.1, bf16[768,1536]{1,0:T(8,128)(2,1)S(1)} %fusion.15.refs_2_.rest_0_.refs_6_, bf16[768,1536]{1,0:T(8,128)(2,1)} %fusion.14.rest_1_.refs_2_.refs_4_, ...), custom_call_target="tpu_custom_call" | custom-call | flops 3623878656 | bytes 12976128 | tf_op jit(solution)/shard_map/input_product/pallas_call | solution.py:195
  54.3 12.8 %weight_product.9 = (bf16[768,1536]{1,0:T(8,128)(2,1)}, bf16[768,1536]{1,0:T(8,128)(2,1)}, f32[8,128]{1,0:T(8,128)S(1)}) custom-call(s32[3]{0:T(128)S(1)} %pad_add_fusion.ids_ref, bf16[1536,3072]{1,0:T(8,128)(2,1)S(1)} %bitcast.7, bf16[1536,3072]{1,0:T(8,128)(2,1)S(1)} %bitcast.7, bf16[768,1536]{1,0:T(8,128)(2,1)S(1)} %fusion.15.refs_2_.rest_0_.refs_6_, ...), custom_call_target="tpu_custom_call" | custom-call | flops 7247757312 | bytes 14155776 | tf_op jit(solution)/shard_map/weight_product/pallas_call | solution.py:135
  70.7 1.5 collective-permute-start.12
  72.2 15.1 %input_product.6 = (bf16[384,3072]{1,0:T(8,128)(2,1)}, f32[8,128]{1,0:T(8,128)S(1)}) custom-call(s32[3]{0:T(128)S(1)} %pad_add_fusion.ids_ref, bf16[3072,3072]{1,0:T(8,128)(2,1)} %refs_9_.1, bf16[768,1536]{1,0:T(8,128)(2,1)S(1)} %fusion.15.refs_2_.rest_0_.refs_6_, bf16[768,1536]{1,0:T(8,128)(2,1)} %fusion.14.rest_1_.refs_2_.refs_4_, ...), custom_call_target="tpu_custom_call" | custom-call | flops 7247757312 | bytes 23592960 | tf_op jit(solution)/shard_map/input_product/pallas_call | solution.py:195
  87.4 1.6 collective-permute-start.13
  89.0 3.8 %collective-permute-start.11 = (bf16[384,3072]{1,0:T(8,128)(2,1)}, bf16[384,3072]{1,0:T(8,128)(2,1)}, u32[]{:S(2)}, u32[]{:S(2)}) collective-permute-start(bf16[384,3072]{1,0:T(8,128)(2,1)} %get-tuple-element.77.refs_0_), channel_id=1, source_target_pairs={{0,1},{1,0},{2,3},{3,2},{4,5},{5,4},{6,7},{7,6},{8,9},{9,8},{10,11... | collective-permute-start | bytes 7077896 | tf_op jit(solution)/shard_map/ppermute | solution.py:352
  92.7 3.6 %plus.6 = (bf16[384,1536]{1,0:T(8,128)(2,1)}, f32[8,128]{1,0:T(8,128)S(1)}) custom-call(bf16[384,1536]{1,0:T(8,128)(2,1)S(1)} %copy-done.15, bf16[384,1536]{1,0:T(8,128)(2,1)} %collective-permute-done.3.refs_1_, f32[8,128]{1,0:T(8,128)S(1)} %get-tuple-element.66.refs_2_, bf16[768,1024]{1,0:T(8,128)(2,1)S(1)} %collective-permute-done.6.refs_3_.refs_9_, ...), custom_call_target="tpu_custom_call" | custom-call | flops 1769472 | bytes 4718592 | tf_op jit(solution)/shard_map/plus/pallas_call | solution.py:327
  96.3 1.8 collective-permute-start.9
  98.1 20.7 %input_product.7 = (bf16[384,3072]{1,0:T(8,128)(2,1)S(1)}, bf16[384,3072]{1,0:T(8,128)(2,1)S(1)}, f32[8,128]{1,0:T(8,128)S(1)}) custom-call(s32[3]{0:T(128)S(1)} %pad_add_fusion.ids_ref, bf16[3072,3072]{1,0:T(8,128)(2,1)} %refs_9_.1, bf16[768,1536]{1,0:T(8,128)(2,1)S(1)} %fusion.15.refs_2_.rest_0_.refs_6_, bf16[768,1536]{1,0:T(8,128)(2,1)} %fusion.14.rest_1_.refs_2_.refs_4_, ...), custom_call_target="tpu_custom_call" | custom-call | flops 14495514624 | bytes 28311552 | tf_op jit(solution)/shard_map/input_product/pallas_call | solution.py:195
  118.8 1.4 copy-done.8
  120.2 2.3 %copy-done.1 = bf16[768,1024]{1,0:T(8,128)(2,1)S(1)} copy-done((bf16[768,1024]{1,0:T(8,128)(2,1)S(1)}, bf16[768,1024]{1,0:T(8,128)(2,1)}, u32[]{:S(2)}) %copy-start.1) | copy-done | bytes 1572888
  122.5 1.4 copy-done.3
  123.9 13.4 %weight_product.10 = (bf16[768,1536]{1,0:T(8,128)(2,1)}, bf16[768,1536]{1,0:T(8,128)(2,1)}, f32[8,128]{1,0:T(8,128)S(1)}) custom-call(s32[3]{0:T(128)S(1)} %pad_add_fusion.ids_ref, bf16[1536,3072]{1,0:T(8,128)(2,1)S(1)} %bitcast.7, bf16[1536,3072]{1,0:T(8,128)(2,1)S(1)} %bitcast.7, bf16[768,1536]{1,0:T(8,128)(2,1)} %fusion.14.rest_1_.refs_2_.refs_4_, ...), custom_call_target="tpu_custom_call" | custom-call | flops 7247757312 | bytes 14155776 | tf_op jit(solution)/shard_map/weight_product/pallas_call | solution.py:135
  138.4 3.9 %plus.7 = (bf16[384,3072]{1,0:T(8,128)(2,1)}, f32[8,128]{1,0:T(8,128)S(1)}) custom-call(bf16[384,3072]{1,0:T(8,128)(2,1)S(1)} %copy-done.9, bf16[384,1536]{1,0:T(8,128)(2,1)S(1)} %copy-done.13, bf16[384,1536]{1,0:T(8,128)(2,1)} %collective-permute-done.9.refs_2_, f32[8,128]{1,0:T(8,128)S(1)} %get-tuple-element.75.refs_3_), custom_call_target="tpu_custom_call" | custom-call | flops 2359296 | bytes 7077888 | tf_op jit(solution)/shard_map/plus/pallas_call | solution.py:327
  142.2 4.7 %collective-permute-start.10 = (bf16[384,3072]{1,0:T(8,128)(2,1)}, bf16[384,3072]{1,0:T(8,128)(2,1)}, u32[]{:S(2)}, u32[]{:S(2)}) collective-permute-start(bf16[384,3072]{1,0:T(8,128)(2,1)} %get-tuple-element.76), channel_id=1, source_target_pairs={{0,1},{1,0},{2,3},{3,2},{4,5},{5,4},{6,7},{7,6},{8,9},{9,8},{10,11... | collective-permute-start | bytes 7077896 | tf_op jit(solution)/shard_map/ppermute | solution.py:352
  146.9 4.5 %plus.8 = (bf16[384,3072]{1,0:T(8,128)(2,1)}, f32[8,128]{1,0:T(8,128)S(1)}) custom-call(bf16[384,3072]{1,0:T(8,128)(2,1)} %get-tuple-element.77.refs_0_, bf16[384,3072]{1,0:T(8,128)(2,1)} %collective-permute-done.11.refs_1_, f32[8,128]{1,0:T(8,128)S(1)} %get-tuple-element.78.refs_2_, bf16[768,1536]{1,0:T(8,128)(2,1)} %collective-permute-done.12.refs_3_.refs_8_, ...), custom_call_target="tpu_custom_call" | custom-call | flops 3538944 | bytes 9437184 | tf_op jit(solution)/shard_map/plus/pallas_call | solution.py:327
  151.4 2.1 collective-permute-start.14
  154.4 14.3 %weight_product.11 = (f32[768,1536]{1,0:T(8,128)S(1)}, f32[768,1536]{1,0:T(8,128)S(1)}, f32[8,128]{1,0:T(8,128)S(1)}) custom-call(s32[3]{0:T(128)S(1)} %pad_add_fusion.ids_ref, bf16[1536,3072]{1,0:T(8,128)(2,1)} %refs_1_.12, bf16[1536,3072]{1,0:T(8,128)(2,1)} %refs_1_.12, bf16[768,1536]{1,0:T(8,128)(2,1)} %fusion.14.rest_1_.refs_2_.refs_4_, ...), custom_call_target="tpu_custom_call" | custom-call | flops 7247757312 | bytes 14155776 | tf_op jit(solution)/shard_map/weight_product/pallas_call | solution.py:135
  168.6 6.5 %staged.1 = (f32[768,1536]{1,0:T(8,128)S(1)}, f32[768,1536]{1,0:T(8,128)S(1)}, f32[768,1536]{1,0:T(8,128)S(1)}, f32[768,1536]{1,0:T(8,128)S(1)}, f32[8,128]{1,0:T(8,128)S(1)}) custom-call(f32[1,768,3072]{2,1,0:T(8,128)} %refs_0_.13, f32[1,768,3072]{2,1,0:T(8,128)} %refs_1_.13, f32[8,128]{1,0:T(8,128)S(1)} %get-tuple-element.85.refs_2_), custom_call_target="tpu_custom_call" | custom-call | bytes 37748736 | tf_op jit(solution)/shard_map/staged/pallas_call | solution.py:242
  175.1 13.7 %collective-permute-done.16.arrived = bf16[768,1536]{1,0:T(8,128)(2,1)} collective-permute-done((bf16[768,1536]{1,0:T(8,128)(2,1)}, bf16[768,1536]{1,0:T(8,128)(2,1)}, u32[]{:S(2)}, u32[]{:S(2)}) %collective-permute-start.16) | collective-permute-done | bytes 2359328 | tf_op jit(solution)/shard_map/ppermute | solution.py:352
  188.9 8.3 %update.2 = (f32[1,768,3072]{2,1,0:T(8,128)}, f32[1,768,3072]{2,1,0:T(8,128)}, f32[1,768,3072]{2,1,0:T(8,128)}, f32[8,128]{1,0:T(8,128)S(1)}) custom-call(f32[768,1536]{1,0:T(8,128)S(1)} %get-tuple-element.88.old, bf16[768,1536]{1,0:T(8,128)(2,1)} %collective-permute-done.16.arrived, f32[768,1536]{1,0:T(8,128)S(1)} %get-tuple-element.90.m, ...), custom_call_target="tpu_custom_call" | custom-call | flops 11796480 | bytes 30670848 | tf_op jit(solution)/shard_map/update/pallas_call | solution.py:272
  197.2 8.6 %update.3 = (f32[1,768,3072]{2,1,0:T(8,128)}, f32[1,768,3072]{2,1,0:T(8,128)}, f32[1,768,3072]{2,1,0:T(8,128)}, f32[8,128]{1,0:T(8,128)S(1)}) custom-call(f32[768,1536]{1,0:T(8,128)S(1)} %get-tuple-element.83.old, bf16[768,1536]{1,0:T(8,128)(2,1)} %collective-permute-done.15.arrived, ...), custom_call_target="tpu_custom_call", output_to_operand_aliasing={{0}: (5, {}), {1}: (6, {}), {2}: (7, {})} | custom-call | flops 11796480 | bytes 30670848 | tf_op jit(solution)/shard_map/update/pallas_call | solution.py:272
  205.8 4.6 %plus.9 = (bf16[384,3072]{1,0:T(8,128)(2,1)}, f32[8,128]{1,0:T(8,128)}) custom-call(bf16[384,3072]{1,0:T(8,128)(2,1)S(1)} %copy-done.7, bf16[384,3072]{1,0:T(8,128)(2,1)} %collective-permute-done.10.refs_1_, bf16[384,3072]{1,0:T(8,128)(2,1)} %collective-permute-done.14.refs_2_, f32[8,128]{1,0:T(8,128)S(1)} %get-tuple-element.97.refs_3_), custom_call_target="tpu_custom_call" | custom-call | flops 4718592 | bytes 11796480 | tf_op jit(solution)/shard_map/plus/pallas_call | solution.py:327
  (68 shorter events, 7.1 us)
Async XLA Ops:
  5.1 5.6 %collective-permute-start = (bf16[768,1536]{1,0:T(8,128)(2,1)S(1)}, bf16[768,1536]{1,0:T(8,128)(2,1)}, u32[]{:S(2)}, u32[]{:S(2)}) collective-permute-start(bf16[768,1536]{1,0:T(8,128)(2,1)S(1)} %fusion.15.refs_2_.rest_0_.refs_6_), channel_id=1, source_target_pairs={{0,4},{4,0},{1,5},{5,1},{2,6},{6,2},{3,7},{7,3},{8,12},{12,8},{9,1... | collective-permute-start | bytes 7077896 | tf_op jit(solution)/shard_map/ppermute | solution.py:352
  10.6 7.0 %collective-permute-start.1 = (bf16[768,1536]{1,0:T(8,128)(2,1)}, bf16[768,1536]{1,0:T(8,128)(2,1)}, u32[]{:S(2)}, u32[]{:S(2)}) collective-permute-start(bf16[768,1536]{1,0:T(8,128)(2,1)} %fusion.14.rest_1_.refs_2_.refs_4_), channel_id=1, source_target_pairs={{0,4},{4,0},{1,5},{5,1},{2,6},{6,2},{3,7},{7,3},{8,12},{12,8},{9,1... | collective-permute-start | bytes 7077896 | tf_op jit(solution)/shard_map/ppermute | solution.py:352
  14.5 30.1 %collective-permute-start.2 = (bf16[768,512]{1,0:T(8,128)(2,1)S(1)}, bf16[768,512]{1,0:T(8,128)(2,1)S(1)}, u32[]{:S(2)}, u32[]{:S(2)}) collective-permute-start(bf16[768,512]{1,0:T(8,128)(2,1)S(1)} %get-tuple-element.59), channel_id=1, source_target_pairs={{0,8},{8,0},{16,24},{24,16},{1,9},{9,1},{17,25},{25,17},{2,10},{10... | collective-permute-start | bytes 2359304 | tf_op jit(solution)/shard_map/ppermute | solution.py:352
  26.6 7.5 %slice-start = ((s8[9437184]{0:T(1024)(128)(4,1)}), s8[4194304]{0:T(1024)(128)(4,1)S(1)}, s32[]{:S(2)}) async-start(s8[9437184]{0:T(1024)(128)(4,1)} %bitcast.6), calls=%async_computation | async-start | bytes 8388608
  26.6 7.5 %slice-start.1 = ((s8[9437184]{0:T(1024)(128)(4,1)}), s8[4194304]{0:T(1024)(128)(4,1)S(1)}, s32[]{:S(2)}) async-start(s8[9437184]{0:T(1024)(128)(4,1)} %bitcast.6), calls=%async_computation.1 | async-start | bytes 8388608
  26.6 7.5 %slice-start.2 = ((s8[9437184]{0:T(1024)(128)(4,1)}), s8[1048576]{0:T(1024)(128)(4,1)S(1)}, s32[]{:S(2)}) async-start(s8[9437184]{0:T(1024)(128)(4,1)} %bitcast.6), calls=%async_computation.2 | async-start | bytes 2097152
  31.0 36.1 %collective-permute-start.5 = (bf16[768,512]{1,0:T(8,128)(2,1)S(1)}, bf16[768,512]{1,0:T(8,128)(2,1)S(1)}, u32[]{:S(2)}, u32[]{:S(2)}) collective-permute-start(bf16[768,512]{1,0:T(8,128)(2,1)S(1)} %get-tuple-element.64), channel_id=1, source_target_pairs={{0,16},{8,24},{16,0},{24,8},{1,17},{9,25},{17,1},{25,9},{2,18},{10... | collective-permute-start | bytes 2359304 | tf_op jit(solution)/shard_map/ppermute | solution.py:352
  32.6 34.5 %collective-permute-start.4 = (bf16[384,1536]{1,0:T(8,128)(2,1)S(1)}, bf16[384,1536]{1,0:T(8,128)(2,1)S(1)}, u32[]{:S(2)}, u32[]{:S(2)}) collective-permute-start(bf16[384,1536]{1,0:T(8,128)(2,1)S(1)} %get-tuple-element.61.refs_0_), channel_id=1, source_target_pairs={{0,1},{1,0},{2,3},{3,2},{4,5},{5,4},{6,7},{7,6},{8,9},{9,8},{10,11... | collective-permute-start | bytes 3538952 | tf_op jit(solution)/shard_map/ppermute | solution.py:352
  43.6 43.7 %collective-permute-start.6 = (bf16[768,1024]{1,0:T(8,128)(2,1)}, bf16[768,1024]{1,0:T(8,128)(2,1)S(1)}, u32[]{:S(2)}, u32[]{:S(2)}) collective-permute-start(bf16[768,1024]{1,0:T(8,128)(2,1)} %get-tuple-element.67), channel_id=1, source_target_pairs={{0,8},{8,0},{16,24},{24,16},{1,9},{9,1},{17,25},{25,17},{2,10},{10... | collective-permute-start | bytes 4718600 | tf_op jit(solution)/shard_map/ppermute | solution.py:352
  44.1 44.8 %collective-permute-start.7 = (bf16[768,1024]{1,0:T(8,128)(2,1)}, bf16[768,1024]{1,0:T(8,128)(2,1)S(1)}, u32[]{:S(2)}, u32[]{:S(2)}) collective-permute-start(bf16[768,1024]{1,0:T(8,128)(2,1)} %get-tuple-element.68), channel_id=1, source_target_pairs={{0,16},{8,24},{16,0},{24,8},{1,17},{9,25},{17,1},{25,9},{2,18},{10... | collective-permute-start | bytes 4718600 | tf_op jit(solution)/shard_map/ppermute | solution.py:352
  44.6 9.1 %copy-start.4 = (bf16[768,512]{1,0:T(8,128)(2,1)}, bf16[768,512]{1,0:T(8,128)(2,1)S(1)}, u32[]{:S(2)}) copy-start(bf16[768,512]{1,0:T(8,128)(2,1)S(1)} %collective-permute-done.2.rest_5_.refs_8_) | copy-start | bytes 2359300
  53.7 13.4 %copy-start.14 = (bf16[384,1536]{1,0:T(8,128)(2,1)}, bf16[384,1536]{1,0:T(8,128)(2,1)S(1)}, u32[]{:S(2)}) copy-start(bf16[384,1536]{1,0:T(8,128)(2,1)S(1)} %get-tuple-element.60.refs_0_) | copy-start | bytes 3538948
  53.8 39.0 %collective-permute-start.3 = (bf16[384,1536]{1,0:T(8,128)(2,1)S(1)}, bf16[384,1536]{1,0:T(8,128)(2,1)}, u32[]{:S(2)}, u32[]{:S(2)}) collective-permute-start(bf16[384,1536]{1,0:T(8,128)(2,1)S(1)} %get-tuple-element.60.refs_0_), channel_id=1, source_target_pairs={{0,1},{1,0},{2,3},{3,2},{4,5},{5,4},{6,7},{7,6},{8,9},{9,8},{10,11... | collective-permute-start | bytes 3538952 | tf_op jit(solution)/shard_map/ppermute | solution.py:352
  69.8 28.3 %collective-permute-start.8 = (bf16[384,1536]{1,0:T(8,128)(2,1)S(1)}, bf16[384,1536]{1,0:T(8,128)(2,1)S(1)}, u32[]{:S(2)}, u32[]{:S(2)}) collective-permute-start(bf16[384,1536]{1,0:T(8,128)(2,1)S(1)} %get-tuple-element.70), channel_id=1, source_target_pairs={{1,2},{2,1},{5,6},{6,5},{9,10},{10,9},{13,14},{14,13},{17,18},{18,... | collective-permute-start | bytes 3538952 | tf_op jit(solution)/shard_map/ppermute | solution.py:383
  70.7 71.5 %collective-permute-start.12 = (bf16[768,1536]{1,0:T(8,128)(2,1)}, bf16[768,1536]{1,0:T(8,128)(2,1)}, u32[]{:S(2)}, u32[]{:S(2)}) collective-permute-start(bf16[768,1536]{1,0:T(8,128)(2,1)} %get-tuple-element.79), channel_id=1, source_target_pairs={{0,8},{8,0},{16,24},{24,16},{1,9},{9,1},{17,25},{25,17},{2,10},{10... | collective-permute-start | bytes 7077896 | tf_op jit(solution)/shard_map/ppermute | solution.py:352
  72.2 20.5 %copy-start.15 = (bf16[384,1536]{1,0:T(8,128)(2,1)S(1)}, bf16[384,1536]{1,0:T(8,128)(2,1)}, u32[]{:S(2)}) copy-start(bf16[384,1536]{1,0:T(8,128)(2,1)} %copy-done.14) | copy-start | bytes 3538948
  87.3 31.4 %copy-start = (bf16[768,1024]{1,0:T(8,128)(2,1)}, bf16[768,1024]{1,0:T(8,128)(2,1)S(1)}, u32[]{:S(2)}) copy-start(bf16[768,1024]{1,0:T(8,128)(2,1)S(1)} %collective-permute-done.6.refs_3_.refs_9_) | copy-start | bytes 4718596
  87.4 59.6 %collective-permute-start.13 = (bf16[768,1536]{1,0:T(8,128)(2,1)}, bf16[768,1536]{1,0:T(8,128)(2,1)}, u32[]{:S(2)}, u32[]{:S(2)}) collective-permute-start(bf16[768,1536]{1,0:T(8,128)(2,1)} %get-tuple-element.80), channel_id=1, source_target_pairs={{0,16},{8,24},{16,0},{24,8},{1,17},{9,25},{17,1},{25,9},{2,18},{10... | collective-permute-start | bytes 7077896 | tf_op jit(solution)/shard_map/ppermute | solution.py:352
  89.0 29.8 %copy-start.2 = (bf16[768,1024]{1,0:T(8,128)(2,1)}, bf16[768,1024]{1,0:T(8,128)(2,1)S(1)}, u32[]{:S(2)}) copy-start(bf16[768,1024]{1,0:T(8,128)(2,1)S(1)} %collective-permute-done.7.refs_4_.refs_5_) | copy-start | bytes 4718596
  89.0 58.0 %collective-permute-start.11 = (bf16[384,3072]{1,0:T(8,128)(2,1)}, bf16[384,3072]{1,0:T(8,128)(2,1)}, u32[]{:S(2)}, u32[]{:S(2)}) collective-permute-start(bf16[384,3072]{1,0:T(8,128)(2,1)} %get-tuple-element.77.refs_0_), channel_id=1, source_target_pairs={{0,1},{1,0},{2,3},{3,2},{4,5},{5,4},{6,7},{7,6},{8,9},{9,8},{10,11... | collective-permute-start | bytes 7077896 | tf_op jit(solution)/shard_map/ppermute | solution.py:352
  96.3 41.6 %collective-permute-start.9 = (bf16[384,1536]{1,0:T(8,128)(2,1)}, bf16[384,1536]{1,0:T(8,128)(2,1)}, u32[]{:S(2)}, u32[]{:S(2)}) collective-permute-start(bf16[384,1536]{1,0:T(8,128)(2,1)} %get-tuple-element.73), channel_id=1, source_target_pairs={{1,2},{2,1},{5,6},{6,5},{9,10},{10,9},{13,14},{14,13},{17,18},{18,... | collective-permute-start | bytes 3538952 | tf_op jit(solution)/shard_map/ppermute | solution.py:383
  98.0 20.7 %copy-start.12 = (bf16[384,1536]{1,0:T(8,128)(2,1)}, bf16[384,1536]{1,0:T(8,128)(2,1)S(1)}, u32[]{:S(2)}) copy-start(bf16[384,1536]{1,0:T(8,128)(2,1)S(1)} %collective-permute-done.8.rest_5_.refs_1_) | copy-start | bytes 3538948
  98.1 22.2 %copy-start.5 = (bf16[768,512]{1,0:T(8,128)(2,1)S(1)}, bf16[768,512]{1,0:T(8,128)(2,1)}, u32[]{:S(2)}) copy-start(bf16[768,512]{1,0:T(8,128)(2,1)} %copy-done.4) | copy-start | bytes 2359300
  120.2 17.0 %copy-start.6 = (bf16[384,3072]{1,0:T(8,128)(2,1)}, bf16[384,3072]{1,0:T(8,128)(2,1)S(1)}, u32[]{:S(2)}) copy-start(bf16[384,3072]{1,0:T(8,128)(2,1)S(1)} %get-tuple-element.71.refs_0_) | copy-start | bytes 7077892
  123.9 14.4 %copy-start.9 = (bf16[384,3072]{1,0:T(8,128)(2,1)S(1)}, bf16[384,3072]{1,0:T(8,128)(2,1)}, u32[]{:S(2)}) copy-start(bf16[384,3072]{1,0:T(8,128)(2,1)} %copy-done.8) | copy-start | bytes 7077892
  123.9 14.4 %copy-start.13 = (bf16[384,1536]{1,0:T(8,128)(2,1)S(1)}, bf16[384,1536]{1,0:T(8,128)(2,1)}, u32[]{:S(2)}) copy-start(bf16[384,1536]{1,0:T(8,128)(2,1)} %copy-done.12) | copy-start | bytes 3538948
  137.3 51.6 %collective-permute-start.16 = (bf16[768,1536]{1,0:T(8,128)(2,1)}, bf16[768,1536]{1,0:T(8,128)(2,1)}, u32[]{:S(2)}, u32[]{:S(2)}) collective-permute-start(bf16[768,1536]{1,0:T(8,128)(2,1)} %get-tuple-element.89), channel_id=1, source_target_pairs={{0,8},{8,0},{16,24},{24,16},{1,9},{9,1},{17,25},{25,17},{2,10},{10... | collective-permute-start | bytes 7077896 | tf_op jit(solution)/shard_map/ppermute | solution.py:352
  137.8 59.4 %collective-permute-start.15 = (bf16[768,1536]{1,0:T(8,128)(2,1)}, bf16[768,1536]{1,0:T(8,128)(2,1)}, u32[]{:S(2)}, u32[]{:S(2)}) collective-permute-start(bf16[768,1536]{1,0:T(8,128)(2,1)} %get-tuple-element.84), channel_id=1, source_target_pairs={{0,16},{8,24},{16,0},{24,8},{1,17},{9,25},{17,1},{25,9},{2,18},{10... | collective-permute-start | bytes 7077896 | tf_op jit(solution)/shard_map/ppermute | solution.py:352
  142.2 63.6 %collective-permute-start.10 = (bf16[384,3072]{1,0:T(8,128)(2,1)}, bf16[384,3072]{1,0:T(8,128)(2,1)}, u32[]{:S(2)}, u32[]{:S(2)}) collective-permute-start(bf16[384,3072]{1,0:T(8,128)(2,1)} %get-tuple-element.76), channel_id=1, source_target_pairs={{0,1},{1,0},{2,3},{3,2},{4,5},{5,4},{6,7},{7,6},{8,9},{9,8},{10,11... | collective-permute-start | bytes 7077896 | tf_op jit(solution)/shard_map/ppermute | solution.py:352
  146.9 7.2 %copy-start.17 = (s32[1,768]{1,0:T(1,128)S(1)}, s32[1,768]{1,0:T(1,128)}, u32[]{:S(2)}) copy-start(s32[1,768]{1,0:T(1,128)} %param.15) | copy-start | bytes 9220
  151.4 54.4 %collective-permute-start.14 = (bf16[384,3072]{1,0:T(8,128)(2,1)}, bf16[384,3072]{1,0:T(8,128)(2,1)}, u32[]{:S(2)}, u32[]{:S(2)}) collective-permute-start(bf16[384,3072]{1,0:T(8,128)(2,1)} %get-tuple-element.81), channel_id=1, source_target_pairs={{1,2},{2,1},{5,6},{6,5},{9,10},{10,9},{13,14},{14,13},{17,18},{18,... | collective-permute-start | bytes 7077896 | tf_op jit(solution)/shard_map/ppermute | solution.py:383
  197.2 8.6 %copy-start.7 = (bf16[384,3072]{1,0:T(8,128)(2,1)S(1)}, bf16[384,3072]{1,0:T(8,128)(2,1)}, u32[]{:S(2)}) copy-start(bf16[384,3072]{1,0:T(8,128)(2,1)} %copy-done.6) | copy-start | bytes 7077892
  (6 other events, 12.4 us)

commit v4 on v3

--- a/solution.py
+++ b/solution.py
@@ -256,7 +256,7 @@
 
 def update(base, last, mean, square, whole, blend, column, bn, scale, before, order):
     share, width = base.shape
-    rows = block_rows(share, 256)
+    rows = block_rows(share, 768)
     across, place = width // bn, column // bn
 
     def kernel(old, arrived, m, s, b, *rest):
@@ -276,7 +276,7 @@
         out_specs=[moment] * 3 + [pl.BlockSpec(TOKEN, lambda i: (0, 0))],
         out_shape=[jax.ShapeDtypeStruct(whole, jnp.float32)] * 3 + [jax.ShapeDtypeStruct(TOKEN, jnp.float32)],
         input_output_aliases={5 + k: k for k in range(len(before))},
-        compiler_params=params(VMEM_LIMIT // 2),
+        compiler_params=params(),
         cost_estimate=cost(10 * share * width, share * width * 26),
         name="update",
     )(base, last, *(pltpu.with_memory_space_constraint(a, pltpu.VMEM) for a in (mean, square)), blend, *before, *order)
@@ -306,7 +306,7 @@
 
 def plus(terms, order, beside=()):
     rows, width = terms[0].shape
-    some = block_rows(rows, 96)
+    some = block_rows(rows, 192)
     count = len(terms)
 
     def kernel(*refs):
@@ -365,8 +365,10 @@
     small = max(1, blocks // 3)
     large = blocks - small
 
-    def products(*jobs, base=None, streamed=False):
-        return weight_product(held(inputs) if streamed else inputs, mine, theirs, ids, share, bn, jobs, order, base)
+    def products(*jobs, base=None, streamed=False, late=False):
+        rows = held(inputs) if streamed else inputs
+        sides = [[held(a) for a in side] if late else side for side in (mine, theirs)]
+        return weight_product(rows, *sides, ids, share, bn, jobs, order, base)
 
     part = width // 2
 
@@ -393,7 +395,7 @@
     order += [got_pass_a0]
     (c0_b,) = chunks([0], part, part)
     got_0b = outer(c0_b)
-    keep_a, keep_b = products((near[0], 0, 0, [], [blocks]), (near[1], 1, 0, [], [blocks]))
+    keep_a, keep_b = products((near[0], 0, 0, [], [blocks]), (near[1], 1, 0, [], [blocks]), late=True)
     got_keep_a, got_keep_b = swap(keep_a, "dp", near[0]), swap(keep_b, "dp", near[1])
     order += [got_pass_b0]
     got_m1a = across(plus([c0_a, got_0a], order))
@@ -406,13 +408,14 @@
     last_b, last_a = products(
         (far[1], 1, 0, [(small, got_pass_b0), (large, got_pass_b1)], [blocks]),
         (far[0], 0, 0, [(small, got_pass_a0), (large, got_pass_a1)], [blocks]),
+        late=True,
     )
     got_last_b, got_last_a = swap(last_b, "dp", far[1]), swap(last_a, "dp", far[0])
     got_2 = outer(plus([c2], order, beside=[got_m1a, got_m1b]))
     order += [got_keep_a, got_keep_b]
     got_m2 = across(plus([c1, got_1], order))
     base_b, base_a = products(
-        (0, 1, 0, [(blocks, got_keep_b)], [blocks]), (0, 0, 0, [(blocks, got_keep_a)], [blocks]), base=(weight, scale)
+        (0, 1, 0, [(blocks, got_keep_b)], [blocks]), (0, 0, 0, [(blocks, got_keep_a)], [blocks]), base=(weight, scale), late=True
     )
     (mean_b, square_b), (mean_a, square_a) = staged((swag_mean, swag_square), ((piece, piece), (0, piece)), order)
     outs = ()

time: 212 us -> 200 us (0.943)
  Pallas kernels: 152 us -> 141 us
  waiting for transfers between devices: 13.8 us -> 10.2 us
    pallas_call x5, Pallas kernels: 16.9 us -> 10.7 us  [plus(): pl.pallas_call(kernel, grid=(rows // some,), in_specs=[block(a) for a in...]
    pallas_call x2, Pallas kernels: 16.9 us -> 12.9 us  [update(): pl.pallas_call(kernel, grid=(share // rows * across,), in_specs=[block] *...]
    ppermute x14, waiting for transfers between devices: 13.8 us -> 10.2 us  [swap(): lax.ppermute(value, axis, [(i, i ^ bit) for i in range(lax.axis_size(axis...]
    ppermute x14, starting transfers between devices: 21 us -> 23.7 us  [swap(): lax.ppermute(value, axis, [(i, i ^ bit) for i in range(lax.axis_size(axis...]
    unnamed x42 -> x32, local copies, waits for them, and re-layouts: 7.44 us -> 7.07 us
  transfers between devices with their start and end apart: 17 -> 17, of which waited for: 1 -> 4; matrix products, arithmetic and copies ran while one was open for 2% -> 3% of each run, Pallas kernels for 70% -> 70%
where the time goes in v4:
time: 200 us; the launch traced here: 197 us
  Pallas kernels  141 us (70%)
  starting transfers between devices  27.4 us (14%)
  waiting for transfers between devices  10.2 us (5%)
  other arithmetic  9.77 us (5%)
  local copies, waits for them, and re-layouts  7.25 us (4%)
    pallas_call x6, Pallas kernels, weight_product(): pl.pallas_call(kernel, grid_spec=pltpu.PrefetchScalarGridSpec(num_scalar_...  57.2 us
    pallas_call x4, Pallas kernels, input_product(): pl.pallas_call(kernel, grid_spec=pltpu.PrefetchScalarGridSpec(num_scalar_...  53.9 us
    ppermute x14, starting transfers between devices, swap(): lax.ppermute(value, axis, [(i, i ^ bit) for i in range(lax.axis_size(axis...  23.7 us
    pallas_call x2, Pallas kernels, update(): pl.pallas_call(kernel, grid=(share // rows * across,), in_specs=[block] *...  12.9 us
    pallas_call x5, Pallas kernels, plus(): pl.pallas_call(kernel, grid=(rows // some,), in_specs=[block(a) for a in...  10.7 us
    ppermute x14, waiting for transfers between devices, swap(): lax.ppermute(value, axis, [(i, i ^ bit) for i in range(lax.axis_size(axis...  10.2 us
    convert_element_type x2, other arithmetic, times_slope(): (out_grad.astype(jnp.float32) * gelu_slope(pre_act.astype(jnp.float32)))....  9.69 us
    unnamed x32, local copies, waits for them, and re-layouts  7.07 us
  transfers between devices with their start and end apart: 17, of which 4 were waited for; matrix products, arithmetic and copies ran while one was open for 3% of the time, Pallas kernels for 70%

profile of v4, /device:TPU:0, one launch (start us, length us, event | category | flops | bytes accessed | tf_op | source)
XLA Modules:
  0.0 197.4 jit_solution(6688248506127025883)
XLA Ops:
  0.6 4.5 %fusion.15.refs_2_.rest_0_.refs_6_ = bf16[768,1536]{1,0:T(8,128)(2,1)S(1)} fusion(bf16[768,3072]{1,0:T(8,128)(2,1)} %param.9, bf16[768,3072]{1,0:T(8,128)(2,1)} %param.10), kind=kLoop, calls=%fused_computation.23 | loop fusion | flops 14155776 | bytes 7077888 | tf_op jit(solution)/shard_map/convert_element_type | solution.py:24
  5.7 5.2 %fusion.14.rest_1_.refs_2_.refs_4_ = bf16[768,1536]{1,0:T(8,128)(2,1)} fusion(bf16[768,3072]{1,0:T(8,128)(2,1)S(1)} %copy-done.11, bf16[768,3072]{1,0:T(8,128)(2,1)} %param.10), kind=kLoop, calls=%fused_computation.22 | loop fusion | flops 14155776 | bytes 7077888 | tf_op jit(solution)/shard_map/convert_element_type | solution.py:24
  11.3 3.8 %weight_product.6 = (bf16[768,512]{1,0:T(8,128)(2,1)S(1)}, f32[8,128]{1,0:T(8,128)S(1)}) custom-call(s32[3]{0:T(128)S(1)} %pad_add_fusion.ids_ref, bf16[1536,3072]{1,0:T(8,128)(2,1)} %refs_1_.12, bf16[1536,3072]{1,0:T(8,128)(2,1)} %refs_1_.12, bf16[768,1536]{1,0:T(8,128)(2,1)S(1)} %fusion.15.refs_2_.rest_0_.refs_6_, ...), custom_call_target="tpu_custom_call" | custom-call | flops 1207959552 | bytes 2359296 | tf_op jit(solution)/shard_map/weight_product/pallas_call | solution.py:135
  15.1 2.5 %collective-permute-start.2 = (bf16[768,512]{1,0:T(8,128)(2,1)S(1)}, bf16[768,512]{1,0:T(8,128)(2,1)S(1)}, u32[]{:S(2)}, u32[]{:S(2)}) collective-permute-start(bf16[768,512]{1,0:T(8,128)(2,1)S(1)} %get-tuple-element.59), channel_id=1, source_target_pairs={{0,8},{8,0},{16,24},{24,16},{1,9},{9,1},{17,25},{25,17},{2,10},{10... | collective-permute-start | bytes 2359304 | tf_op jit(solution)/shard_map/ppermute | solution.py:352
  17.6 9.1 %input_product.4 = (bf16[384,1536]{1,0:T(8,128)(2,1)S(1)}, f32[8,128]{1,0:T(8,128)S(1)}) custom-call(s32[3]{0:T(128)S(1)} %pad_add_fusion.ids_ref, bf16[3072,3072]{1,0:T(8,128)(2,1)} %refs_9_.1, bf16[768,1536]{1,0:T(8,128)(2,1)S(1)} %fusion.15.refs_2_.rest_0_.refs_6_, bf16[768,1536]{1,0:T(8,128)(2,1)} %fusion.14.rest_1_.refs_2_.refs_4_, ...), custom_call_target="tpu_custom_call" | custom-call | flops 3623878656 | bytes 12976128 | tf_op jit(solution)/shard_map/input_product/pallas_call | solution.py:195
  26.7 4.3 %weight_product.7 = (bf16[768,512]{1,0:T(8,128)(2,1)S(1)}, f32[8,128]{1,0:T(8,128)S(1)}) custom-call(s32[3]{0:T(128)S(1)} %pad_add_fusion.ids_ref, bf16[1536,3072]{1,0:T(8,128)(2,1)} %refs_1_.12, bf16[1536,3072]{1,0:T(8,128)(2,1)} %refs_1_.12, bf16[768,1536]{1,0:T(8,128)(2,1)} %fusion.14.rest_1_.refs_2_.refs_4_, ...), custom_call_target="tpu_custom_call" | custom-call | flops 1207959552 | bytes 2359296 | tf_op jit(solution)/shard_map/weight_product/pallas_call | solution.py:135
  31.1 1.6 collective-permute-start.5
  32.7 1.6 collective-permute-start.4
  34.3 9.2 %weight_product.8 = (bf16[768,1024]{1,0:T(8,128)(2,1)}, bf16[768,1024]{1,0:T(8,128)(2,1)S(1)}, f32[8,128]{1,0:T(8,128)S(1)}) custom-call(s32[3]{0:T(128)S(1)} %pad_add_fusion.ids_ref, bf16[1536,3072]{1,0:T(8,128)(2,1)S(1)} %bitcast.7, bf16[1536,3072]{1,0:T(8,128)(2,1)S(1)} %bitcast.7, bf16[768,1536]{1,0:T(8,128)(2,1)S(1)} %fusion.15.refs_2_.rest_0_.refs_6_, ...), custom_call_target="tpu_custom_call" | custom-call | flops 4831838208 | bytes 9437184 | tf_op jit(solution)/shard_map/weight_product/pallas_call | solution.py:135
  44.9 9.1 %input_product.5 = (bf16[384,1536]{1,0:T(8,128)(2,1)S(1)}, f32[8,128]{1,0:T(8,128)S(1)}) custom-call(s32[3]{0:T(128)S(1)} %pad_add_fusion.ids_ref, bf16[3072,3072]{1,0:T(8,128)(2,1)} %refs_9_.1, bf16[768,1536]{1,0:T(8,128)(2,1)S(1)} %fusion.15.refs_2_.rest_0_.refs_6_, bf16[768,1536]{1,0:T(8,128)(2,1)} %fusion.14.rest_1_.refs_2_.refs_4_, ...), custom_call_target="tpu_custom_call" | custom-call | flops 3623878656 | bytes 12976128 | tf_op jit(solution)/shard_map/input_product/pallas_call | solution.py:195
  54.5 12.9 %weight_product.9 = (bf16[768,1536]{1,0:T(8,128)(2,1)}, bf16[768,1536]{1,0:T(8,128)(2,1)}, f32[8,128]{1,0:T(8,128)S(1)}) custom-call(s32[3]{0:T(128)S(1)} %pad_add_fusion.ids_ref, bf16[1536,3072]{1,0:T(8,128)(2,1)S(1)} %bitcast.7, bf16[1536,3072]{1,0:T(8,128)(2,1)S(1)} %bitcast.7, bf16[768,1536]{1,0:T(8,128)(2,1)} %copy-done.1, ...), custom_call_target="tpu_custom_call" | custom-call | flops 7247757312 | bytes 14155776 | tf_op jit(solution)/shard_map/weight_product/pallas_call | solution.py:135
  69.9 15.1 %input_product.6 = (bf16[384,3072]{1,0:T(8,128)(2,1)}, f32[8,128]{1,0:T(8,128)S(1)}) custom-call(s32[3]{0:T(128)S(1)} %pad_add_fusion.ids_ref, bf16[3072,3072]{1,0:T(8,128)(2,1)} %refs_9_.1, bf16[768,1536]{1,0:T(8,128)(2,1)S(1)} %copy-done.2, bf16[768,1536]{1,0:T(8,128)(2,1)} %fusion.14.rest_1_.refs_2_.refs_4_, ...), custom_call_target="tpu_custom_call" | custom-call | flops 7247757312 | bytes 23592960 | tf_op jit(solution)/shard_map/input_product/pallas_call | solution.py:195
  85.0 1.6 collective-permute-start.13
  86.6 3.8 %collective-permute-start.11 = (bf16[384,3072]{1,0:T(8,128)(2,1)}, bf16[384,3072]{1,0:T(8,128)(2,1)}, u32[]{:S(2)}, u32[]{:S(2)}) collective-permute-start(bf16[384,3072]{1,0:T(8,128)(2,1)} %get-tuple-element.77.refs_0_), channel_id=1, source_target_pairs={{0,1},{1,0},{2,3},{3,2},{4,5},{5,4},{6,7},{7,6},{8,9},{9,8},{10,11... | collective-permute-start | bytes 7077896 | tf_op jit(solution)/shard_map/ppermute | solution.py:352
  90.4 1.2 plus.6
  92.4 20.6 %input_product.7 = (bf16[384,3072]{1,0:T(8,128)(2,1)S(1)}, bf16[384,3072]{1,0:T(8,128)(2,1)S(1)}, f32[8,128]{1,0:T(8,128)S(1)}) custom-call(s32[3]{0:T(128)S(1)} %pad_add_fusion.ids_ref, bf16[3072,3072]{1,0:T(8,128)(2,1)} %refs_9_.1, bf16[768,1536]{1,0:T(8,128)(2,1)S(1)} %copy-done.2, bf16[768,1536]{1,0:T(8,128)(2,1)} %fusion.14.rest_1_.refs_2_.refs_4_, ...), custom_call_target="tpu_custom_call" | custom-call | flops 14495514624 | bytes 28311552 | tf_op jit(solution)/shard_map/input_product/pallas_call | solution.py:195
  113.0 13.6 %weight_product.10 = (bf16[768,1536]{1,0:T(8,128)(2,1)}, bf16[768,1536]{1,0:T(8,128)(2,1)}, f32[8,128]{1,0:T(8,128)S(1)}) custom-call(s32[3]{0:T(128)S(1)} %pad_add_fusion.ids_ref, bf16[1536,3072]{1,0:T(8,128)(2,1)S(1)} %bitcast.7, bf16[1536,3072]{1,0:T(8,128)(2,1)S(1)} %bitcast.7, bf16[768,1536]{1,0:T(8,128)(2,1)} %fusion.14.rest_1_.refs_2_.refs_4_, ...), custom_call_target="tpu_custom_call" | custom-call | flops 7247757312 | bytes 14155776 | tf_op jit(solution)/shard_map/weight_product/pallas_call | solution.py:135
  128.1 1.7 plus.7
  129.8 1.8 collective-permute-done.12.refs_3_.refs_8_
  131.6 7.2 %collective-permute-start.10 = (bf16[384,3072]{1,0:T(8,128)(2,1)}, bf16[384,3072]{1,0:T(8,128)(2,1)}, u32[]{:S(2)}, u32[]{:S(2)}) collective-permute-start(bf16[384,3072]{1,0:T(8,128)(2,1)} %get-tuple-element.76), channel_id=1, source_target_pairs={{0,1},{1,0},{2,3},{3,2},{4,5},{5,4},{6,7},{7,6},{8,9},{9,8},{10,11... | collective-permute-start | bytes 7077896 | tf_op jit(solution)/shard_map/ppermute | solution.py:352
  139.5 3.4 %collective-permute-done.11.refs_1_ = bf16[384,3072]{1,0:T(8,128)(2,1)} collective-permute-done((bf16[384,3072]{1,0:T(8,128)(2,1)}, bf16[384,3072]{1,0:T(8,128)(2,1)}, u32[]{:S(2)}, u32[]{:S(2)}) %collective-permute-start.11) | collective-permute-done | bytes 2359328 | tf_op jit(solution)/shard_map/ppermute | solution.py:352
  142.9 3.7 %plus.8 = (bf16[384,3072]{1,0:T(8,128)(2,1)}, f32[8,128]{1,0:T(8,128)S(1)}) custom-call(bf16[384,3072]{1,0:T(8,128)(2,1)} %get-tuple-element.77.refs_0_, bf16[384,3072]{1,0:T(8,128)(2,1)} %collective-permute-done.11.refs_1_, f32[8,128]{1,0:T(8,128)S(1)} %get-tuple-element.78.refs_2_, bf16[768,1536]{1,0:T(8,128)(2,1)S(1)} %collective-permute-done.12.refs_3_.refs_8_, ...), custom_call_target="tpu_custom_call" | custom-call | flops 3538944 | bytes 9437184 | tf_op jit(solution)/shard_map/plus/pallas_call | solution.py:327
  146.6 2.1 %collective-permute-start.14 = (bf16[384,3072]{1,0:T(8,128)(2,1)}, bf16[384,3072]{1,0:T(8,128)(2,1)}, u32[]{:S(2)}, u32[]{:S(2)}) collective-permute-start(bf16[384,3072]{1,0:T(8,128)(2,1)} %get-tuple-element.81), channel_id=1, source_target_pairs={{1,2},{2,1},{5,6},{6,5},{9,10},{10,9},{13,14},{14,13},{17,18},{18,... | collective-permute-start | bytes 7077896 | tf_op jit(solution)/shard_map/ppermute | solution.py:385
  149.6 3.7 %copy-done = bf16[1536,3072]{1,0:T(8,128)(2,1)S(1)} copy-done((bf16[1536,3072]{1,0:T(8,128)(2,1)S(1)}, bf16[1536,3072]{1,0:T(8,128)(2,1)}, u32[]{:S(2)}) %copy-start) | copy-done | bytes 9437208
  153.2 1.7 copy-done.4
  154.9 1.7 copy-done.6
  156.6 13.2 %weight_product.11 = (f32[768,1536]{1,0:T(8,128)S(1)}, f32[768,1536]{1,0:T(8,128)S(1)}, f32[8,128]{1,0:T(8,128)S(1)}) custom-call(s32[3]{0:T(128)S(1)} %pad_add_fusion.ids_ref, bf16[1536,3072]{1,0:T(8,128)(2,1)S(1)} %copy-done, bf16[1536,3072]{1,0:T(8,128)(2,1)S(1)} %copy-done, bf16[768,1536]{1,0:T(8,128)(2,1)} %fusion.14.rest_1_.refs_2_.refs_4_, ...), custom_call_target="tpu_custom_call" | custom-call | flops 7247757312 | bytes 14155776 | tf_op jit(solution)/shard_map/weight_product/pallas_call | solution.py:135
  169.8 6.5 %staged.1 = (f32[768,1536]{1,0:T(8,128)S(1)}, f32[768,1536]{1,0:T(8,128)S(1)}, f32[768,1536]{1,0:T(8,128)S(1)}, f32[768,1536]{1,0:T(8,128)S(1)}, f32[8,128]{1,0:T(8,128)S(1)}) custom-call(f32[1,768,3072]{2,1,0:T(8,128)} %refs_0_.13, f32[1,768,3072]{2,1,0:T(8,128)} %refs_1_.13, f32[8,128]{1,0:T(8,128)S(1)} %get-tuple-element.85.refs_2_), custom_call_target="tpu_custom_call" | custom-call | bytes 37748736 | tf_op jit(solution)/shard_map/staged/pallas_call | solution.py:242
  176.3 4.3 %collective-permute-done.16.arrived = bf16[768,1536]{1,0:T(8,128)(2,1)} collective-permute-done((bf16[768,1536]{1,0:T(8,128)(2,1)}, bf16[768,1536]{1,0:T(8,128)(2,1)}, u32[]{:S(2)}, u32[]{:S(2)}) %collective-permute-start.16) | collective-permute-done | bytes 2359328 | tf_op jit(solution)/shard_map/ppermute | solution.py:352
  180.6 6.7 %update.2 = (f32[1,768,3072]{2,1,0:T(8,128)}, f32[1,768,3072]{2,1,0:T(8,128)}, f32[1,768,3072]{2,1,0:T(8,128)}, f32[8,128]{1,0:T(8,128)S(1)}) custom-call(f32[768,1536]{1,0:T(8,128)S(1)} %get-tuple-element.88.old, bf16[768,1536]{1,0:T(8,128)(2,1)} %collective-permute-done.16.arrived, f32[768,1536]{1,0:T(8,128)S(1)} %get-tuple-element.90.m, ...), custom_call_target="tpu_custom_call" | custom-call | flops 11796480 | bytes 30670848 | tf_op jit(solution)/shard_map/update/pallas_call | solution.py:272
  187.3 6.3 %update.3 = (f32[1,768,3072]{2,1,0:T(8,128)}, f32[1,768,3072]{2,1,0:T(8,128)}, f32[1,768,3072]{2,1,0:T(8,128)}, f32[8,128]{1,0:T(8,128)S(1)}) custom-call(f32[768,1536]{1,0:T(8,128)S(1)} %get-tuple-element.83.old, bf16[768,1536]{1,0:T(8,128)(2,1)S(1)} %collective-permute-done.15.arrived, ...), custom_call_target="tpu_custom_call", output_to_operand_aliasing={{0}: (5, {}), {1}: (6, {}), {2}: (7, {})} | custom-call | flops 11796480 | bytes 30670848 | tf_op jit(solution)/shard_map/update/pallas_call | solution.py:272
  193.6 3.8 %plus.9 = (bf16[384,3072]{1,0:T(8,128)(2,1)}, f32[8,128]{1,0:T(8,128)}) custom-call(bf16[384,3072]{1,0:T(8,128)(2,1)S(1)} %copy-done.8, bf16[384,3072]{1,0:T(8,128)(2,1)} %collective-permute-done.10.refs_1_, bf16[384,3072]{1,0:T(8,128)(2,1)} %collective-permute-done.14.refs_2_, f32[8,128]{1,0:T(8,128)S(1)} %get-tuple-element.97.refs_3_), custom_call_target="tpu_custom_call" | custom-call | flops 4718592 | bytes 11796480 | tf_op jit(solution)/shard_map/plus/pallas_call | solution.py:327
  (58 shorter events, 8.4 us)
Async XLA Ops:
  0.6 5.0 %copy-start.11 = (bf16[768,3072]{1,0:T(8,128)(2,1)S(1)}, bf16[768,3072]{1,0:T(8,128)(2,1)}, u32[]{:S(2)}) copy-start(bf16[768,3072]{1,0:T(8,128)(2,1)} %param.9) | copy-start | bytes 14155780
  5.1 39.8 %copy-start.1 = (bf16[768,1536]{1,0:T(8,128)(2,1)}, bf16[768,1536]{1,0:T(8,128)(2,1)S(1)}, u32[]{:S(2)}) copy-start(bf16[768,1536]{1,0:T(8,128)(2,1)S(1)} %fusion.15.refs_2_.rest_0_.refs_6_) | copy-start | bytes 7077892
  5.1 6.2 %collective-permute-start = (bf16[768,1536]{1,0:T(8,128)(2,1)S(1)}, bf16[768,1536]{1,0:T(8,128)(2,1)}, u32[]{:S(2)}, u32[]{:S(2)}) collective-permute-start(bf16[768,1536]{1,0:T(8,128)(2,1)S(1)} %fusion.15.refs_2_.rest_0_.refs_6_), channel_id=1, source_target_pairs={{0,4},{4,0},{1,5},{5,1},{2,6},{6,2},{3,7},{7,3},{8,12},{12,8},{9,1... | collective-permute-start | bytes 7077896 | tf_op jit(solution)/shard_map/ppermute | solution.py:352
  10.9 6.8 %collective-permute-start.1 = (bf16[768,1536]{1,0:T(8,128)(2,1)}, bf16[768,1536]{1,0:T(8,128)(2,1)}, u32[]{:S(2)}, u32[]{:S(2)}) collective-permute-start(bf16[768,1536]{1,0:T(8,128)(2,1)} %fusion.14.rest_1_.refs_2_.refs_4_), channel_id=1, source_target_pairs={{0,4},{4,0},{1,5},{5,1},{2,6},{6,2},{3,7},{7,3},{8,12},{12,8},{9,1... | collective-permute-start | bytes 7077896 | tf_op jit(solution)/shard_map/ppermute | solution.py:352
  15.1 29.8 %collective-permute-start.2 = (bf16[768,512]{1,0:T(8,128)(2,1)S(1)}, bf16[768,512]{1,0:T(8,128)(2,1)S(1)}, u32[]{:S(2)}, u32[]{:S(2)}) collective-permute-start(bf16[768,512]{1,0:T(8,128)(2,1)S(1)} %get-tuple-element.59), channel_id=1, source_target_pairs={{0,8},{8,0},{16,24},{24,16},{1,9},{9,1},{17,25},{25,17},{2,10},{10... | collective-permute-start | bytes 2359304 | tf_op jit(solution)/shard_map/ppermute | solution.py:352
  26.7 7.5 %slice-start = ((s8[9437184]{0:T(1024)(128)(4,1)}), s8[4194304]{0:T(1024)(128)(4,1)S(1)}, s32[]{:S(2)}) async-start(s8[9437184]{0:T(1024)(128)(4,1)} %bitcast.6), calls=%async_computation | async-start | bytes 8388608
  26.7 7.5 %slice-start.1 = ((s8[9437184]{0:T(1024)(128)(4,1)}), s8[4194304]{0:T(1024)(128)(4,1)S(1)}, s32[]{:S(2)}) async-start(s8[9437184]{0:T(1024)(128)(4,1)} %bitcast.6), calls=%async_computation.1 | async-start | bytes 8388608
  26.7 7.5 %slice-start.2 = ((s8[9437184]{0:T(1024)(128)(4,1)}), s8[1048576]{0:T(1024)(128)(4,1)S(1)}, s32[]{:S(2)}) async-start(s8[9437184]{0:T(1024)(128)(4,1)} %bitcast.6), calls=%async_computation.2 | async-start | bytes 2097152
  31.1 36.4 %collective-permute-start.5 = (bf16[768,512]{1,0:T(8,128)(2,1)S(1)}, bf16[768,512]{1,0:T(8,128)(2,1)S(1)}, u32[]{:S(2)}, u32[]{:S(2)}) collective-permute-start(bf16[768,512]{1,0:T(8,128)(2,1)S(1)} %get-tuple-element.64), channel_id=1, source_target_pairs={{0,16},{8,24},{16,0},{24,8},{1,17},{9,25},{17,1},{25,9},{2,18},{10... | collective-permute-start | bytes 2359304 | tf_op jit(solution)/shard_map/ppermute | solution.py:352
  32.7 34.8 %collective-permute-start.4 = (bf16[384,1536]{1,0:T(8,128)(2,1)S(1)}, bf16[384,1536]{1,0:T(8,128)(2,1)S(1)}, u32[]{:S(2)}, u32[]{:S(2)}) collective-permute-start(bf16[384,1536]{1,0:T(8,128)(2,1)S(1)} %get-tuple-element.61.refs_0_), channel_id=1, source_target_pairs={{0,1},{1,0},{2,3},{3,2},{4,5},{5,4},{6,7},{7,6},{8,9},{9,8},{10,11... | collective-permute-start | bytes 3538952 | tf_op jit(solution)/shard_map/ppermute | solution.py:352
  43.5 41.6 %collective-permute-start.6 = (bf16[768,1024]{1,0:T(8,128)(2,1)}, bf16[768,1024]{1,0:T(8,128)(2,1)S(1)}, u32[]{:S(2)}, u32[]{:S(2)}) collective-permute-start(bf16[768,1024]{1,0:T(8,128)(2,1)} %get-tuple-element.67), channel_id=1, source_target_pairs={{0,8},{8,0},{16,24},{24,16},{1,9},{9,1},{17,25},{25,17},{2,10},{10... | collective-permute-start | bytes 4718600 | tf_op jit(solution)/shard_map/ppermute | solution.py:352
  44.4 42.2 %collective-permute-start.7 = (bf16[768,1024]{1,0:T(8,128)(2,1)S(1)}, bf16[768,1024]{1,0:T(8,128)(2,1)S(1)}, u32[]{:S(2)}, u32[]{:S(2)}) collective-permute-start(bf16[768,1024]{1,0:T(8,128)(2,1)S(1)} %get-tuple-element.68), channel_id=1, source_target_pairs={{0,16},{8,24},{16,0},{24,8},{1,17},{9,25},{17,1},{25,9},{2,18},{10... | collective-permute-start | bytes 4718600 | tf_op jit(solution)/shard_map/ppermute | solution.py:352
  54.0 36.4 %collective-permute-start.3 = (bf16[384,1536]{1,0:T(8,128)(2,1)S(1)}, bf16[384,1536]{1,0:T(8,128)(2,1)S(1)}, u32[]{:S(2)}, u32[]{:S(2)}) collective-permute-start(bf16[384,1536]{1,0:T(8,128)(2,1)S(1)} %get-tuple-element.60.refs_0_), channel_id=1, source_target_pairs={{0,1},{1,0},{2,3},{3,2},{4,5},{5,4},{6,7},{7,6},{8,9},{9,8},{10,11... | collective-permute-start | bytes 3538952 | tf_op jit(solution)/shard_map/ppermute | solution.py:352
  54.5 15.4 %copy-start.2 = (bf16[768,1536]{1,0:T(8,128)(2,1)S(1)}, bf16[768,1536]{1,0:T(8,128)(2,1)}, u32[]{:S(2)}) copy-start(bf16[768,1536]{1,0:T(8,128)(2,1)} %copy-done.1) | copy-start | bytes 7077892
  67.8 24.5 %collective-permute-start.8 = (bf16[384,1536]{1,0:T(8,128)(2,1)S(1)}, bf16[384,1536]{1,0:T(8,128)(2,1)S(1)}, u32[]{:S(2)}, u32[]{:S(2)}) collective-permute-start(bf16[384,1536]{1,0:T(8,128)(2,1)S(1)} %get-tuple-element.70), channel_id=1, source_target_pairs={{1,2},{2,1},{5,6},{6,5},{9,10},{10,9},{13,14},{14,13},{17,18},{18,... | collective-permute-start | bytes 3538952 | tf_op jit(solution)/shard_map/ppermute | solution.py:385
  68.7 62.8 %collective-permute-start.12 = (bf16[768,1536]{1,0:T(8,128)(2,1)}, bf16[768,1536]{1,0:T(8,128)(2,1)S(1)}, u32[]{:S(2)}, u32[]{:S(2)}) collective-permute-start(bf16[768,1536]{1,0:T(8,128)(2,1)} %get-tuple-element.79), channel_id=1, source_target_pairs={{0,8},{8,0},{16,24},{24,16},{1,9},{9,1},{17,25},{25,17},{2,10},{10... | collective-permute-start | bytes 7077896 | tf_op jit(solution)/shard_map/ppermute | solution.py:352
  85.0 54.5 %collective-permute-start.13 = (bf16[768,1536]{1,0:T(8,128)(2,1)}, bf16[768,1536]{1,0:T(8,128)(2,1)S(1)}, u32[]{:S(2)}, u32[]{:S(2)}) collective-permute-start(bf16[768,1536]{1,0:T(8,128)(2,1)} %get-tuple-element.80), channel_id=1, source_target_pairs={{0,16},{8,24},{16,0},{24,8},{1,17},{9,25},{17,1},{25,9},{2,18},{10... | collective-permute-start | bytes 7077896 | tf_op jit(solution)/shard_map/ppermute | solution.py:352
  86.6 56.3 %collective-permute-start.11 = (bf16[384,3072]{1,0:T(8,128)(2,1)}, bf16[384,3072]{1,0:T(8,128)(2,1)}, u32[]{:S(2)}, u32[]{:S(2)}) collective-permute-start(bf16[384,3072]{1,0:T(8,128)(2,1)} %get-tuple-element.77.refs_0_), channel_id=1, source_target_pairs={{0,1},{1,0},{2,3},{3,2},{4,5},{5,4},{6,7},{7,6},{8,9},{9,8},{10,11... | collective-permute-start | bytes 7077896 | tf_op jit(solution)/shard_map/ppermute | solution.py:352
  91.6 36.0 %collective-permute-start.9 = (bf16[384,1536]{1,0:T(8,128)(2,1)}, bf16[384,1536]{1,0:T(8,128)(2,1)S(1)}, u32[]{:S(2)}, u32[]{:S(2)}) collective-permute-start(bf16[384,1536]{1,0:T(8,128)(2,1)} %get-tuple-element.73), channel_id=1, source_target_pairs={{1,2},{2,1},{5,6},{6,5},{9,10},{10,9},{13,14},{14,13},{17,18},{18,... | collective-permute-start | bytes 3538952 | tf_op jit(solution)/shard_map/ppermute | solution.py:385
  92.4 20.6 %copy-start.9 = (bf16[384,1536]{1,0:T(8,128)(2,1)}, bf16[384,1536]{1,0:T(8,128)(2,1)S(1)}, u32[]{:S(2)}) copy-start(bf16[384,1536]{1,0:T(8,128)(2,1)S(1)} %collective-permute-done.8.rest_5_.refs_1_) | copy-start | bytes 3538948
  113.0 13.7 %copy-start.7 = (bf16[384,3072]{1,0:T(8,128)(2,1)}, bf16[384,3072]{1,0:T(8,128)(2,1)S(1)}, u32[]{:S(2)}) copy-start(bf16[384,3072]{1,0:T(8,128)(2,1)S(1)} %get-tuple-element.71.refs_0_) | copy-start | bytes 7077892
  113.0 15.1 %copy-start.10 = (bf16[384,1536]{1,0:T(8,128)(2,1)S(1)}, bf16[384,1536]{1,0:T(8,128)(2,1)}, u32[]{:S(2)}) copy-start(bf16[384,1536]{1,0:T(8,128)(2,1)} %copy-done.9) | copy-start | bytes 3538948
  126.7 53.9 %collective-permute-start.16 = (bf16[768,1536]{1,0:T(8,128)(2,1)}, bf16[768,1536]{1,0:T(8,128)(2,1)}, u32[]{:S(2)}, u32[]{:S(2)}) collective-permute-start(bf16[768,1536]{1,0:T(8,128)(2,1)} %get-tuple-element.89), channel_id=1, source_target_pairs={{0,8},{8,0},{16,24},{24,16},{1,9},{9,1},{17,25},{25,17},{2,10},{10... | collective-permute-start | bytes 7077896 | tf_op jit(solution)/shard_map/ppermute | solution.py:352
  127.6 59.7 %collective-permute-start.15 = (bf16[768,1536]{1,0:T(8,128)(2,1)}, bf16[768,1536]{1,0:T(8,128)(2,1)S(1)}, u32[]{:S(2)}, u32[]{:S(2)}) collective-permute-start(bf16[768,1536]{1,0:T(8,128)(2,1)} %get-tuple-element.84), channel_id=1, source_target_pairs={{0,16},{8,24},{16,0},{24,8},{1,17},{9,25},{17,1},{25,9},{2,18},{10... | collective-permute-start | bytes 7077896 | tf_op jit(solution)/shard_map/ppermute | solution.py:352
  131.6 15.0 %copy-start.3 = (bf16[768,1536]{1,0:T(8,128)(2,1)}, bf16[768,1536]{1,0:T(8,128)(2,1)S(1)}, u32[]{:S(2)}) copy-start(bf16[768,1536]{1,0:T(8,128)(2,1)S(1)} %collective-permute-done.12.refs_3_.refs_8_) | copy-start | bytes 7077892
  131.6 62.0 %collective-permute-start.10 = (bf16[384,3072]{1,0:T(8,128)(2,1)}, bf16[384,3072]{1,0:T(8,128)(2,1)}, u32[]{:S(2)}, u32[]{:S(2)}) collective-permute-start(bf16[384,3072]{1,0:T(8,128)(2,1)} %get-tuple-element.76), channel_id=1, source_target_pairs={{0,1},{1,0},{2,3},{3,2},{4,5},{5,4},{6,7},{7,6},{8,9},{9,8},{10,11... | collective-permute-start | bytes 7077896 | tf_op jit(solution)/shard_map/ppermute | solution.py:352
  139.5 7.1 %copy-start.5 = (bf16[768,1536]{1,0:T(8,128)(2,1)}, bf16[768,1536]{1,0:T(8,128)(2,1)S(1)}, u32[]{:S(2)}) copy-start(bf16[768,1536]{1,0:T(8,128)(2,1)S(1)} %collective-permute-done.13.refs_4_) | copy-start | bytes 7077892
  142.9 6.4 %copy-start.12 = (s32[1,768]{1,0:T(1,128)S(1)}, s32[1,768]{1,0:T(1,128)}, u32[]{:S(2)}) copy-start(s32[1,768]{1,0:T(1,128)} %param.15) | copy-start | bytes 9220
  146.6 47.0 %collective-permute-start.14 = (bf16[384,3072]{1,0:T(8,128)(2,1)}, bf16[384,3072]{1,0:T(8,128)(2,1)}, u32[]{:S(2)}, u32[]{:S(2)}) collective-permute-start(bf16[384,3072]{1,0:T(8,128)(2,1)} %get-tuple-element.81), channel_id=1, source_target_pairs={{1,2},{2,1},{5,6},{6,5},{9,10},{10,9},{13,14},{14,13},{17,18},{18,... | collective-permute-start | bytes 7077896 | tf_op jit(solution)/shard_map/ppermute | solution.py:385
  149.6 3.7 %copy-start = (bf16[1536,3072]{1,0:T(8,128)(2,1)S(1)}, bf16[1536,3072]{1,0:T(8,128)(2,1)}, u32[]{:S(2)}) copy-start(bf16[1536,3072]{1,0:T(8,128)(2,1)} %refs_1_.12) | copy-start | bytes 28311556
  153.2 1.7 copy-start.4
  187.3 6.3 %copy-start.8 = (bf16[384,3072]{1,0:T(8,128)(2,1)S(1)}, bf16[384,3072]{1,0:T(8,128)(2,1)}, u32[]{:S(2)}) copy-start(bf16[384,3072]{1,0:T(8,128)(2,1)} %copy-done.7) | copy-start | bytes 7077892
  (1 other events, 1.7 us)
